TPU v7x, 32 devices: a whole 2x2x4 slice. The times are simulated.
32 devices in a mesh: dp: 4 (over y, core), seq: 8 (over z, x).
Axes of the slice: x: 2, y: 2, z: 4, core: 2. Of those that a mesh axis runs over, the one named last changes fastest.
Arguments:
- latents: bfloat16 [2, 4, 2048, 16], P(None, 'dp', 'seq'), may hold values from -6 to 6
- noise: bfloat16 [2, 4, 2048, 16], P(None, 'dp', 'seq'), may hold values from -6 to 6
- captions: bfloat16 [2, 4, 960, 4096], P(None, 'dp', 'seq'), may hold values from -6 to 6
- image_sizes: int32 [2, 4, 8], replicated, may hold values from 0 to 1024, as said below
- caption_lengths: int32 [2, 4, 8], replicated, may hold values from 1 to 120
- timesteps: int32 [2, 4, 8], replicated, may hold values from 0 to 999
- weights: float32 [32000, 1152], P(('dp', 'seq'))
- vectors: float32 [78, 1152], replicated
- weights_m: float32 [32000, 1152], P(('dp', 'seq')), may hold values from -2.0861626e-07 to 2.0861626e-07
- weights_v: float32 [32000, 1152], P(('dp', 'seq')), may hold values from 1.082431e-16 to 4.329724e-16
- vectors_m: float32 [78, 1152], replicated, may hold values from -8.34465e-07 to 8.34465e-07
- vectors_v: float32 [78, 1152], replicated, may hold values from 1.7318896e-15 to 6.9275585e-15
Outputs:
- new_weights: float32 [32000, 1152], P(('dp', 'seq'))
- new_weights_m: float32 [32000, 1152], P(('dp', 'seq'))
- new_weights_v: float32 [32000, 1152], P(('dp', 'seq'))
- new_vectors: float32 [78, 1152], replicated
- new_vectors_m: float32 [78, 1152], replicated
- new_vectors_v: float32 [78, 1152], replicated
- loss_sum: float32 [], replicated
- image_count: float32 [], replicated
- grad_norm: float32 [], replicated
- down_bias_grad: float32 [1152], replicated
Inputs may be any that keep to these rules, and one draw needn't show every extreme that they name: `image_sizes`: in each row the first slots hold 256 or 1024, the rest 0; each row sums to 2048; every draw has an image of 1024 patches.
All inputs are finite; a program needn't handle non-finite values.
Results may differ from a plain program's by a relative error of at most 0.0062.
The roundings to bfloat16 on the way count: a program that leaves them out, or rounds other values in their place, can miss the bound.
Values may be sent and summed in bfloat16 or wider, within the bound.
A program may use at most 512 MiB of HBM per device.

v0:
```python
import functools
import math

import jax
import jax.numpy as jnp
from jax import lax
from jax.experimental import pallas as pl
from jax.experimental.pallas import tpu as pltpu
from jax.sharding import PartitionSpec as P

HEADS = 16
FF = 4608
TEXT_W = 4096
FREQ = 256
CAP = 120
CAP_PAD = 128
SIDE = 16
PATCH = 16
MICRO = 2
STEP = 10
BLOCK = 256
LARGE = 1024
VMEM_BYTES = 56 * 1024 * 1024

exact = lax.Precision.HIGHEST
clip_norm = 0.002
contrastive_sharpness_divisor = 0.1
beta_one = 0.9
beta_two = 0.999
adam_eps = 1e-08
weight_decay = 0.01
rate_matrix = 0.05
rate_vector = 0.3
norm_eps = 1e-06
neg_large = -1e30
log_two = math.log(2.0)
both_axes = ("dp", "seq")


def matrix_rows(width):
    return (FREQ, width, 6 * width, TEXT_W, width, 3 * width, width, width, 2 * width, width, FF, FF)


def vector_rows(width):
    return (6, 2, PATCH, 2 * PATCH, 1, 1, 1, 6, 1, 1, 1, 1, 1, 1, 1, 1, FF // width, 1)


def split_rows(whole, rows):
    pieces = []
    offset = 0
    for number in rows:
        pieces.append(whole[offset : offset + number])
        offset = offset + number
    return pieces


def device_index():
    return lax.axis_index("dp") * lax.axis_size("seq") + lax.axis_index("seq")


def modulate(hidden, shift, scale):
    centre = hidden - jnp.mean(hidden, axis=-1, keepdims=True)
    normed = centre * lax.rsqrt(jnp.mean(centre * centre, axis=-1, keepdims=True) + norm_eps)
    return normed * (1.0 + scale) + shift


def gelu_tanh(values):
    return jax.nn.gelu(values, approximate=True)


def time_features(steps_now):
    half_size = FREQ // 2
    frequency = jnp.exp(-math.log(10000.0) * jnp.arange(half_size, dtype=jnp.float32) / half_size)
    angles = steps_now.astype(jnp.float32)[:, None] * frequency[None, :]
    return jnp.concatenate([jnp.cos(angles), jnp.sin(angles)], axis=1)


def noise_level(steps_now):
    phase = (steps_now.astype(jnp.float32) / 1000.0 + 0.008) / 1.008 * (math.pi / 2.0)
    return jnp.cos(phase) ** 2


def variance_logs(level, level_prev):
    beta_now = jnp.minimum(1.0 - level / level_prev, 0.999)
    tilde_log = jnp.log(beta_now * (1.0 - level_prev) / (1.0 - level))
    return (jnp.log(beta_now), tilde_log)


def dot_nn(left, right):
    return lax.dot_general(left, right, (((1,), (0,)), ((), ())), preferred_element_type=jnp.float32)


def dot_nt(left, right):
    return lax.dot_general(left, right, (((1,), (1,)), ((), ())), preferred_element_type=jnp.float32)


def dot_tn(left, right):
    return lax.dot_general(left, right, (((0,), (0,)), ((), ())), preferred_element_type=jnp.float32)


def low(values):
    return values.astype(jnp.bfloat16)


def self_forward_kernel(heads, dim, start_ref, big_ref, qkv_ref, out_ref, key_s, value_s):
    micro = pl.program_id(0)
    blocks = qkv_ref.shape[0]
    scale = dim ** (-0.5)
    for b in range(blocks):
        for h in range(heads):
            rows = pl.ds(b * BLOCK, BLOCK)
            key_s[h, rows, :] = qkv_ref[b, 0, :, (heads + h) * dim : (heads + h + 1) * dim]
            value_s[h, rows, :] = qkv_ref[b, 0, :, (2 * heads + h) * dim : (2 * heads + h + 1) * dim]

    def one_block(b, carry):
        start = pl.multiple_of(start_ref[micro, b] * BLOCK, BLOCK)
        queries = qkv_ref[b, 0]

        def go(span):
            outs = []
            for h in range(heads):
                key = key_s[h, pl.ds(start, span), :]
                value = value_s[h, pl.ds(start, span), :]
                scores = dot_nt(queries[:, h * dim : (h + 1) * dim], key) * scale
                top = jnp.max(scores, axis=-1, keepdims=True)
                weight = jnp.exp(scores - top)
                total = jnp.sum(weight, axis=-1, keepdims=True)
                probs = low(weight * (1.0 / total))
                outs.append(low(dot_nn(probs, value)))
            out_ref[b, 0] = jnp.concatenate(outs, axis=-1)

        big = big_ref[micro, b]

        @pl.when(big == 1)
        def _():
            go(LARGE)

        @pl.when(big == 0)
        def _():
            go(BLOCK)

        return carry

    lax.fori_loop(0, blocks, one_block, 0)


def self_forward(start, big, qkv, heads, dim):
    blocks, micros = qkv.shape[0], qkv.shape[1]
    span = blocks * BLOCK
    return pl.pallas_call(
        functools.partial(self_forward_kernel, heads, dim),
        out_shape=jax.ShapeDtypeStruct((blocks, micros, BLOCK, heads * dim), jnp.bfloat16),
        grid_spec=pltpu.PrefetchScalarGridSpec(
            num_scalar_prefetch=2,
            grid=(micros,),
            in_specs=[pl.BlockSpec((blocks, 1, BLOCK, 3 * heads * dim), lambda m, s, g: (0, m, 0, 0))],
            out_specs=pl.BlockSpec((blocks, 1, BLOCK, heads * dim), lambda m, s, g: (0, m, 0, 0)),
            scratch_shapes=[
                pltpu.VMEM((heads, span, dim), jnp.bfloat16),
                pltpu.VMEM((heads, span, dim), jnp.bfloat16),
            ],
        ),
        compiler_params=pltpu.CompilerParams(vmem_limit_bytes=VMEM_BYTES),
    )(start, big, qkv)


def self_backward_kernel(
    heads, dim, start_ref, big_ref, qkv_ref, grad_ref, out_ref, sum_ref, key_s, value_s, dq_s, dk_s, dv_s
):
    micro = pl.program_id(0)
    blocks = qkv_ref.shape[0]
    scale = dim ** (-0.5)
    for b in range(blocks):
        for h in range(heads):
            rows = pl.ds(b * BLOCK, BLOCK)
            key_s[h, rows, :] = qkv_ref[b, 0, :, (heads + h) * dim : (heads + h + 1) * dim]
            value_s[h, rows, :] = qkv_ref[b, 0, :, (2 * heads + h) * dim : (2 * heads + h + 1) * dim]
    dk_s[...] = jnp.zeros_like(dk_s)
    dv_s[...] = jnp.zeros_like(dv_s)

    def one_block(b, carry):
        start = pl.multiple_of(start_ref[micro, b] * BLOCK, BLOCK)
        place = pl.multiple_of(b * BLOCK, BLOCK)
        queries = qkv_ref[b, 0]
        grads = grad_ref[b, 0]

        def go(span):
            keep = pl.ds(start, span)
            for h in range(heads):
                query = queries[:, h * dim : (h + 1) * dim]
                grad = grads[:, h * dim : (h + 1) * dim]
                key = key_s[h, keep, :]
                value = value_s[h, keep, :]
                scores = dot_nt(key, query) * scale
                top = jnp.max(scores, axis=0, keepdims=True)
                weight = jnp.exp(scores - top)
                probs = weight * (1.0 / jnp.sum(weight, axis=0, keepdims=True))
                dv_s[h, keep, :] += dot_nn(low(probs), grad)
                grad_probs = dot_nt(value, grad)
                inner = jnp.sum(probs * grad_probs, axis=0, keepdims=True)
                grad_scores = low(probs * (grad_probs - inner) * scale)
                dk_s[h, keep, :] += dot_nn(grad_scores, query)
                dq_s[h, pl.ds(place, BLOCK), :] = dot_tn(grad_scores, key)

        big = big_ref[micro, b]

        @pl.when(big == 1)
        def _():
            go(LARGE)

        @pl.when(big == 0)
        def _():
            go(BLOCK)

        return carry

    lax.fori_loop(0, blocks, one_block, 0)
    for b in range(blocks):
        rows = pl.ds(b * BLOCK, BLOCK)
        out_ref[b, 0] = jnp.concatenate(
            [low(part[h, rows, :]) for part in (dq_s, dk_s, dv_s) for h in range(heads)], axis=-1
        )
    sum_ref[0] = jnp.concatenate(
        [jnp.sum(part[h], axis=0, keepdims=True) for part in (dq_s, dv_s) for h in range(heads)], axis=-1
    )


def self_backward(start, big, qkv, grad, heads, dim):
    blocks, micros = qkv.shape[0], qkv.shape[1]
    span = blocks * BLOCK
    wide = pltpu.VMEM((heads, span, dim), jnp.float32)
    narrow = pltpu.VMEM((heads, span, dim), jnp.bfloat16)
    return pl.pallas_call(
        functools.partial(self_backward_kernel, heads, dim),
        out_shape=(
            jax.ShapeDtypeStruct((blocks, micros, BLOCK, 3 * heads * dim), jnp.bfloat16),
            jax.ShapeDtypeStruct((micros, 1, 2 * heads * dim), jnp.float32),
        ),
        grid_spec=pltpu.PrefetchScalarGridSpec(
            num_scalar_prefetch=2,
            grid=(micros,),
            in_specs=[
                pl.BlockSpec((blocks, 1, BLOCK, 3 * heads * dim), lambda m, s, g: (0, m, 0, 0)),
                pl.BlockSpec((blocks, 1, BLOCK, heads * dim), lambda m, s, g: (0, m, 0, 0)),
            ],
            out_specs=(
                pl.BlockSpec((blocks, 1, BLOCK, 3 * heads * dim), lambda m, s, g: (0, m, 0, 0)),
                pl.BlockSpec((1, 1, 2 * heads * dim), lambda m, s, g: (m, 0, 0)),
            ),
            scratch_shapes=[narrow, narrow, wide, wide, wide],
        ),
        compiler_params=pltpu.CompilerParams(vmem_limit_bytes=VMEM_BYTES),
    )(start, big, qkv, grad)


def cross_forward_kernel(dim, length_ref, query_ref, key_ref, value_ref, out_ref):
    length = length_ref[pl.program_id(0)]
    scale = dim ** (-0.5)
    live = lax.broadcasted_iota(jnp.int32, (BLOCK, CAP_PAD), 1) < length
    outs = []
    for h in range(HEADS):
        part = slice(h * dim, (h + 1) * dim)
        scores = jnp.where(live, dot_nt(query_ref[0, :, part], key_ref[0, :, part]) * scale, neg_large)
        weight = jnp.exp(scores - jnp.max(scores, axis=-1, keepdims=True))
        probs = low(weight * (1.0 / jnp.sum(weight, axis=-1, keepdims=True)))
        outs.append(low(dot_nn(probs, value_ref[0, :, part])))
    out_ref[0] = jnp.concatenate(outs, axis=-1)


def cross_backward_kernel(
    dim, length_ref, query_ref, key_ref, value_ref, grad_ref, dq_ref, dk_ref, dv_ref
):
    length = length_ref[pl.program_id(0)]
    scale = dim ** (-0.5)
    live = lax.broadcasted_iota(jnp.int32, (CAP_PAD, BLOCK), 0) < length
    dq, dk, dv = [], [], []
    for h in range(HEADS):
        part = slice(h * dim, (h + 1) * dim)
        query, key, value, grad = (
            query_ref[0, :, part],
            key_ref[0, :, part],
            value_ref[0, :, part],
            grad_ref[0, :, part],
        )
        scores = jnp.where(live, dot_nt(key, query) * scale, neg_large)
        weight = jnp.exp(scores - jnp.max(scores, axis=0, keepdims=True))
        probs = weight * (1.0 / jnp.sum(weight, axis=0, keepdims=True))
        dv.append(dot_nn(low(probs), grad))
        grad_probs = dot_nt(value, grad)
        inner = jnp.sum(probs * grad_probs, axis=0, keepdims=True)
        grad_scores = low(probs * (grad_probs - inner) * scale)
        dk.append(dot_nn(grad_scores, query))
        dq.append(dot_tn(grad_scores, key))
    dq_ref[0] = jnp.concatenate(dq, axis=-1)
    dk_ref[0] = jnp.concatenate(dk, axis=-1)
    dv_ref[0] = jnp.concatenate(dv, axis=-1)


def cross_call(kernel, length, arrays, outs):
    def spec(array):
        return pl.BlockSpec((1,) + array.shape[1:], lambda m, s: (m, 0, 0))

    return pl.pallas_call(
        kernel,
        out_shape=outs,
        grid_spec=pltpu.PrefetchScalarGridSpec(
            num_scalar_prefetch=1,
            grid=(MICRO,),
            in_specs=[spec(array) for array in arrays],
            out_specs=jax.tree.map(spec, outs),
        ),
        compiler_params=pltpu.CompilerParams(vmem_limit_bytes=VMEM_BYTES),
    )(length, *arrays)


UNIT = 8
SPLIT = 640
PIECE = 3
TILE = 96
TILE_START = 1024
LAG = 2
RING = LAG + 1
MESH = pl.DeviceIdType.MESH


def my_place():
    row, seq = lax.axis_index("dp"), lax.axis_index("seq")
    return lax.div(row, 2), lax.rem(row, 2), lax.div(seq, 2), lax.rem(seq, 2)


def peer(y, core, z, x):
    return (y * 2 + core, z * 2 + x)


def greet_all(devices, seq_count):
    me = lax.axis_index("dp") * seq_count + lax.axis_index("seq")
    barrier = pltpu.get_barrier_semaphore()

    def one(step, carry):
        other = lax.rem(me + step, devices)
        pl.semaphore_signal(
            barrier,
            inc=1,
            device_id=(lax.div(other, seq_count), lax.rem(other, seq_count)),
            device_id_type=MESH,
        )
        return carry

    lax.fori_loop(1, devices, one, 0)
    pl.semaphore_wait(barrier, devices - 1)


def global_tile(ranges, index):
    tile = index + ranges[0][0]
    at = ranges[0][1] - ranges[0][0]
    for start, stop in ranges[1:]:
        tile = jnp.where(index >= at, index - at + start, tile)
        at += stop - start
    return tile


def reduce_kernel(
    ranges,
    shard_units,
    devices,
    sources,
    receivers,
    *refs,
):
    rows_refs, refs = refs[: len(sources)], list(refs[len(sources) :])
    if receivers:
        block_ref, all_ref = refs.pop(0), refs.pop(1)
        refs, push_sems = refs[:-3], refs[-3:]
    (
    out_ref,
    own_s,
    core_s,
    first_s,
    second_s,
    first_y_s,
    second_x_s,
    first_two_s,
    second_two_s,
    first_x_s,
    second_y_s,
    third_s,
    along_s,
    leaf_s,
    load_sem,
    core_send,
    core_recv,
    one_send,
    one_recv,
    two_send,
    two_recv,
    z_send,
    z_recv,
    leaf_send,
    leaf_recv,
    ) = refs
    tiles = core_s.shape[0]
    seq_count = devices // 4
    y, core, z, x = my_place()
    me = (y * 2 + core) * seq_count + z * 2 + x
    place = ((core * 2 + y) * 2 + x) * 4 + z
    half, quarter, eighth = TILE // 2, TILE // 4, TILE // 8
    across_core = peer(y, 1 - core, z, x)
    across_y = peer(1 - y, core, z, x)
    across_x = peer(y, core, z, 1 - x)

    def remote(source, target, send, recv, device):
        return pltpu.make_async_remote_copy(
            src_ref=source,
            dst_ref=target,
            send_sem=send,
            recv_sem=recv,
            device_id=device,
            device_id_type=MESH,
        )

    def core_copy(t, rows_ref=None, start=0):
        source = own_s.at[0] if rows_ref is None else rows_ref.at[pl.ds(start, half)]
        return remote(source, core_s.at[t], core_send.at[t], core_recv.at[t], across_core)

    def load(t, rows_ref=None, start=0):
        slot = lax.rem(t, 2)
        source = rows_refs[-1] if rows_ref is None else rows_ref
        return pltpu.make_async_copy(
            source.at[pl.ds(start, half)], own_s.at[slot], load_sem.at[slot]
        )

    def start_from(copy, t, side):
        index = t * 2 + side
        at = 0
        for rows_ref, (start, count) in zip(rows_refs, sources):

            @pl.when((index >= at) & (index < at + count))
            def _(rows_ref=rows_ref, start=start, at=at):
                copy(t, rows_ref, start + (index - at) * half).start()

            at += count

    def first_one(t):
        return remote(
            first_s.at[lax.rem(t, RING), pl.ds((1 - y) * quarter, quarter)],
            first_y_s.at[t],
            one_send.at[lax.rem(t, RING), 0],
            one_recv.at[t, 0],
            across_y,
        )

    def second_one(t, side):
        return remote(
            second_s.at[lax.rem(t, RING), pl.ds(side * quarter + (1 - x) * eighth, eighth)],
            second_x_s.at[t, pl.ds(side * eighth, eighth)],
            one_send.at[lax.rem(t, RING), 1 + side],
            one_recv.at[t, 1 + side],
            across_x,
        )

    def first_two(t):
        return remote(
            first_two_s.at[lax.rem(t, RING), pl.ds((1 - x) * eighth, eighth)],
            first_x_s.at[t],
            two_send.at[lax.rem(t, RING), 0],
            two_recv.at[t, 0],
            across_x,
        )

    def second_two(t):
        return remote(
            second_two_s.at[lax.rem(t, RING), pl.ds((1 - y) * eighth, eighth)],
            second_y_s.at[t],
            two_send.at[lax.rem(t, RING), 1],
            two_recv.at[t, 1],
            across_y,
        )

    def z_copy(t, distance):
        other = z ^ distance
        return remote(
            third_s.at[lax.rem(t, RING), pl.ds(other * PIECE, PIECE)],
            along_s.at[t, distance - 1],
            z_send.at[lax.rem(t, RING), distance - 1],
            z_recv.at[t, distance - 1],
            peer(y, core, other, x),
        )

    def add(count, step, target, *sources):
        def one(index, carry):
            at = index * step
            total = sources[0](at, step).astype(jnp.float32)
            for source in sources[1:]:
                total = total + source(at, step).astype(jnp.float32)
            target(at, step, total.astype(jnp.bfloat16))
            return carry

        lax.fori_loop(0, count // step, one, 0)

    def leaf_send_all(t, stage):
        unit = TILE_START + global_tile(ranges, t) * TILE + place * PIECE
        owner = lax.div(unit, shard_units)
        at = unit - owner * shard_units

        def go(part, count, slot, holder):
            source = leaf_s.at[t, pl.ds(part, count)]
            target = out_ref.at[pl.ds(slot, count)]
            sending = remote(
                source,
                target,
                leaf_send.at[t, part],
                leaf_recv.at[slot],
                (lax.div(holder, seq_count), lax.rem(holder, seq_count)),
            )

            @pl.when(holder != me)
            def _():
                if stage == 0:
                    sending.start()
                else:
                    sending.wait_send()

            if stage == 0:

                @pl.when(holder == me)
                def _():
                    pltpu.make_async_copy(source, target, leaf_recv.at[slot]).start()

        together = at + PIECE <= shard_units

        @pl.when(together)
        def _():
            go(0, PIECE, at, owner)

        @pl.when(jnp.logical_not(together))
        def _():
            for part in range(PIECE):
                over = at + part >= shard_units
                go(
                    part,
                    1,
                    jnp.where(over, at + part - shard_units, at + part),
                    jnp.where(over, owner + 1, owner),
                )

    for t in range(min(2, tiles)):
        start_from(load, t, core)
    greet_all(devices, seq_count)

    def start_core(t, carry):
        start_from(core_copy, t, 1 - core)
        return carry

    lax.fori_loop(0, tiles, start_core, 0)
    if receivers:
        start_push(block_ref, all_ref, devices, receivers, me, *push_sems)

    def one_step(step, carry):
        @pl.when(step < tiles)
        def _():
            t = step
            slot = lax.rem(t, RING)
            load(t).wait()
            core_copy(t).wait_recv()

            def one(index, inner):
                at = pl.ds(index * 4, 4)
                total = own_s[lax.rem(t, 2), at].astype(jnp.float32) + core_s[t, at].astype(jnp.float32)
                total = total.astype(jnp.bfloat16)
                first_s[slot, at] = total[:, :, :SPLIT]
                second_s[slot, at] = total[:, :, SPLIT:]
                return inner

            lax.fori_loop(0, half // 4, one, 0)
            first_one(t).start()
            second_one(t, 0).start()
            second_one(t, 1).start()

            @pl.when(t + 2 < tiles)
            def _():
                start_from(load, t + 2, core)

        @pl.when((step >= LAG) & (step < tiles + LAG))
        def _():
            t = step - LAG
            slot = lax.rem(t, RING)
            first_one(t).wait()

            def one(index, inner):
                at = pl.ds(index * 4, 4)
                mine = first_s[slot, pl.ds(y * quarter + index * 4, 4)].astype(jnp.float32)
                total = mine + first_y_s[t, at].astype(jnp.float32)
                first_two_s[slot, at] = total.astype(jnp.bfloat16)
                return inner

            lax.fori_loop(0, quarter // 4, one, 0)
            first_two(t).start()
            for side in range(2):
                second_one(t, side).wait()

                def two(index, inner):
                    mine = second_s[slot, pl.ds(side * quarter + x * eighth + index * 4, 4)]
                    at = pl.ds(side * eighth + index * 4, 4)
                    total = mine.astype(jnp.float32) + second_x_s[t, at].astype(jnp.float32)
                    second_two_s[slot, at] = total.astype(jnp.bfloat16)
                    return inner

                lax.fori_loop(0, eighth // 4, two, 0)
            second_two(t).start()

        @pl.when((step >= 2 * LAG) & (step < tiles + 2 * LAG))
        def _():
            t = step - 2 * LAG
            slot = lax.rem(t, RING)
            first_two(t).wait()
            second_two(t).wait()

            def one(index, inner):
                at = pl.ds(index * 4, 4)
                mine = first_two_s[slot, pl.ds(x * eighth + index * 4, 4)].astype(jnp.float32)
                total = mine + first_x_s[t, at].astype(jnp.float32)
                third_s[slot, at, :, :SPLIT] = total.astype(jnp.bfloat16)
                mine = second_two_s[slot, pl.ds(y * eighth + index * 4, 4)].astype(jnp.float32)
                total = mine + second_y_s[t, at].astype(jnp.float32)
                third_s[slot, at, :, SPLIT:] = total.astype(jnp.bfloat16)
                return inner

            lax.fori_loop(0, eighth // 4, one, 0)
            for distance in (1, 2, 3):
                z_copy(t, distance).start()

        @pl.when(step >= 3 * LAG)
        def _():
            t = step - 3 * LAG
            slot = lax.rem(t, RING)
            for distance in (1, 2, 3):
                z_copy(t, distance).wait()
            total = third_s[slot, pl.ds(z * PIECE, PIECE)].astype(jnp.float32)
            for distance in (1, 2, 3):
                total = total + along_s[t, distance - 1].astype(jnp.float32)
            leaf_s[t] = total.astype(jnp.bfloat16)
            leaf_send_all(t, 0)

        return carry

    lax.fori_loop(0, tiles + 3 * LAG, one_step, 0)

    def finish(t, carry):
        core_copy(t).wait_send()
        leaf_send_all(t, 1)
        return carry

    lax.fori_loop(0, tiles, finish, 0)
    if receivers:
        finish_push(block_ref, all_ref, devices, receivers, me, *push_sems)
    far = TILE_START - TILE * (TILE_START // TILE)
    begin = me * shard_units
    first_at = lax.rem(PIECE - lax.rem(begin + PIECE - far % PIECE, PIECE), PIECE)

    def arrive(index, count):
        unit = begin + index
        inside = False
        for start, stop in ranges:
            low_end, high_end = TILE_START + start * TILE, TILE_START + stop * TILE
            inside = inside | ((unit >= low_end) & (unit < high_end))

        @pl.when(inside)
        def _():
            part = out_ref.at[pl.ds(index, count)]
            pltpu.make_async_copy(part, part, leaf_recv.at[index]).wait()

    def arrive_three(step, carry):
        index = first_at + step * PIECE

        @pl.when(index + PIECE <= shard_units)
        def _():
            arrive(index, PIECE)

        return carry

    steps = shard_units // PIECE
    lax.fori_loop(0, steps, arrive_three, 0)
    covered = first_at + lax.div(shard_units - first_at, PIECE) * PIECE
    for step in range(PIECE - 1):

        @pl.when(step < first_at)
        def _():
            arrive(step, 1)

        @pl.when(covered + step < shard_units)
        def _():
            arrive(covered + step, 1)


def push_copy(block_ref, all_ref, devices, me, step, send_sem, recv_sem):
    seq_count = devices // 4
    other = lax.rem(me + step, devices)
    return other, pltpu.make_async_remote_copy(
        src_ref=block_ref,
        dst_ref=all_ref.at[me],
        send_sem=send_sem.at[step],
        recv_sem=recv_sem.at[me],
        device_id=(lax.div(other, seq_count), lax.rem(other, seq_count)),
        device_id_type=MESH,
    )


def start_push(block_ref, all_ref, devices, receivers, me, send_sem, recv_sem, keep_sem):
    @pl.when(me < receivers)
    def _():
        pltpu.make_async_copy(block_ref, all_ref.at[me], keep_sem).start()

    def send(step, carry):
        other, sending = push_copy(block_ref, all_ref, devices, me, step, send_sem, recv_sem)

        @pl.when(other < receivers)
        def _():
            sending.start()

        return carry

    lax.fori_loop(1, devices, send, 0)


def finish_push(block_ref, all_ref, devices, receivers, me, send_sem, recv_sem, keep_sem):
    @pl.when(me < receivers)
    def _():
        pltpu.make_async_copy(block_ref, all_ref.at[me], keep_sem).wait()

    def finish(step, carry):
        other, sending = push_copy(block_ref, all_ref, devices, me, step, send_sem, recv_sem)

        @pl.when(other < receivers)
        def _():
            sending.wait_send()

        source = lax.rem(me + devices - step, devices)

        @pl.when(me < receivers)
        def _():
            pltpu.make_async_copy(block_ref, all_ref.at[source], recv_sem.at[source]).wait()

        return carry

    lax.fori_loop(1, devices, finish, 0)


def push_sems(devices):
    dma = pltpu.SemaphoreType.DMA
    return [dma((devices,)), dma((devices,)), dma]


def reduce_rows(ranges, shard_units, devices, collective_id, pieces, block=None, receivers=0):
    tiles = sum(stop - start for start, stop in ranges)
    width = pieces[0][0].shape[1]
    sources = tuple(piece[1:] for piece in pieces)
    assert sum(count for _, count in sources) == 2 * tiles
    half, quarter, eighth = TILE // 2, TILE // 4, TILE // 8
    rest = width - SPLIT

    def vmem(*shape):
        return pltpu.VMEM(shape, jnp.bfloat16)

    dma = pltpu.SemaphoreType.DMA
    blocks = [] if block is None else [block]
    outs = [jax.ShapeDtypeStruct((shard_units, UNIT, width), jnp.bfloat16)]
    outs += [jax.ShapeDtypeStruct((devices,) + one.shape, one.dtype) for one in blocks]
    out = pl.pallas_call(
        functools.partial(reduce_kernel, ranges, shard_units, devices, sources, receivers),
        out_shape=outs,
        in_specs=[pl.BlockSpec(memory_space=pl.ANY)] * (len(pieces) + len(blocks)),
        out_specs=[pl.BlockSpec(memory_space=pl.ANY)] * len(outs),
        scratch_shapes=[
            vmem(2, half, UNIT, width),
            vmem(tiles, half, UNIT, width),
            vmem(RING, half, UNIT, SPLIT),
            vmem(RING, half, UNIT, rest),
            vmem(tiles, quarter, UNIT, SPLIT),
            vmem(tiles, quarter, UNIT, rest),
            vmem(RING, quarter, UNIT, SPLIT),
            vmem(RING, quarter, UNIT, rest),
            vmem(tiles, eighth, UNIT, SPLIT),
            vmem(tiles, eighth, UNIT, rest),
            vmem(RING, eighth, UNIT, width),
            vmem(tiles, 3, PIECE, UNIT, width),
            vmem(tiles, PIECE, UNIT, width),
            dma((2,)),
            dma((tiles,)),
            dma((tiles,)),
            dma((RING, 3)),
            dma((tiles, 3)),
            dma((RING, 2)),
            dma((tiles, 2)),
            dma((RING, 3)),
            dma((tiles, 3)),
            dma((tiles, PIECE)),
            dma((shard_units,)),
        ]
        + (push_sems(devices) if blocks else []),
        compiler_params=pltpu.CompilerParams(
            collective_id=collective_id, has_side_effects=True, vmem_limit_bytes=VMEM_BYTES
        ),
    )(*[piece[0].reshape(-1, UNIT, width) for piece in pieces], *blocks)
    return out if blocks else out[0]


STRIDE = 3
Z_LAG = 2
Z_RING = 3 * Z_LAG + 1


def gather_kernel(
    openings,
    ahead,
    devices,
    shard_ref,
    out_ref,
    later_ref,
    deal_send,
    deal_recv,
    z_send,
    z_recv,
    one_send,
    one_recv,
    two_send,
    two_recv,
    core_send,
    core_recv,
):
    shard_units = shard_ref.shape[0]
    seq_count = devices // 4
    width = shard_ref.shape[2]
    tiles = out_ref.shape[0] // TILE
    later_tiles = later_ref.shape[0] // TILE
    streams = ((openings[0], tiles, out_ref, 0), (openings[1], later_tiles, later_ref, tiles))
    y, core, z, x = my_place()
    me = (y * 2 + core) * seq_count + z * 2 + x
    half, quarter, eighth = TILE // 2, TILE // 4, TILE // 8
    leaves = TILE // PIECE
    upward = peer(y, core, jnp.minimum(z + 1, 3), x)
    downward = peer(y, core, jnp.maximum(z - 1, 0), x)

    def bounds(stream):
        begin = me * shard_units - stream[0]
        finish = begin + shard_units
        return begin, finish, lax.div(begin + PIECE - 1, PIECE), lax.div(finish, PIECE)

    def deal_some(stream, stage, three, part, count):
        begin = bounds(stream)[0]
        ref = stream[2]
        tile = lax.div(three, leaves)
        leaf = three - tile * leaves
        eight = lax.div(leaf, 4)
        slot = leaf - eight * 4 if count == PIECE else 4 + part
        holder_core = lax.div(eight, 4)
        holder_y = lax.rem(lax.div(eight, 2), 2)
        holder_x = lax.rem(eight, 2)
        holder = (holder_y * 2 + holder_core) * seq_count + z * 2 + holder_x
        index = three * PIECE + part - begin
        source = shard_ref.at[pl.ds(index, count)]
        target = ref.at[pl.ds(three * PIECE + part, count)]
        recv = deal_recv.at[stream[3] + tile, slot]
        sending = pltpu.make_async_remote_copy(
            src_ref=source,
            dst_ref=target,
            send_sem=deal_send.at[0 if stream[3] == 0 else 1, index],
            recv_sem=recv,
            device_id=peer(holder_y, holder_core, z, holder_x),
            device_id_type=MESH,
        )

        @pl.when(holder != me)
        def _():
            if stage == 0:
                sending.start()
            else:
                sending.wait_send()

        if stage == 0:

            @pl.when(holder == me)
            def _():
                pltpu.make_async_copy(source, target, recv).start()

    def deal_between(stream, stage, low_three, count, base):
        begin, finish, first_three, last_three = bounds(stream)
        base = first_three if base is None else base

        @pl.when((low_three <= last_three) & (low_three + count >= first_three))
        def _():
            def one(step, carry):
                three = base + step

                @pl.when(
                    (three >= first_three)
                    & (three < last_three)
                    & (three >= low_three)
                    & (three < low_three + count)
                )
                def _():
                    deal_some(stream, stage, three, 0, PIECE)

                return carry

            lax.fori_loop(0, min(count, shard_units // PIECE + 1), one, 0)
            for step in range(PIECE - 1):
                three = first_three - 1
                here = (three >= low_three) & (three < low_three + count)

                @pl.when(here & (begin + step < first_three * PIECE))
                def _(three=three):
                    deal_some(stream, stage, three, begin + step - three * PIECE, 1)

                three = last_three
                here = (three >= low_three) & (three < low_three + count)

                @pl.when(here & (three * PIECE + step < finish))
                def _(three=three):
                    deal_some(stream, stage, three, step, 1)

    def deal_tile(stream, step):
        low_three = tile_at(step, stream[1]) * leaves
        deal_between(stream, 0, low_three, leaves, low_three)

    def each_three(stream, t, visit):
        def one(index, carry):
            row = t * TILE + ((core * 2 + y) * 2 + x) * eighth + index * PIECE
            unit = stream[0] + row
            owner = lax.div(unit, shard_units)
            at = unit - owner * shard_units

            @pl.when(at + PIECE <= shard_units)
            def _():
                visit(row, index, PIECE, lax.rem(lax.div(owner, 2), 4))

            @pl.when(at + PIECE > shard_units)
            def _():
                for part in range(PIECE):
                    holder = jnp.where(at + part >= shard_units, owner + 1, owner)
                    visit(row + part, 4 + part, 1, lax.rem(lax.div(holder, 2), 4))

            return carry

        lax.fori_loop(0, eighth // PIECE, one, 0)

    def wait_units(ref, count, sem):
        part = ref.at[pl.ds(0, count)]
        pltpu.make_async_copy(part, part, sem).wait()

    def z_copy(stream, step, row, slot, count, way):
        part = stream[2].at[pl.ds(row, count)]
        which = 0 if stream[3] == 0 else 1
        return pltpu.make_async_remote_copy(
            src_ref=part,
            dst_ref=part,
            send_sem=z_send.at[which, lax.rem(step, Z_RING), slot, way],
            recv_sem=z_recv.at[stream[3] + tile_at(step, stream[1]), slot],
            device_id=(upward, downward)[way],
            device_id_type=MESH,
        )

    def along_z(stream, step, distance):
        t = tile_at(step, stream[1])

        def visit(row, slot, count, owner_z):
            @pl.when(jnp.abs(owner_z - z) == distance)
            def _():
                sem = deal_recv if distance == 0 else z_recv
                wait_units(out_ref, count, sem.at[stream[3] + t, slot])

                @pl.when((owner_z <= z) & (z < 3))
                def _():
                    z_copy(stream, step, row, slot, count, 0).start()

                @pl.when((owner_z >= z) & (z > 0))
                def _():
                    z_copy(stream, step, row, slot, count, 1).start()

        each_three(stream, t, visit)

    def along_z_done(stream, step):
        t = tile_at(step, stream[1])

        def visit(row, slot, count, owner_z):
            @pl.when((owner_z <= z) & (z < 3))
            def _():
                z_copy(stream, step, row, slot, count, 0).wait_send()

            @pl.when((owner_z >= z) & (z > 0))
            def _():
                z_copy(stream, step, row, slot, count, 1).wait_send()

        each_three(stream, t, visit)

    def z_stage(stream, step):
        for distance in range(4):
            old = step - distance * Z_LAG

            @pl.when((old >= 0) & (old < stream[1]))
            def _(old=old, distance=distance):
                along_z(stream, old, distance)
                if distance == 3:
                    along_z_done(stream, old)

    spreading = spread_steps(
        out_ref, one_send, one_recv, two_send, two_recv, core_send, core_recv
    )
    main, late = streams
    greet_all(devices, seq_count)
    for step in range(min(ahead, tiles)):
        deal_tile(main, step)
    for step in range(min(ahead, later_tiles)):
        deal_tile(late, step)

    def one_step(step, carry):
        @pl.when(step + ahead < tiles)
        def _():
            deal_tile(main, step + ahead)

        @pl.when(step + ahead < later_tiles)
        def _():
            deal_tile(late, step + ahead)

        z_stage(main, step)
        spreading(step - 3 * Z_LAG)
        z_stage(late, step)
        return carry

    lax.fori_loop(0, tiles + 3 * LAG + 3 * Z_LAG, one_step, 0)
    for stream in streams:
        deal_between(stream, 1, 0, stream[1] * leaves, None)


def tile_at(step, tiles):
    return lax.rem(step * STRIDE, tiles)


def spread_steps(out_ref, one_send, one_recv, two_send, two_recv, core_send, core_recv):
    tiles = out_ref.shape[0] // TILE
    width = out_ref.shape[2]
    y, core, z, x = my_place()
    half, quarter, eighth = TILE // 2, TILE // 4, TILE // 8
    left, right = pl.ds(0, SPLIT), pl.ds(SPLIT, width - SPLIT)
    whole = pl.ds(0, width)
    across_core = peer(y, 1 - core, z, x)
    across_y = peer(1 - y, core, z, x)
    across_x = peer(y, core, z, 1 - x)

    def remote(start, count, columns, send, recv, device):
        part = out_ref.at[pl.ds(start, count), :, columns]
        return pltpu.make_async_remote_copy(
            src_ref=part,
            dst_ref=part,
            send_sem=send,
            recv_sem=recv,
            device_id=device,
            device_id_type=MESH,
        )

    def block(t, y_at, x_at):
        return t * TILE + ((core * 2 + y_at) * 2 + x_at) * eighth

    def one_first(step):
        t = tile_at(step, tiles)
        sems = (one_send.at[lax.rem(step, RING), 0], one_recv.at[t, 0])
        return remote(block(t, y, x), eighth, left, *sems, across_x)

    def one_second(step):
        t = tile_at(step, tiles)
        sems = (one_send.at[lax.rem(step, RING), 1], one_recv.at[t, 1])
        return remote(block(t, y, x), eighth, right, *sems, across_y)

    def two_first(step):
        t = tile_at(step, tiles)
        sems = (two_send.at[lax.rem(step, RING), 0], two_recv.at[t, 0])
        return remote(block(t, y, 0), quarter, left, *sems, across_y)

    def two_second(step, side):
        t = tile_at(step, tiles)
        sems = (two_send.at[lax.rem(step, RING), 1 + side], two_recv.at[t, 1 + side])
        return remote(block(t, side, x), eighth, right, *sems, across_x)

    def core_copy(step):
        t = tile_at(step, tiles)
        sems = (core_send.at[lax.rem(step, RING)], core_recv.at[t])
        return remote(t * TILE + core * half, half, whole, *sems, across_core)

    def go(step):
        @pl.when((step >= 0) & (step < tiles))
        def _():
            one_first(step).start()
            one_second(step).start()

        @pl.when((step >= LAG) & (step < tiles + LAG))
        def _():
            old = step - LAG
            one_first(old).wait()
            two_first(old).start()
            one_second(old).wait()
            for side in range(2):
                two_second(old, side).start()

        @pl.when((step >= 2 * LAG) & (step < tiles + 2 * LAG))
        def _():
            old = step - 2 * LAG
            two_first(old).wait()
            for side in range(2):
                two_second(old, side).wait()
            core_copy(old).start()

        @pl.when(step >= 3 * LAG)
        def _():
            core_copy(step - 3 * LAG).wait()

    return go


def spread_sems(tiles):
    dma = pltpu.SemaphoreType.DMA
    return [
        dma((RING, 2)),
        dma((tiles, 2)),
        dma((RING, 3)),
        dma((tiles, 3)),
        dma((RING,)),
        dma((tiles,)),
    ]


def spread_kernel(devices, rows_ref, block_ref, out_ref, all_ref, *sems):
    seq_count = devices // 4
    me = lax.axis_index("dp") * seq_count + lax.axis_index("seq")
    sems, push = sems[:-3], sems[-3:]
    greet_all(devices, seq_count)
    start_push(block_ref, all_ref, devices, devices, me, *push)
    spreading = spread_steps(out_ref, *sems)

    def one_step(step, carry):
        spreading(step)
        return carry

    lax.fori_loop(0, out_ref.shape[0] // TILE + 3 * LAG, one_step, 0)
    finish_push(block_ref, all_ref, devices, devices, me, *push)


def spread_rows(rows, block, devices, collective_id):
    return pl.pallas_call(
        functools.partial(spread_kernel, devices),
        out_shape=(
            jax.ShapeDtypeStruct(rows.shape, rows.dtype),
            jax.ShapeDtypeStruct((devices,) + block.shape, block.dtype),
        ),
        in_specs=[pl.BlockSpec(memory_space=pl.ANY)] * 2,
        out_specs=(pl.BlockSpec(memory_space=pl.ANY), pl.BlockSpec(memory_space=pl.ANY)),
        scratch_shapes=spread_sems(rows.shape[0] // TILE) + push_sems(devices),
        input_output_aliases={0: 0},
        compiler_params=pltpu.CompilerParams(
            collective_id=collective_id, has_side_effects=True, vmem_limit_bytes=VMEM_BYTES
        ),
    )(rows, block)


def gather_rows(openings, counts, ahead, devices, collective_id, shard):
    units, _, width = shard.shape
    assert all(count % STRIDE for count in counts) and counts[1] <= counts[0]
    dma = pltpu.SemaphoreType.DMA
    anywhere = pl.BlockSpec(memory_space=pl.ANY)
    return pl.pallas_call(
        functools.partial(gather_kernel, openings, ahead, devices),
        out_shape=[
            jax.ShapeDtypeStruct((count * TILE, UNIT, width), jnp.bfloat16) for count in counts
        ],
        in_specs=[anywhere],
        out_specs=[anywhere, anywhere],
        scratch_shapes=[
            dma((2, units)),
            dma((sum(counts), 7)),
            dma((2, Z_RING, 7, 2)),
            dma((sum(counts), 7)),
        ]
        + spread_sems(counts[0]),
        compiler_params=pltpu.CompilerParams(
            collective_id=collective_id, has_side_effects=True, vmem_limit_bytes=VMEM_BYTES
        ),
    )(shard)


def share_kernel(devices, block_ref, out_ref, *sems):
    seq_count = devices // 4
    me = lax.axis_index("dp") * seq_count + lax.axis_index("seq")
    greet_all(devices, seq_count)
    start_push(block_ref, out_ref, devices, devices, me, *sems)
    finish_push(block_ref, out_ref, devices, devices, me, *sems)


def share(block, devices, collective_id):
    return pl.pallas_call(
        functools.partial(share_kernel, devices),
        out_shape=jax.ShapeDtypeStruct((devices,) + block.shape, block.dtype),
        in_specs=[pl.BlockSpec(memory_space=pltpu.VMEM)],
        out_specs=pl.BlockSpec(memory_space=pltpu.VMEM),
        scratch_shapes=push_sems(devices),
        compiler_params=pltpu.CompilerParams(
            collective_id=collective_id, has_side_effects=True, vmem_limit_bytes=16 * 1024 * 1024
        ),
    )(block)


def sum_kernel(devices, parts_ref, out_ref, extra_ref, got_s, part_s, send_sem, recv_sem, keep_sem, *sems):
    seq_count = devices // 4
    me = lax.axis_index("dp") * seq_count + lax.axis_index("seq")
    keep = pltpu.make_async_copy(parts_ref.at[me], got_s.at[me], keep_sem)
    keep.start()
    greet_all(devices, seq_count)

    def scatter(step):
        other = lax.rem(me + step, devices)
        return pltpu.make_async_remote_copy(
            src_ref=parts_ref.at[other],
            dst_ref=got_s.at[me],
            send_sem=send_sem.at[step],
            recv_sem=recv_sem.at[me],
            device_id=(lax.div(other, seq_count), lax.rem(other, seq_count)),
            device_id_type=MESH,
        )

    def start(step, carry):
        scatter(step).start()
        return carry

    def finish(step, carry):
        scatter(step).wait_send()
        source = lax.rem(me + devices - step, devices)
        pltpu.make_async_copy(parts_ref.at[0], got_s.at[source], recv_sem.at[source]).wait()
        return carry

    lax.fori_loop(1, devices, start, 0)
    keep.wait()
    lax.fori_loop(1, devices, finish, 0)
    total = jnp.sum(got_s[...], axis=0)
    part_s[...] = total[:-1]
    extra_ref[...] = total[-1]
    start_push(part_s, out_ref, devices, devices, me, *sems)
    finish_push(part_s, out_ref, devices, devices, me, *sems)


def sum_all(array, extra, devices, collective_id):
    tile = 8 * 128
    count = -(-array.size // (tile * devices))
    flat = jnp.pad(array.reshape(-1), (0, count * tile * devices - array.size))
    parts = flat.reshape(devices, count, 8, 128)
    parts = jnp.concatenate([parts, jnp.full((devices, 1, 8, 128), extra)], axis=1)
    vmem = pl.BlockSpec(memory_space=pltpu.VMEM)
    out, total = pl.pallas_call(
        functools.partial(sum_kernel, devices),
        out_shape=(
            jax.ShapeDtypeStruct((devices, count, 8, 128), jnp.float32),
            jax.ShapeDtypeStruct((8, 128), jnp.float32),
        ),
        in_specs=[vmem],
        out_specs=(vmem, vmem),
        scratch_shapes=[
            pltpu.VMEM((devices, count + 1, 8, 128), jnp.float32),
            pltpu.VMEM((count, 8, 128), jnp.float32),
        ]
        + push_sems(devices)
        + push_sems(devices),
        compiler_params=pltpu.CompilerParams(
            collective_id=collective_id, has_side_effects=True, vmem_limit_bytes=16 * 1024 * 1024
        ),
    )(parts)
    return out.reshape(-1)[: array.size].reshape(array.shape), total[0, 0]


def contrast_kernel(pooled_ref, pick_ref, row_ref, col_ref, scale_ref, pool_ref, text_ref, loss_ref):
    count = pick_ref.shape[1]
    scale = scale_ref[0, 0] / contrastive_sharpness_divisor
    diagonal = lax.broadcasted_iota(jnp.int32, (count, count), 0) == lax.broadcasted_iota(
        jnp.int32, (count, count), 1
    )
    loss = jnp.zeros((1, 1), jnp.float32)
    for m in range(MICRO):
        row = row_ref[m]
        col = col_ref[m] > 0.0
        image = jnp.dot(
            pick_ref[m], pooled_ref[m], precision=exact, preferred_element_type=jnp.float32
        )
        words = pooled_ref[MICRO + m]
        image_norm = lax.rsqrt(jnp.sum(image * image, axis=-1, keepdims=True) + norm_eps)
        words_norm = lax.rsqrt(jnp.sum(words * words, axis=-1, keepdims=True) + norm_eps)
        image = image * image_norm
        words = words * words_norm
        cosines = lax.dot_general(
            image,
            words,
            (((1,), (1,)), ((), ())),
            precision=exact,
            preferred_element_type=jnp.float32,
        )
        cosines = jnp.where(col, cosines / contrastive_sharpness_divisor, neg_large)
        top = jnp.max(cosines, axis=-1, keepdims=True)
        weight = jnp.exp(cosines - top)
        total = jnp.sum(weight, axis=-1, keepdims=True)
        matched = jnp.sum(jnp.where(diagonal, cosines, 0.0), axis=-1, keepdims=True)
        lost = jnp.where(row > 0.0, top + jnp.log(total) - matched, 0.0)
        loss = loss + jnp.sum(lost, axis=0, keepdims=True)
        grad = weight / total - jnp.where(diagonal, 1.0, 0.0)
        grad = jnp.where((row > 0.0) & col, grad * scale, 0.0)
        grad_image = jnp.dot(grad, words, precision=exact, preferred_element_type=jnp.float32)
        grad_words = lax.dot_general(
            grad,
            image,
            (((0,), (0,)), ((), ())),
            precision=exact,
            preferred_element_type=jnp.float32,
        )
        inner = jnp.sum(image * grad_image, axis=-1, keepdims=True)
        pool_ref[m] = image_norm * (grad_image - image * inner)
        inner = jnp.sum(words * grad_words, axis=-1, keepdims=True)
        text_ref[m] = words_norm * (grad_words - words * inner)
    loss_ref[...] = jnp.broadcast_to(loss, loss_ref.shape)


def contrast(pooled, pick, valid, scale):
    count, width = pooled.shape[1], pooled.shape[2]
    grads = jax.ShapeDtypeStruct((MICRO, count, width), jnp.float32)
    return pl.pallas_call(
        contrast_kernel,
        out_shape=(grads, grads, jax.ShapeDtypeStruct((1, 128), jnp.float32)),
        compiler_params=pltpu.CompilerParams(vmem_limit_bytes=VMEM_BYTES),
    )(pooled, pick, valid[:, :, None], valid[:, None, :], scale.reshape(1, 1))


def joint_forward_kernel(rows_ref, matrix_ref, bias_ref, out_ref):
    part, width = matrix_ref.shape[2], matrix_ref.shape[3]
    matrix = matrix_ref[...].reshape(3 * part, width)
    out_ref[0] = low(dot_nt(rows_ref[...], matrix) + bias_ref[0])


def joint_forward(rows, matrix, bias):
    count, width = rows.shape
    groups, _, columns = bias.shape
    return pl.pallas_call(
        joint_forward_kernel,
        out_shape=jax.ShapeDtypeStruct((groups, count, columns), jnp.bfloat16),
        grid=(groups,),
        in_specs=[
            pl.BlockSpec((count, width), lambda j: (0, 0)),
            pl.BlockSpec((3, 1, columns // 3, width), lambda j: (0, j, 0, 0)),
            pl.BlockSpec((1, 1, columns), lambda j: (j, 0, 0)),
        ],
        out_specs=pl.BlockSpec((1, count, columns), lambda j: (j, 0, 0)),
        compiler_params=pltpu.CompilerParams(vmem_limit_bytes=VMEM_BYTES),
    )(rows, matrix.reshape(3, groups, columns // 3, width), bias)


def joint_backward_kernel(grad_ref, matrix_ref, rows_ref, out_ref, weight_ref):
    part, width = matrix_ref.shape[2], matrix_ref.shape[3]
    grad = grad_ref[0]
    term = dot_nn(grad, matrix_ref[...].reshape(3 * part, width))
    weight_ref[...] = low(dot_tn(grad, rows_ref[...])).reshape(3, 1, part, width)

    @pl.when(pl.program_id(0) == 0)
    def _():
        out_ref[...] = term

    @pl.when(pl.program_id(0) > 0)
    def _():
        out_ref[...] += term


def joint_backward(grad, matrix, rows):
    groups, count, columns = grad.shape
    width = rows.shape[1]
    part = columns // 3
    out, weight = pl.pallas_call(
        joint_backward_kernel,
        out_shape=(
            jax.ShapeDtypeStruct((count, width), jnp.float32),
            jax.ShapeDtypeStruct((3, groups, part, width), jnp.bfloat16),
        ),
        grid=(groups,),
        in_specs=[
            pl.BlockSpec((1, count, columns), lambda j: (j, 0, 0)),
            pl.BlockSpec((3, 1, part, width), lambda j: (0, j, 0, 0)),
            pl.BlockSpec((count, width), lambda j: (0, 0)),
        ],
        out_specs=(
            pl.BlockSpec((count, width), lambda j: (0, 0)),
            pl.BlockSpec((3, 1, part, width), lambda j: (0, j, 0, 0)),
        ),
        compiler_params=pltpu.CompilerParams(vmem_limit_bytes=VMEM_BYTES),
    )(grad, matrix.reshape(3, groups, part, width), rows)
    return out, weight.reshape(3 * groups * part, width)


def adamw(param, grad, first, second, rate, decay):
    first_new = beta_one * first + (1.0 - beta_one) * grad
    second_new = beta_two * second + (1.0 - beta_two) * grad * grad
    step_dir = (
        first_new
        / (1.0 - beta_one**STEP)
        / (jnp.sqrt(second_new / (1.0 - beta_two**STEP)) + adam_eps)
    )
    return (param - rate * (step_dir + decay * param), first_new, second_new)


def per_device(
    latents,
    noise,
    captions,
    image_sizes,
    caption_lengths,
    timesteps,
    weights,
    vectors,
    weights_m,
    weights_v,
    vectors_m,
    vectors_v,
):
    width = weights.shape[1]
    seq_count = lax.axis_size("seq")
    dp_count = lax.axis_size("dp")
    seq_index = lax.axis_index("seq")
    row_index = lax.axis_index("dp")
    devices = dp_count * seq_count
    layout = matrix_rows(width)
    shard_rows = weights.shape[0]
    paired = dp_count == 4 and seq_count == 8
    weights_low = weights.astype(jnp.bfloat16)
    if paired:
        shard = weights_low.reshape(shard_rows // UNIT, UNIT, width)
        rows_all, rows_late = gather_rows((0, 2176), (23, 19), 8, devices, 7, shard)
        flat = (-1, width)
        self_head = 384
        (
            time_one,
            time_two,
            time_block,
            text_one,
            text_two,
            joint_qkv,
            self_out_head,
        ) = split_rows(rows_all.reshape(flat), layout[:6] + (self_head,))
    else:
        gathered = lax.all_gather(weights_low, both_axes, axis=0, tiled=True)
        (
            time_one,
            time_two,
            time_block,
            text_one,
            text_two,
            joint_qkv,
            self_out,
            cross_query,
            cross_kv,
            cross_out,
            mlp_up,
            mlp_down,
        ) = split_rows(gathered, layout)
    (
        table,
        final_table,
        patch_in,
        patch_out,
        b_patch,
        b_time_one,
        b_time_two,
        b_block,
        b_text_one,
        b_text_two,
        b_query,
        b_value,
        b_self_out,
        b_cross_query,
        b_cross_value,
        b_cross_out,
        b_up,
        b_down,
    ) = split_rows(vectors.astype(jnp.bfloat16).astype(jnp.float32), vector_rows(width))
    head_dim = width // HEADS
    heads = HEADS // seq_count
    part = heads * head_dim
    images = image_sizes.shape[2]
    slots = latents.shape[2]
    assert slots == BLOCK and images == seq_count
    rows = MICRO * slots
    wide = (MICRO, slots, width)
    image_count = jnp.sum((image_sizes > 0).astype(jnp.float32))
    loss_scale = 1.0 / image_count

    ends_all = jnp.cumsum(image_sizes, axis=2)
    firsts = jnp.arange(seq_count, dtype=jnp.int32) * BLOCK
    segment_all = jnp.sum(
        (ends_all[:, :, None, :] <= firsts[None, None, :, None]).astype(jnp.int32), axis=3
    )
    onehot_all = (
        segment_all[:, :, :, None] == jnp.arange(images, dtype=jnp.int32)[None, None, None, :]
    )
    size_all = jnp.sum(jnp.where(onehot_all, image_sizes[:, :, None, :], 0), axis=3)
    start_all = jnp.sum(jnp.where(onehot_all, (ends_all - image_sizes)[:, :, None, :], 0), axis=3)
    step_all = jnp.sum(jnp.where(onehot_all, timesteps[:, :, None, :], 0), axis=3)
    length_all = jnp.sum(jnp.where(onehot_all, caption_lengths[:, :, None, :], 0), axis=3)
    row_start = start_all[:, row_index]
    row_size = size_all[:, row_index]
    kv_start = row_start // BLOCK
    kv_big = (row_size == LARGE).astype(jnp.int32)
    own_segment = segment_all[:, row_index, seq_index]
    own_size = row_size[:, seq_index]
    own_start = row_start[:, seq_index]
    own_step = step_all[:, row_index, seq_index]
    own_length = length_all[:, row_index, seq_index]

    quarter = width // 4
    omega = 1.0 / 10000.0 ** (jnp.arange(quarter, dtype=jnp.float32) / quarter)
    angle = jnp.arange(2 * SIDE, dtype=jnp.float32)[:, None] * omega[None, :]
    angle_table = jnp.concatenate([jnp.sin(angle), jnp.cos(angle)], axis=1)
    within = (
        seq_index * BLOCK - own_start[:, None] + jnp.arange(slots, dtype=jnp.int32)[None, :]
    ).reshape(rows)
    side = jnp.where(own_size == LARGE, 2 * SIDE, SIDE).astype(jnp.int32)
    side = jnp.broadcast_to(side[:, None], (MICRO, slots)).reshape(rows)
    places = jnp.arange(2 * SIDE, dtype=jnp.int32)[None, :]
    pick_row = ((within // side)[:, None] == places).astype(jnp.float32)
    pick_col = ((within % side)[:, None] == places).astype(jnp.float32)
    position = jnp.concatenate(
        [
            jnp.dot(pick_row, angle_table, precision=exact),
            jnp.dot(pick_col, angle_table, precision=exact),
        ],
        axis=1,
    )

    level = noise_level(own_step)[:, None, None]
    level_prev = noise_level(own_step - 1)[:, None, None]
    beta_log, tilde_log = variance_logs(level, level_prev)
    target = noise[:, 0].astype(jnp.float32)
    noisy = jnp.sqrt(level) * latents[:, 0].astype(jnp.float32) + jnp.sqrt(1.0 - level) * target
    noisy = noisy.reshape(rows, PATCH)

    time_low = low(time_features(own_step))
    time_first = dot_nn(time_low, time_one) + b_time_one
    time_act, time_act_back = jax.vjp(jax.nn.silu, time_first)
    time_act_low = low(time_act)
    time_embed = dot_nn(time_act_low, time_two) + b_time_two
    embed_act, embed_act_back = jax.vjp(jax.nn.silu, time_embed)
    embed_low = low(embed_act)
    block_mod = dot_nt(embed_low, time_block) + b_block.reshape(1, -1) + table.reshape(1, -1)
    shift_one, scale_one, gate_one, shift_two, scale_two, gate_two = [
        piece[:, None, :] for piece in jnp.split(block_mod, 6, axis=1)
    ]
    shift_final = (final_table[0][None, :] + time_embed)[:, None, :]
    scale_final = (final_table[1][None, :] + time_embed)[:, None, :]

    hidden_zero = (jnp.dot(noisy, patch_in, precision=exact) + b_patch + position).reshape(wide)
    normed_one, mod_one_back = jax.vjp(modulate, hidden_zero, shift_one, scale_one)
    normed_one_low = low(normed_one).reshape(rows, width)
    joint_bias = jnp.concatenate([b_query, jnp.zeros_like(b_query), b_value], axis=0)
    joint_bias = jnp.transpose(joint_bias.reshape(3, seq_count, part), (1, 0, 2))
    qkv = joint_forward(normed_one_low, joint_qkv, joint_bias.reshape(seq_count, 1, 3 * part))
    caption_low = captions[:, 0].reshape(MICRO * CAP, TEXT_W)
    caption_first = dot_nn(caption_low, text_one) + b_text_one
    caption_act, caption_act_back = jax.vjp(gelu_tanh, caption_first)
    caption_act_low = low(caption_act)
    text = dot_nn(caption_act_low, text_two) + b_text_two
    lengths_slot = lax.dynamic_slice_in_dim(caption_lengths[:, row_index], seq_index, 1, 1)
    token_live = (jnp.arange(CAP, dtype=jnp.int32)[None, :] < lengths_slot).astype(jnp.float32)
    lengths_slot_float = lengths_slot.astype(jnp.float32)
    caption_pool = (
        jnp.sum(text.reshape(MICRO, CAP, width) * token_live[:, :, None], axis=1) / lengths_slot_float
    )
    text_own = low(text)
    if paired:
        qkv, text_own, rows_late = lax.optimization_barrier((qkv, text_own, rows_late))
    qkv = lax.all_to_all(qkv, "seq", split_axis=0, concat_axis=0, tiled=True)
    text_all = lax.all_gather(text_own.reshape(MICRO, CAP, width), "seq", axis=0)
    if paired:
        rows_late, words_all = spread_rows(rows_late, caption_pool.reshape(-1, 128), devices, 8)
        qkv, rows_late = lax.optimization_barrier((qkv, rows_late))
        self_out_tail, cross_query, cross_kv, cross_out, mlp_up, mlp_down = split_rows(
            rows_late.reshape(flat), (layout[6] - self_head,) + layout[7:]
        )
        self_out = jnp.concatenate([self_out_head, self_out_tail], axis=0)
    qkv = qkv.reshape(seq_count, MICRO, slots, 3 * part)
    mixed = self_forward(kv_start, kv_big, qkv, heads, head_dim)
    mixed = lax.all_to_all(
        mixed.reshape(seq_count, rows, part), "seq", split_axis=0, concat_axis=0, tiled=True
    )
    mixed_low = jnp.transpose(mixed, (1, 0, 2)).reshape(rows, width)
    attended = (dot_nn(mixed_low, self_out) + b_self_out).reshape(wide)
    hidden_one = hidden_zero + gate_one * attended

    text_low = jnp.concatenate(
        [
            lax.dynamic_slice(text_all, (own_segment[m], m, 0, 0), (1, 1, CAP, width))[0, 0]
            for m in range(MICRO)
        ],
        axis=0,
    )
    text_kv = dot_nt(text_low, cross_kv)
    pad_rows = ((0, 0), (0, CAP_PAD - CAP), (0, 0))
    key_text = jnp.pad(low(text_kv[:, :width]).reshape(MICRO, CAP, width), pad_rows)
    value_text = jnp.pad(
        low(text_kv[:, width:] + b_cross_value).reshape(MICRO, CAP, width), pad_rows
    )
    hidden_one_low = low(hidden_one).reshape(rows, width)
    query_cross = low(dot_nn(hidden_one_low, cross_query) + b_cross_query).reshape(wide)
    cross_low = cross_call(
        functools.partial(cross_forward_kernel, head_dim),
        own_length,
        (query_cross, key_text, value_text),
        jax.ShapeDtypeStruct(wide, jnp.bfloat16),
    ).reshape(rows, width)
    hidden_two = hidden_one + (dot_nn(cross_low, cross_out) + b_cross_out).reshape(wide)
    normed_two, mod_two_back = jax.vjp(modulate, hidden_two, shift_two, scale_two)
    normed_two_low = low(normed_two).reshape(rows, width)
    upward = dot_nt(normed_two_low, mlp_up) + b_up.reshape(1, -1)
    upward_act, upward_back = jax.vjp(gelu_tanh, upward)
    upward_low = low(upward_act)
    feed = (dot_nn(upward_low, mlp_down) + b_down).reshape(wide)
    hidden_three = hidden_two + gate_two * feed
    final_normed, final_back = jax.vjp(modulate, hidden_three, shift_final, scale_final)
    final_flat = final_normed.reshape(rows, width)
    predicted = jnp.dot(final_flat, patch_out.T, precision=exact).reshape(MICRO, slots, 2 * PATCH)
    error = predicted[:, :, :PATCH] - target
    frac = (predicted[:, :, PATCH:] + 1.0) * 0.5
    model_log = frac * beta_log + (1.0 - frac) * tilde_log
    ratio = jnp.exp(tilde_log - model_log)
    spread = 0.5 * (model_log - tilde_log - 1.0 + ratio) / log_two
    error_weight = (1.0 / (float(PATCH) * own_size.astype(jnp.float32)))[:, None, None]
    squared_loss = jnp.sum((error * error + spread) * error_weight)

    pooled = jnp.sum(final_normed, axis=1)
    if paired:
        pooled_all = share(pooled.reshape(-1, 128), devices, 1)
    else:
        pooled_all = lax.all_gather(pooled, both_axes, axis=0)
        words_all = lax.all_gather(caption_pool, both_axes, axis=0)
    each = (devices, MICRO, width)
    pooled_all = jnp.concatenate([pooled_all.reshape(each), words_all.reshape(each)], axis=1)
    pooled_all = jnp.transpose(pooled_all, (1, 0, 2))
    size_float = jnp.maximum(image_sizes.astype(jnp.float32), 1.0)
    pick = onehot_all.astype(jnp.float32) / size_float[:, :, None, :]
    same_row = jnp.eye(dp_count, dtype=jnp.float32)
    pick = jnp.einsum("mrsi,rq->mriqs", pick, same_row, precision=exact).reshape(
        MICRO, dp_count * images, devices
    )
    valid = (image_sizes > 0).astype(jnp.float32).reshape(MICRO, dp_count * images)
    grad_pool, grad_caption, contrast_value = contrast(pooled_all, pick, valid, loss_scale)
    contrast_value = contrast_value[0, 0]
    own_pool = row_index * images + own_segment
    grad_pool_own = jnp.concatenate(
        [lax.dynamic_slice(grad_pool, (m, own_pool[m], 0), (1, 1, width))[0] for m in range(MICRO)]
    ) / own_size.astype(jnp.float32)[:, None]
    grad_caption = lax.dynamic_slice_in_dim(
        grad_caption, row_index * images + seq_index, 1, 1
    )[:, 0]

    grad_spread = 0.5 * (1.0 - ratio) / log_two * 0.5 * (beta_log - tilde_log)
    grad_predicted = (
        loss_scale * error_weight * jnp.concatenate([2.0 * error, grad_spread], axis=2)
    ).reshape(rows, 2 * PATCH)
    grad_final = grad_pool_own[:, None, :] + jnp.dot(
        grad_predicted, patch_out, precision=exact
    ).reshape(wide)
    grad_patch_out = lax.dot_general(
        grad_predicted, final_flat, (((0,), (0,)), ((), ())), precision=exact
    )
    grad_three, grad_shift_final, grad_scale_final = final_back(grad_final)
    grad_shift_final = grad_shift_final[:, 0]
    grad_scale_final = grad_scale_final[:, 0]
    grad_final_table = jnp.stack([grad_shift_final.sum(axis=0), grad_scale_final.sum(axis=0)])
    grad_embed = grad_shift_final + grad_scale_final

    grad_feed = (grad_three * gate_two).reshape(rows, width)
    grad_feed_low = low(grad_feed)
    grad_upward = upward_back(dot_nt(grad_feed_low, mlp_down))[0]
    grad_upward_low = low(grad_upward)
    weight_down = dot_tn(upward_low, grad_feed_low)
    weight_up = dot_tn(grad_upward_low, normed_two_low)
    grad_two_mod, grad_shift_two, grad_scale_two = mod_two_back(
        dot_nn(grad_upward_low, mlp_up).reshape(wide)
    )
    grad_gate_two = jnp.sum(grad_three * feed, axis=1, keepdims=True)
    grad_two = grad_three + grad_two_mod
    grad_two_flat = grad_two.reshape(rows, width)
    grad_two_low = low(grad_two_flat)
    weight_cross_out = dot_tn(cross_low, grad_two_low)
    grad_cross_low = low(dot_nt(grad_two_low, cross_out)).reshape(wide)
    padded = jax.ShapeDtypeStruct((MICRO, CAP_PAD, width), jnp.float32)
    grad_query_cross, grad_key_text, grad_value_text = cross_call(
        functools.partial(cross_backward_kernel, head_dim),
        own_length,
        (query_cross, key_text, value_text, grad_cross_low),
        (jax.ShapeDtypeStruct(wide, jnp.float32), padded, padded),
    )
    grad_query_cross = grad_query_cross.reshape(rows, width)
    grad_query_low = low(grad_query_cross)
    weight_cross_query = dot_tn(hidden_one_low, grad_query_low)
    grad_one = grad_two + dot_nt(grad_query_low, cross_query).reshape(wide)

    grad_kv = jnp.concatenate([grad_key_text[:, :CAP], grad_value_text[:, :CAP]], axis=2).reshape(
        MICRO * CAP, 2 * width
    )
    grad_kv_low = low(grad_kv)
    weight_cross_kv = dot_tn(grad_kv_low, text_low)
    grad_text_part = low(dot_nn(grad_kv_low, cross_kv)).reshape(MICRO, CAP, width)
    grad_text_all = lax.all_gather(grad_text_part, "seq", axis=0).astype(jnp.float32)
    mine = (segment_all[:, row_index] == seq_index).astype(jnp.float32)
    grad_text = jnp.sum(grad_text_all * jnp.transpose(mine)[:, :, None, None], axis=0) + (
        (grad_caption / lengths_slot_float)[:, None, :] * token_live[:, :, None]
    )
    grad_text = grad_text.reshape(MICRO * CAP, width)
    grad_text_low = low(grad_text)
    weight_text_two = dot_tn(caption_act_low, grad_text_low)
    grad_caption_first = caption_act_back(dot_nt(grad_text_low, text_two))[0]
    grad_caption_low = low(grad_caption_first)
    head_rows = TILE_START * UNIT - sum(layout[:3]) + TILE * UNIT // 2 if paired else 0
    weight_text_one = dot_tn(caption_low[:, head_rows:], grad_caption_low)

    grad_attended = (grad_one * gate_one).reshape(rows, width)
    grad_gate_one = jnp.sum(grad_one * attended, axis=1, keepdims=True)
    grad_attended_low = low(grad_attended)
    weight_self_out = dot_tn(mixed_low, grad_attended_low)
    grad_mixed = low(dot_nt(grad_attended_low, self_out)).reshape(rows, seq_count, part)
    grad_mixed = jnp.transpose(grad_mixed, (1, 0, 2))
    if paired:
        weight_up, weight_down, grad_mixed = lax.optimization_barrier(
            (low(weight_up), low(weight_down), grad_mixed)
        )
    grad_mixed = lax.all_to_all(grad_mixed, "seq", split_axis=0, concat_axis=0, tiled=True)
    if paired:
        summed_feed = reduce_rows(
            ((19, 31),), shard_rows // UNIT, devices, 2, ((weight_up, 0, 12), (weight_down, 0, 12))
        )
        grad_mixed, summed_feed = lax.optimization_barrier((grad_mixed, summed_feed))
    grad_mixed = grad_mixed.reshape(seq_count, MICRO, slots, part)
    grad_qkv, head_sums = self_backward(kv_start, kv_big, qkv, grad_mixed, heads, head_dim)
    head_sums = jnp.sum(head_sums[:, 0], axis=0)
    column = seq_index * part
    grad_bias_query = lax.dynamic_update_slice(
        jnp.zeros((width,), jnp.float32), head_sums[:part], (column,)
    )
    grad_bias_value = lax.dynamic_update_slice(
        jnp.zeros((width,), jnp.float32), head_sums[part:], (column,)
    )
    grad_qkv = grad_qkv.reshape(seq_count, rows, 3 * part)
    if paired:
        time_rows = layout[0] + layout[1]
        block_rows = layout[2]
        weight_self_out = low(weight_self_out)
        first_half = low(dot_tn(caption_low[:, :head_rows], grad_caption_low))
        first_half = jnp.pad(first_half, ((TILE * UNIT // 2 - head_rows, 0), (0, 0)))
        (
            first_half,
            weight_text_one,
            weight_text_two,
            weight_self_out,
            weight_cross_query,
            weight_cross_kv,
            weight_cross_out,
            grad_qkv,
        ) = lax.optimization_barrier(
            (
                first_half,
                low(weight_text_one),
                low(weight_text_two),
                weight_self_out,
                low(weight_cross_query),
                low(weight_cross_kv),
                low(weight_cross_out),
                grad_qkv,
            )
        )
    grad_qkv = lax.all_to_all(
        grad_qkv, "seq", split_axis=0, concat_axis=0, tiled=True
    )
    if paired:
        summed_middle = reduce_rows(
            ((0, 7), (12, 19)),
            shard_rows // UNIT,
            devices,
            3,
            (
                (first_half, 0, 1),
                (weight_text_one, 0, 10),
                (weight_text_two, 0, 3),
                (weight_self_out, TILE // 2, 2),
                (weight_cross_query, 0, 3),
                (weight_cross_kv, 0, 6),
                (weight_cross_out, 0, 3),
            ),
        )
        grad_qkv, summed_middle = lax.optimization_barrier((grad_qkv, summed_middle))
    grad_normed_one, weight_joint = joint_backward(grad_qkv, joint_qkv, normed_one_low)
    grad_zero_mod, grad_shift_one, grad_scale_one = mod_one_back(grad_normed_one.reshape(wide))
    grad_zero = (grad_one + grad_zero_mod).reshape(rows, width)
    grad_patch_in = lax.dot_general(noisy, grad_zero, (((0,), (0,)), ((), ())), precision=exact)

    grad_mod = jnp.concatenate(
        [grad_shift_one, grad_scale_one, grad_gate_one, grad_shift_two, grad_scale_two, grad_gate_two],
        axis=1,
    )
    grad_table = jnp.sum(grad_mod, axis=0)
    grad_mod_low = low(grad_mod.reshape(MICRO, 6 * width))
    weight_block = dot_tn(grad_mod_low, embed_low)
    grad_embed = grad_embed + embed_act_back(dot_nn(grad_mod_low, time_block))[0]
    grad_embed_low = low(grad_embed)
    weight_time_two = dot_tn(time_act_low, grad_embed_low)
    grad_time_first = time_act_back(dot_nt(grad_embed_low, time_two))[0]
    weight_time_one = dot_tn(time_low, low(grad_time_first))

    if paired:
        holders = -(-(time_rows + block_rows) // shard_rows)
        own_grads = jnp.concatenate(
            [grad_mod_low, grad_embed_low, low(grad_time_first), embed_low, time_act_low, time_low],
            axis=1,
        )
        summed_joint, grads_all = reduce_rows(
            ((7, 12),),
            shard_rows // UNIT,
            devices,
            4,
            ((low(weight_joint), 0, 9), (weight_self_out, 0, 1)),
            own_grads.reshape(-1, 128),
            holders,
        )
        grads_all = jnp.where(device_index() < holders, grads_all, 0)
        grads_all = grads_all.reshape(devices * MICRO, -1)
        ends = [6 * width, 7 * width, 8 * width, 9 * width, 10 * width]
        grad_block_all, grad_two_all, grad_one_all, embed_all, act_all, features_all = jnp.split(
            grads_all, ends, axis=1
        )
        first_row = device_index() * shard_rows

        def own_columns(array, start):
            stop = start + array.shape[1]
            spread = jnp.pad(array, ((0, 0), (start, shard_rows + (-stop) % shard_rows)))
            place = jnp.minimum(first_row, spread.shape[1] - shard_rows)
            return lax.dynamic_slice(spread, (0, place), (array.shape[0], shard_rows))

        summed_time = (
            dot_tn(own_columns(features_all, 0), grad_one_all)
            + dot_tn(own_columns(act_all, layout[0]), grad_two_all)
            + dot_tn(own_columns(grad_block_all, time_rows), embed_all)
        )
        row = first_row + jnp.arange(shard_rows, dtype=jnp.int32)
        tile = ((row - TILE_START * UNIT) // (TILE * UNIT))[:, None]
        flat = (shard_rows, width)
        reduced = jnp.where(
            tile >= 19,
            summed_feed.reshape(flat),
            jnp.where(
                (tile >= 7) & (tile < 12), summed_joint.reshape(flat), summed_middle.reshape(flat)
            ),
        ).astype(jnp.float32)
        summed = jnp.where(row[:, None] < time_rows + block_rows, summed_time, reduced)
    else:
        grad_weights = jnp.concatenate(
            [
                low(piece)
                for piece in (
                    weight_time_one,
                    weight_time_two,
                    weight_block,
                    weight_text_one,
                    weight_text_two,
                    weight_joint,
                    weight_self_out,
                    weight_cross_query,
                    weight_cross_kv,
                    weight_cross_out,
                    weight_up,
                    weight_down,
                )
            ],
            axis=0,
        )
        summed = lax.psum_scatter(
            grad_weights, both_axes, scatter_dimension=0, tiled=True
        ).astype(jnp.float32)
    grad_vector = jnp.concatenate(
        [
            grad_table,
            grad_final_table,
            grad_patch_in,
            grad_patch_out,
            jnp.sum(grad_zero, axis=0)[None, :],
            jnp.sum(grad_time_first, axis=0)[None, :],
            jnp.sum(grad_embed, axis=0)[None, :],
            grad_table,
            jnp.sum(grad_caption_first, axis=0)[None, :],
            jnp.sum(grad_text, axis=0)[None, :],
            grad_bias_query[None, :],
            grad_bias_value[None, :],
            jnp.sum(grad_attended, axis=0)[None, :],
            jnp.sum(grad_query_cross, axis=0)[None, :],
            jnp.sum(grad_kv[:, width:], axis=0)[None, :],
            jnp.sum(grad_two_flat, axis=0)[None, :],
            jnp.sum(grad_upward, axis=0).reshape(-1, width),
            jnp.sum(grad_feed, axis=0)[None, :],
            jnp.full((2, width), squared_loss),
        ],
        axis=0,
    )
    squares = jnp.sum(summed * summed)
    if paired:
        grad_vectors, squares_all = sum_all(grad_vector, squares, devices, 6)
    else:
        grad_vectors, squares_all = lax.psum((grad_vector, squares), both_axes)
    loss_sum = grad_vectors[vectors.shape[0], 0] + contrast_value
    grad_vectors = grad_vectors[: vectors.shape[0]]
    down_bias_grad = grad_vectors[grad_vectors.shape[0] - 1]
    grad_norm = jnp.sqrt(squares_all + jnp.sum(grad_vectors * grad_vectors))
    factor = jnp.minimum(1.0, clip_norm / (grad_norm + 1e-06))
    new_w, first_w, second_w = adamw(
        weights, summed * factor, weights_m, weights_v, rate_matrix, weight_decay
    )
    new_v, first_v, second_v = adamw(
        vectors, grad_vectors * factor, vectors_m, vectors_v, rate_vector, 0.0
    )
    return (
        new_w,
        first_w,
        second_w,
        new_v,
        first_v,
        second_v,
        loss_sum,
        image_count,
        grad_norm,
        down_bias_grad,
    )


def solution(mesh):
    shard = P(both_axes, None)
    data = P(None, "dp", "seq", None)
    return jax.shard_map(
        per_device,
        mesh=mesh,
        in_specs=(data, data, data, P(), P(), P(), shard, P(), shard, shard, P(), P()),
        out_specs=(shard, shard, shard, P(), P(), P(), P(), P(), P(), P()),
        check_vma=False,
    )
```

profile of v0, /device:TPU:0, one launch (start us, length us, event | category | flops | bytes accessed | tf_op | source)
XLA Modules:
  0.0 1425.3 jit_solution(8495227104689409860)
XLA Ops:
  21.0 229.5 %shard_map.195 = (bf16[2208,8,1152]{2,1,0:T(8,128)(2,1)}, bf16[1824,8,1152]{2,1,0:T(8,128)(2,1)}) custom-call(bf16[125,8,1152]{2,1,0:T(8,128)(2,1)} %convert_bitcast_fusion.shard_ref), custom_call_target="tpu_custom_call" | custom-call | tf_op jit(solution)/shard_map/pallas_call | solution.py:1168
  250.5 7.0 slice.218
  261.7 9.7 fusion.33
  272.9 7.0 fusion.50
  285.7 11.2 shard_map.196
  296.9 6.3 copy.114
  303.2 9.1 all-to-all-start
  324.4 196.7 %shard_map.197 = (bf16[1824,8,1152]{2,1,0:T(8,128)(2,1)}, f32[32,18,128]{2,1,0:T(8,128)}) custom-call(bf16[1824,8,1152]{2,1,0:T(8,128)(2,1)} %get-tuple-element.51.rows_ref, f32[18,128]{1,0:T(8,128)} %broadcast_divide_fusion.block_ref), custom_call_target="tpu_custom_call", output_to_operand_aliasing={{0}: (0, {})} | custom-call | tf_op jit(solution)/shard_map/pallas_call | solution.py:1147
  538.6 30.1 %shard_map.198 = bf16[8,2,256,144]{3,2,1,0:T(8,128)(2,1)} custom-call(s32[2,8]{1,0:T(2,128)} %and_select_fusion.start_ref, s32[2,8]{1,0:T(2,128)} %bitcast.414, bf16[8,2,256,432]{3,2,1,0:T(8,128)(2,1)} %bitcast.360), custom_call_target="tpu_custom_call" | custom-call | tf_op jit(solution)/shard_map/pallas_call | solution.py:150
  572.4 9.5 all-to-all-start.1
  594.2 13.0 all-to-all-done.1
  617.3 13.7 shard_map.199
  641.1 13.3 fusion.13
  654.5 16.2 %fusion.202 = (f32[512]{0:T(512)S(1)}, f32[512,1152]{1,0:T(8,128)}, f32[512,1152]{1,0:T(8,128)}) fusion(f32[512,1152]{1,0:T(8,128)S(1)} %copy-done.2, f32[2,1152]{1,0:T(2,128)S(1)} %copy-done.53, f32[1152]{0:T(1024)S(1)} %copy-done.85, bf16[1824,8,1152]{2,1,0:T(8,128)(2,1)} %get-tuple-element.54, f32[512,4608]{1,0:T(8,128)} %fusion.13, f32[4608]{0:T(1024)S(1)} %copy-done.66), kind=kOutput, calls=%fused_computation.401 | convolution fusion | flops 5461769728 | bytes 27166208 | tf_op jit(solution)/shard_map/dot_general | solution.py:90
  676.4 6.4 fusion.90
  682.8 11.8 shard_map.200
  709.8 17.8 %fusion.207 = (f32[4608]{0:T(1024)}, bf16[512,4608]{1,0:T(8,128)(2,1)}) fusion(f32[512,4608]{1,0:T(8,128)} %fusion.13, f32[4608]{0:T(1024)S(1)} %copy-done.67, bf16[512,1152]{1,0:T(8,128)(2,1)S(1)} %bitcast.393, bf16[1824,8,1152]{2,1,0:T(8,128)(2,1)} %get-tuple-element.54), kind=kOutput, calls=%fused_computation.404 | convolution fusion | flops 5487717888 | bytes 25989120 | tf_op jit(solution)/shard_map/dot_general | solution.py:94
  727.6 12.4 multiply_reduce_fusion.6
  749.1 13.5 shard_map.202
  774.2 6.6 multiply_reduce_fusion.11
  785.1 11.0 convolution_convert_fusion.1
  796.2 10.4 convolution_convert_fusion
  815.0 131.2 %shard_map.203 = bf16[125,8,1152]{2,1,0:T(8,128)(2,1)} custom-call(bf16[576,8,1152]{2,1,0:T(8,128)(2,1)} %bitcast.366, bf16[576,8,1152]{2,1,0:T(8,128)(2,1)} %bitcast.367), custom_call_target="tpu_custom_call" | custom-call | tf_op jit(solution)/shard_map/pallas_call | solution.py:768
  964.2 53.5 %shard_map.204 = (bf16[8,2,256,432]{3,2,1,0:T(8,128)(2,1)}, f32[2,1,288]{2,1,0:T(1,128)}) custom-call(s32[2,8]{1,0:T(2,128)} %and_select_fusion.start_ref, s32[2,8]{1,0:T(2,128)} %bitcast.415, bf16[8,2,256,432]{3,2,1,0:T(8,128)(2,1)} %bitcast.361, bf16[8,2,256,144]{3,2,1,0:T(8,128)(2,1)} %bitcast.373), custom_call_target="tpu_custom_call" | custom-call | tf_op jit(solution)/shard_map/pallas_call | solution.py:233
  1041.5 13.2 all-to-all-start.3
  1067.3 12.7 copy.127
  1081.5 138.5 %shard_map.205 = bf16[125,8,1152]{2,1,0:T(8,128)(2,1)} custom-call(bf16[48,8,1152]{2,1,0:T(8,128)(2,1)} %bitcast.383, bf16[480,8,1152]{2,1,0:T(8,128)(2,1)} %bitcast.362, bf16[144,8,1152]{2,1,0:T(8,128)(2,1)} %bitcast.386, bf16[144,8,1152]{2,1,0:T(8,128)(2,1)} %bitcast.368, bf16[144,8,1152]{2,1,0:T(8,128)(2,1)} %bitcast.385, ...), custom_call_target="tpu_custom_call" | custom-call | tf_op jit(solution)/shard_map/pallas_call | solution.py:768
  1226.3 17.1 %shard_map.206 = (f32[512,1152]{1,0:T(8,128)}, bf16[3,8,144,1152]{3,2,1,0:T(8,128)(2,1)}) custom-call(bf16[8,512,432]{2,1,0:T(8,128)(2,1)} %copy.128.grad_ref, bf16[3,8,144,1152]{3,2,1,0:T(8,128)(2,1)} %bitcast.359, bf16[512,1152]{1,0:T(8,128)(2,1)} %fusion.72.rows_ref), custom_call_target="tpu_custom_call" | custom-call | tf_op jit(solution)/shard_map/pallas_call | solution.py:1376
  1252.3 6.7 constant_dynamic-update-slice_fusion.5
  1262.4 85.9 %shard_map.207 = (bf16[125,8,1152]{2,1,0:T(8,128)(2,1)}, bf16[32,184,128]{2,1,0:T(8,128)(2,1)}) custom-call(bf16[432,8,1152]{2,1,0:T(8,128)(2,1)} %bitcast.375, bf16[144,8,1152]{2,1,0:T(8,128)(2,1)} %bitcast.369, bf16[184,128]{1,0:T(8,128)(2,1)} %reshape.771.refs_2_), custom_call_target="tpu_custom_call" | custom-call | tf_op jit(solution)/shard_map/pallas_call | solution.py:768
  1368.5 30.9 %shard_map.208 = (f32[32,3,8,128]{3,2,1,0:T(8,128)S(1)}, f32[8,128]{1,0:T(8,128)S(1)}) custom-call(f32[32,4,8,128]{3,2,1,0:T(8,128)S(1)} %concatenate.80.parts_ref), custom_call_target="tpu_custom_call" | custom-call | tf_op jit(solution)/shard_map/pallas_call | solution.py:1254
  1405.1 10.9 multiply_subtract_fusion
  (525 shorter events, 233.7 us)
Async XLA Ops:
  7.2 579.5 %all-gather.3.cloned.1.call-start = ((), (), s32[]{:S(2)}) async-start(), calls=%async_computation.4 | async-start | bytes 4976640 | tf_op jit(solution)/shard_map/all_gather | solution.py:1577
  18.1 658.3 %copy-start = (f32[512,1152]{1,0:T(8,128)}, f32[512,1152]{1,0:T(8,128)S(1)}, u32[]{:S(2)}) copy-start(f32[512,1152]{1,0:T(8,128)S(1)} %get-tuple-element.207) | copy-start | bytes 7077892
  18.1 265.9 %copy-start.69 = (f32[512]{0:T(512)}, f32[512]{0:T(512)S(1)}, u32[]{:S(2)}) copy-start(f32[512]{0:T(512)S(1)} %broadcast_multiply_fusion.2) | copy-start | bytes 6148
  303.2 229.2 %all-to-all-start = ((bf16[8,512,432]{1,2,0:T(8,128)(2,1)}), bf16[8,512,432]{1,2,0:T(8,128)(2,1)}, u32[]{:S(2)}, u32[]{:S(2)}) async-start(bf16[8,512,432]{1,2,0:T(8,128)(2,1)} %copy.114), calls=%async_computation | async-start | bytes 7077888 | tf_op jit(solution)/shard_map/all_to_all | solution.py:1576
  322.1 199.0 %copy-start.135 = (f32[2]{0:T(128)}, f32[2]{0:T(128)S(1)}, u32[]{:S(2)}) copy-start(f32[2]{0:T(128)S(1)} %convert_element_type.302) | copy-start | bytes 28
  572.4 34.8 %all-to-all-start.1 = ((bf16[8,512,144]{1,2,0:T(8,128)(2,1)}), bf16[8,512,144]{1,2,0:T(8,128)(2,1)S(1)}, u32[]{:S(2)}, u32[]{:S(2)}) async-start(bf16[8,512,144]{1,2,0:T(8,128)(2,1)} %copy.116), calls=%async_computation.1 | async-start | bytes 2359296 | tf_op jit(solution)/shard_map/all_to_all | solution.py:1587
  581.9 435.8 %all-gather.5.cloned.1.call-start = ((), (), s32[]{:S(2)}) async-start(), calls=%async_computation.5 | async-start | bytes 4976640 | tf_op jit(solution)/shard_map/all_gather | solution.py:1709
  611.3 19.6 %copy-start.3 = (f32[512,1152]{1,0:T(8,128)}, f32[512,1152]{1,0:T(8,128)S(1)}, u32[]{:S(2)}) copy-start(f32[512,1152]{1,0:T(8,128)S(1)} %get-tuple-element.211) | copy-start | bytes 7077892
  675.9 30.9 %copy-start.87 = (f32[2,256]{1,0:T(2,128)}, f32[2,256]{1,0:T(2,128)S(1)}, u32[]{:S(2)}) copy-start(f32[2,256]{1,0:T(2,128)S(1)} %rsqrt.42) | copy-start | bytes 6148
  676.4 18.5 %copy-start.33 = (f32[32,2,1152]{2,0,1:T(8,128)S(1)}, f32[32,2,1152]{2,0,1:T(8,128)}, u32[]{:S(2)}) copy-start(f32[32,2,1152]{2,0,1:T(8,128)} %copy.118) | copy-start | bytes 884740
  682.8 20.3 %copy-start.7 = (f32[2,256,1152]{2,1,0:T(8,128)S(1)}, f32[2,256,1152]{2,1,0:T(8,128)}, u32[]{:S(2)}) copy-start(f32[2,256,1152]{2,1,0:T(8,128)} %get-tuple-element.139) | copy-start | bytes 7077892
  709.7 17.8 %copy-start.29 = (bf16[2,256,1152]{2,1,0:T(8,128)(2,1)}, bf16[2,256,1152]{2,1,0:T(8,128)(2,1)S(1)}, u32[]{:S(2)}) copy-start(bf16[2,256,1152]{2,1,0:T(8,128)(2,1)S(1)} %get-tuple-element.153) | copy-start | bytes 3538948
  709.7 17.8 %copy-start.49 = (f32[2,1152]{1,0:T(2,128)S(1)}, f32[2,1152]{1,0:T(2,128)}, u32[]{:S(2)}) copy-start(f32[2,1152]{1,0:T(2,128)} %get-tuple-element.172) | copy-start | bytes 27652
  709.7 17.8 %copy-start.91 = (f32[2,256]{1,0:T(2,128)S(1)}, f32[2,256]{1,0:T(2,128)}, u32[]{:S(2)}) copy-start(f32[2,256]{1,0:T(2,128)} %div.271) | copy-start | bytes 6148
  806.6 155.1 %all-to-all-start.2 = ((bf16[8,512,144]{1,2,0:T(8,128)(2,1)}), bf16[8,512,144]{1,2,0:T(8,128)(2,1)S(1)}, u32[]{:S(2)}, u32[]{:S(2)}) async-start(bf16[8,512,144]{1,2,0:T(8,128)(2,1)} %bitcast.80), calls=%async_computation.2 | async-start | bytes 2359296 | tf_op jit(solution)/shard_map/all_to_all | solution.py:1732
  815.0 131.2 %copy-start.21 = (bf16[2,256,1152]{2,1,0:T(8,128)(2,1)S(1)}, bf16[2,256,1152]{2,1,0:T(8,128)(2,1)}, u32[]{:S(2)}) copy-start(bf16[2,256,1152]{2,1,0:T(8,128)(2,1)} %shard_map.199) | copy-start | bytes 3538948
  815.0 131.2 %copy-start.32 = (bf16[2,256,1152]{2,1,0:T(8,128)(2,1)S(1)}, bf16[2,256,1152]{2,1,0:T(8,128)(2,1)}, u32[]{:S(2)}) copy-start(bf16[2,256,1152]{2,1,0:T(8,128)(2,1)} %copy-done.31) | copy-start | bytes 3538948
  1041.4 18.2 %copy-start.82 = (f32[1152]{0:T(1024)S(1)}, f32[1152]{0:T(1024)}, u32[]{:S(2)}) copy-start(f32[1152]{0:T(1024)} %get-tuple-element.129) | copy-start | bytes 13828
  1041.4 18.8 %copy-start.90 = (f32[4608]{0:T(1024)S(1)}, f32[4608]{0:T(1024)}, u32[]{:S(2)}) copy-start(f32[4608]{0:T(1024)} %get-tuple-element.147) | copy-start | bytes 55300
  1041.4 18.8 %copy-start.81 = (f32[1152]{0:T(1024)S(1)}, f32[1152]{0:T(1024)}, u32[]{:S(2)}) copy-start(f32[1152]{0:T(1024)} %get-tuple-element.91) | copy-start | bytes 13828
  1041.4 19.4 %copy-start.117 = (f32[1152]{0:T(1024)S(1)}, f32[1152]{0:T(1024)}, u32[]{:S(2)}) copy-start(f32[1152]{0:T(1024)} %get-tuple-element.95) | copy-start | bytes 13828
  1041.5 20.0 %copy-start.116 = (f32[1152]{0:T(1024)S(1)}, f32[1152]{0:T(1024)}, u32[]{:S(2)}) copy-start(f32[1152]{0:T(1024)} %get-tuple-element.88) | copy-start | bytes 13828
  1041.5 20.6 %copy-start.9 = (f32[2,256,1152]{2,1,0:T(8,128)S(1)}, f32[2,256,1152]{2,1,0:T(8,128)}, u32[]{:S(2)}) copy-start(f32[2,256,1152]{2,1,0:T(8,128)} %get-tuple-element.139) | copy-start | bytes 7077892
  1041.5 20.6 %copy-start.52 = (f32[2,1152]{1,0:T(2,128)S(1)}, f32[2,1152]{1,0:T(2,128)}, u32[]{:S(2)}) copy-start(f32[2,1152]{1,0:T(2,128)} %get-tuple-element.176) | copy-start | bytes 27652
  1041.5 20.6 %copy-start.58 = (f32[2,256,16]{1,2,0:T(8,128)S(1)}, f32[2,256,16]{1,2,0:T(8,128)}, u32[]{:S(2)}) copy-start(f32[2,256,16]{1,2,0:T(8,128)} %copy-done.57) | copy-start | bytes 98308
  1041.5 20.6 %copy-start.60 = (f32[2,256,16]{1,2,0:T(8,128)S(1)}, f32[2,256,16]{1,2,0:T(8,128)}, u32[]{:S(2)}) copy-start(f32[2,256,16]{1,2,0:T(8,128)} %copy-done.59) | copy-start | bytes 98308
  1041.5 20.6 %copy-start.65 = (f32[2,1152]{1,0:T(2,128)S(1)}, f32[2,1152]{1,0:T(2,128)}, u32[]{:S(2)}) copy-start(f32[2,1152]{1,0:T(2,128)} %get-tuple-element.177) | copy-start | bytes 27652
  1041.5 178.5 %all-to-all-start.3 = ((bf16[8,512,432]{1,2,0:T(8,128)(2,1)}), bf16[8,512,432]{1,2,0:T(8,128)(2,1)}, u32[]{:S(2)}, u32[]{:S(2)}) async-start(bf16[8,512,432]{1,2,0:T(8,128)(2,1)} %copy.125), calls=%async_computation.3 | async-start | bytes 7077888 | tf_op jit(solution)/shard_map/all_to_all | solution.py:1776
  1367.7 35.6 %copy-start.137 = (f32[1,128]{1,0:T(1,128)S(1)}, f32[1,128]{1,0:T(1,128)}, u32[]{:S(2)}) copy-start(f32[1,128]{1,0:T(1,128)} %get-tuple-element.85) | copy-start | bytes 1540
  1367.7 36.2 %copy-start.26 = (f32[78,1152]{1,0:T(8,128)S(1)}, f32[78,1152]{1,0:T(8,128)}, u32[]{:S(2)}) copy-start(f32[78,1152]{1,0:T(8,128)} %param.19) | copy-start | bytes 1078276
  1367.7 36.2 %copy-start.43 = (f32[78,1152]{1,0:T(8,128)S(1)}, f32[78,1152]{1,0:T(8,128)}, u32[]{:S(2)}) copy-start(f32[78,1152]{1,0:T(8,128)} %param.22) | copy-start | bytes 1078276
  1367.7 36.2 %copy-start.44 = (f32[78,1152]{1,0:T(8,128)S(1)}, f32[78,1152]{1,0:T(8,128)}, u32[]{:S(2)}) copy-start(f32[78,1152]{1,0:T(8,128)} %param.23) | copy-start | bytes 1078276
  (120 other events, 725.7 us)
Sparse Core Ops, SparseCore 0:
  297.1 156.4 all-gather.2
  770.4 112.4 all-gather.4
where the time goes:
time: 1440 us; the launch traced here: 1430 us
  Pallas kernels  968 us (67%)
  matrix products  200 us (14%)
  local copies, waits for them, and re-layouts  105 us (7%)
  other arithmetic  73.7 us (5%)
  starting transfers between devices  36.6 us (3%)
  between operations  29 us (2%)
    pallas_call x3, Pallas kernels, reduce_rows(): pl.pallas_call(functools.partial(reduce_kernel, ranges, shard_units, devi...  356 us
    pallas_call x1, Pallas kernels, gather_rows(): pl.pallas_call(functools.partial(gather_kernel, openings, ahead, devices)...  229 us
    pallas_call x1, Pallas kernels, spread_rows(): pl.pallas_call(functools.partial(spread_kernel, devices), out_shape=(jax....  197 us
    dot_general x11, matrix products, dot_nn(): lax.dot_general(left, right, (((1,), (0,)), ((), ())), preferred_element_...  71.5 us
    dot_general x9, matrix products, dot_nt(): lax.dot_general(left, right, (((1,), (1,)), ((), ())), preferred_element_...  65.9 us
    pallas_call x1, Pallas kernels, self_backward(): pl.pallas_call(functools.partial(self_backward_kernel, heads, dim), out_s...  53.5 us
    dot_general x12, matrix products, dot_tn(): lax.dot_general(left, right, (((0,), (0,)), ((), ())), preferred_element_...  50.9 us
    pallas_call x1, Pallas kernels, sum_all(): pl.pallas_call(functools.partial(sum_kernel, devices), out_shape=(jax.Sha...  30.9 us
  transfers between devices with their start and end apart: 6, of which 1 were waited for; matrix products, arithmetic and copies ran while one was open for 9% of the time, Pallas kernels for 39%

commit v1 on v0

--- a/solution.py
+++ b/solution.py
@@ -1392,6 +1392,98 @@
         compiler_params=pltpu.CompilerParams(vmem_limit_bytes=VMEM_BYTES),
     )(grad, matrix.reshape(3, groups, part, width), rows)
     return out, weight.reshape(3 * groups * part, width)
+
+
+FEED_BLOCK = 768
+
+
+def feed_forward_kernel(rows_ref, up_ref, down_ref, b_up_ref, b_down_ref, before_ref, act_ref, out_ref):
+    before = dot_nt(rows_ref[...], up_ref[...]) + b_up_ref[0]
+    before_ref[...] = before
+    act = low(gelu_tanh(before))
+    act_ref[...] = act
+    term = dot_nn(act, down_ref[...])
+
+    @pl.when(pl.program_id(0) == 0)
+    def _():
+        out_ref[...] = term + b_down_ref[...]
+
+    @pl.when(pl.program_id(0) > 0)
+    def _():
+        out_ref[...] += term
+
+
+def feed_specs(count, width, up_start, down_start):
+    return (
+        pl.BlockSpec((count, width), lambda j: (0, 0)),
+        pl.BlockSpec((FEED_BLOCK, width), lambda j: (up_start + j, 0)),
+        pl.BlockSpec((FEED_BLOCK, width), lambda j: (down_start + j, 0)),
+        pl.BlockSpec((1, 1, FEED_BLOCK), lambda j: (j, 0, 0)),
+        pl.BlockSpec((count, FEED_BLOCK), lambda j: (0, j)),
+    )
+
+
+def feed_forward(rows, up, up_start, down, down_start, b_up, b_down):
+    count, width = rows.shape
+    whole, up_spec, down_spec, line, column = feed_specs(count, width, up_start, down_start)
+    return pl.pallas_call(
+        feed_forward_kernel,
+        out_shape=(
+            jax.ShapeDtypeStruct((count, FF), jnp.float32),
+            jax.ShapeDtypeStruct((count, FF), jnp.bfloat16),
+            jax.ShapeDtypeStruct((count, width), jnp.float32),
+        ),
+        grid=(FF // FEED_BLOCK,),
+        in_specs=[whole, up_spec, down_spec, line, pl.BlockSpec((1, width), lambda j: (0, 0))],
+        out_specs=(column, column, whole),
+        compiler_params=pltpu.CompilerParams(vmem_limit_bytes=VMEM_BYTES),
+    )(rows, up, down, b_up.reshape(-1, 1, FEED_BLOCK), b_down)
+
+
+def feed_backward_kernel(
+    grad_ref, up_ref, down_ref, before_ref, act_ref, rows_ref, out_ref, w_up_ref, w_down_ref, sum_ref
+):
+    grad = grad_ref[...]
+    before = before_ref[...]
+    factor = math.sqrt(2.0 / math.pi)
+    square = before * before
+    bend = jnp.tanh(factor * (before + 0.044715 * (square * before)))
+    slope = 0.5 * (1.0 + bend) + (0.5 * factor) * before * (1.0 - bend * bend) * (
+        1.0 + (3.0 * 0.044715) * square
+    )
+    grad_up = dot_nt(grad, down_ref[...]) * slope
+    sum_ref[0] = jnp.sum(grad_up, axis=0, keepdims=True)
+    grad_up = low(grad_up)
+    w_up_ref[...] = low(dot_tn(grad_up, rows_ref[...]))
+    w_down_ref[...] = low(dot_tn(act_ref[...], grad))
+    term = dot_nn(grad_up, up_ref[...])
+
+    @pl.when(pl.program_id(0) == 0)
+    def _():
+        out_ref[...] = term
+
+    @pl.when(pl.program_id(0) > 0)
+    def _():
+        out_ref[...] += term
+
+
+def feed_backward(grad, up, up_start, down, down_start, before, act, rows):
+    count, width = rows.shape
+    whole, up_spec, down_spec, line, column = feed_specs(count, width, up_start, down_start)
+    block = pl.BlockSpec((FEED_BLOCK, width), lambda j: (j, 0))
+    return pl.pallas_call(
+        feed_backward_kernel,
+        out_shape=(
+            jax.ShapeDtypeStruct((count, width), jnp.float32),
+            jax.ShapeDtypeStruct((FF, width), jnp.bfloat16),
+            jax.ShapeDtypeStruct((FF, width), jnp.bfloat16),
+            jax.ShapeDtypeStruct((FF // FEED_BLOCK, 1, FEED_BLOCK), jnp.float32),
+        ),
+        grid=(FF // FEED_BLOCK,),
+        in_specs=[whole, up_spec, down_spec, column, column, whole],
+        out_specs=(whole, block, block, line),
+        compiler_params=pltpu.CompilerParams(vmem_limit_bytes=VMEM_BYTES),
+    )(grad, up, down, before, act, rows)
 
 
 def adamw(param, grad, first, second, rate, decay):
@@ -1578,9 +1670,15 @@
     if paired:
         rows_late, words_all = spread_rows(rows_late, caption_pool.reshape(-1, 128), devices, 8)
         qkv, rows_late = lax.optimization_barrier((qkv, rows_late))
-        self_out_tail, cross_query, cross_kv, cross_out, mlp_up, mlp_down = split_rows(
-            rows_late.reshape(flat), (layout[6] - self_head,) + layout[7:]
-        )
+        rows_late = rows_late.reshape(flat)
+        self_out_tail, cross_query, cross_kv, cross_out = split_rows(
+            rows_late, (layout[6] - self_head,) + layout[7:10]
+        )
+        up_start = (layout[6] - self_head + sum(layout[7:10])) // FEED_BLOCK
+        feed_weights = (rows_late, up_start, rows_late, up_start + FF // FEED_BLOCK)
+    else:
+        feed_weights = (mlp_up, 0, mlp_down, 0)
+    if paired:
         self_out = jnp.concatenate([self_out_head, self_out_tail], axis=0)
     qkv = qkv.reshape(seq_count, MICRO, slots, 3 * part)
     mixed = self_forward(kv_start, kv_big, qkv, heads, head_dim)
@@ -1615,10 +1713,8 @@
     hidden_two = hidden_one + (dot_nn(cross_low, cross_out) + b_cross_out).reshape(wide)
     normed_two, mod_two_back = jax.vjp(modulate, hidden_two, shift_two, scale_two)
     normed_two_low = low(normed_two).reshape(rows, width)
-    upward = dot_nt(normed_two_low, mlp_up) + b_up.reshape(1, -1)
-    upward_act, upward_back = jax.vjp(gelu_tanh, upward)
-    upward_low = low(upward_act)
-    feed = (dot_nn(upward_low, mlp_down) + b_down).reshape(wide)
+    upward, upward_low, feed = feed_forward(normed_two_low, *feed_weights, b_up, b_down)
+    feed = feed.reshape(wide)
     hidden_three = hidden_two + gate_two * feed
     final_normed, final_back = jax.vjp(modulate, hidden_three, shift_final, scale_final)
     final_flat = final_normed.reshape(rows, width)
@@ -1675,13 +1771,10 @@
 
     grad_feed = (grad_three * gate_two).reshape(rows, width)
     grad_feed_low = low(grad_feed)
-    grad_upward = upward_back(dot_nt(grad_feed_low, mlp_down))[0]
-    grad_upward_low = low(grad_upward)
-    weight_down = dot_tn(upward_low, grad_feed_low)
-    weight_up = dot_tn(grad_upward_low, normed_two_low)
-    grad_two_mod, grad_shift_two, grad_scale_two = mod_two_back(
-        dot_nn(grad_upward_low, mlp_up).reshape(wide)
-    )
+    grad_normed_two, weight_up, weight_down, grad_b_up = feed_backward(
+        grad_feed_low, *feed_weights, upward, upward_low, normed_two_low
+    )
+    grad_two_mod, grad_shift_two, grad_scale_two = mod_two_back(grad_normed_two.reshape(wide))
     grad_gate_two = jnp.sum(grad_three * feed, axis=1, keepdims=True)
     grad_two = grad_three + grad_two_mod
     grad_two_flat = grad_two.reshape(rows, width)
@@ -1898,7 +1991,7 @@
             jnp.sum(grad_query_cross, axis=0)[None, :],
             jnp.sum(grad_kv[:, width:], axis=0)[None, :],
             jnp.sum(grad_two_flat, axis=0)[None, :],
-            jnp.sum(grad_upward, axis=0).reshape(-1, width),
+            grad_b_up.reshape(-1, width),
             jnp.sum(grad_feed, axis=0)[None, :],
             jnp.full((2, width), squared_loss),
         ],

time: 1440 us -> 1440 us (level); the launches traced: 1430 us -> 1440 us
  Pallas kernels: 968 us -> 1050 us
  matrix products: 200 us -> 119 us
    pallas_call x0 -> x2, Pallas kernels: none -> 58.8 us  [the longest x1 37.2 us: feed_backward(): pl.pallas_call(feed_backward_kernel, out_shape=(jax.ShapeDtypeStruct((cou...]
    dot_general x9 -> x7, matrix products: 65.9 us -> 34.7 us  [dot_nt(): lax.dot_general(left, right, (((1,), (1,)), ((), ())), preferred_element_...]
    dot_general x11 -> x9, matrix products: 71.5 us -> 42.4 us  [dot_nn(): lax.dot_general(left, right, (((1,), (0,)), ((), ())), preferred_element_...]
    dot_general x12 -> x10, matrix products: 50.9 us -> 29.3 us  [dot_tn(): lax.dot_general(left, right, (((0,), (0,)), ((), ())), preferred_element_...]
    pallas_call x3, Pallas kernels: 356 us -> 376 us  [reduce_rows(): pl.pallas_call(functools.partial(reduce_kernel, ranges, shard_units, devi...]
  transfers between devices with their start and end apart: 6 -> 6, of which waited for: 1 -> 1; matrix products, arithmetic and copies ran while one was open for 9% -> 7% of each run, Pallas kernels for 39% -> 39%
where the time goes in v1:
time: 1440 us
  Pallas kernels  1050 us (73%)
  matrix products  119 us (8%)
  local copies, waits for them, and re-layouts  108 us (8%)
  other arithmetic  87.9 us (6%)
  starting transfers between devices  33.8 us (2%)
  between operations  29.4 us (2%)
  waiting for transfers between devices  16.8 us (1%)
    pallas_call x3, Pallas kernels, reduce_rows(): pl.pallas_call(functools.partial(reduce_kernel, ranges, shard_units, devi...  376 us
    pallas_call x1, Pallas kernels, gather_rows(): pl.pallas_call(functools.partial(gather_kernel, openings, ahead, devices)...  229 us
    pallas_call x1, Pallas kernels, spread_rows(): pl.pallas_call(functools.partial(spread_kernel, devices), out_shape=(jax....  196 us
    pallas_call x1, Pallas kernels, self_backward(): pl.pallas_call(functools.partial(self_backward_kernel, heads, dim), out_s...  53.1 us
    dot_general x9, matrix products, dot_nn(): lax.dot_general(left, right, (((1,), (0,)), ((), ())), preferred_element_...  42.4 us
    pallas_call x1, Pallas kernels, feed_backward(): pl.pallas_call(feed_backward_kernel, out_shape=(jax.ShapeDtypeStruct((cou...  37.2 us
    dot_general x7, matrix products, dot_nt(): lax.dot_general(left, right, (((1,), (1,)), ((), ())), preferred_element_...  34.7 us
    pallas_call x1, Pallas kernels, sum_all(): pl.pallas_call(functools.partial(sum_kernel, devices), out_shape=(jax.Sha...  30.9 us
  transfers between devices with their start and end apart: 6, of which 1 were waited for; matrix products, arithmetic and copies ran while one was open for 7% of the time, Pallas kernels for 39%

profile of v1, /device:TPU:0, one launch (start us, length us, event | category | flops | bytes accessed | tf_op | source)
XLA Modules:
  0.0 1441.1 jit_solution(18189511192995021748)
XLA Ops:
  24.2 229.5 %shard_map.195 = (bf16[2208,8,1152]{2,1,0:T(8,128)(2,1)}, bf16[1824,8,1152]{2,1,0:T(8,128)(2,1)}) custom-call(bf16[125,8,1152]{2,1,0:T(8,128)(2,1)} %convert_bitcast_fusion.shard_ref), custom_call_target="tpu_custom_call" | custom-call | tf_op jit(solution)/shard_map/pallas_call | solution.py:1168
  253.7 7.0 slice.206
  264.9 9.9 fusion.13
  275.5 6.5 fusion.27
  287.7 11.2 shard_map.196
  298.9 6.3 copy.118
  305.2 9.1 all-to-all-start
  329.4 195.9 %shard_map.197 = (bf16[1824,8,1152]{2,1,0:T(8,128)(2,1)}, f32[32,18,128]{2,1,0:T(8,128)}) custom-call(bf16[1824,8,1152]{2,1,0:T(8,128)(2,1)} %get-tuple-element.58.rows_ref, f32[18,128]{1,0:T(8,128)} %broadcast_divide_fusion.block_ref), custom_call_target="tpu_custom_call", output_to_operand_aliasing={{0}: (0, {})} | custom-call | tf_op jit(solution)/shard_map/pallas_call | solution.py:1147
  535.1 6.2 copy.119
  541.4 30.1 %shard_map.198 = bf16[8,2,256,144]{3,2,1,0:T(8,128)(2,1)} custom-call(s32[2,8]{1,0:T(2,128)} %and_select_fusion.start_ref, s32[2,8]{1,0:T(2,128)} %bitcast.399, bf16[8,2,256,432]{3,2,1,0:T(8,128)(2,1)} %bitcast.347), custom_call_target="tpu_custom_call" | custom-call | tf_op jit(solution)/shard_map/pallas_call | solution.py:150
  575.1 7.3 all-to-all-start.1
  594.9 16.7 %all-to-all-done.1 = bf16[8,512,144]{1,2,0:T(8,128)(2,1)S(1)} async-done(((bf16[8,512,144]{1,2,0:T(8,128)(2,1)}), bf16[8,512,144]{1,2,0:T(8,128)(2,1)S(1)}, u32[]{:S(2)}, u32[]{:S(2)}) %all-to-all-start.1) | async-done | bytes 1179680 | tf_op jit(solution)/shard_map/all_to_all | solution.py:1685
  621.6 13.7 shard_map.199
  635.2 6.1 fusion.186
  646.5 21.6 %shard_map.200 = (f32[512,4608]{1,0:T(8,128)}, bf16[512,4608]{1,0:T(8,128)(2,1)}, f32[512,1152]{1,0:T(8,128)}) custom-call(bf16[512,1152]{1,0:T(8,128)(2,1)} %fusion.54.rows_ref, bf16[14592,1152]{1,0:T(8,128)(2,1)} %bitcast.341, bf16[14592,1152]{1,0:T(8,128)(2,1)} %bitcast.342, f32[6,1,768]{2,1,0:T(1,128)} %reshape.813.b_up_ref, ...), custom_call_target="tpu_custom_call" | custom-call | tf_op jit(solution)/shard_map/pallas_call | solution.py:1429
  677.2 6.3 fusion.72
  683.5 11.8 shard_map.201
  711.3 37.2 %shard_map.203 = (f32[512,1152]{1,0:T(8,128)}, bf16[4608,1152]{1,0:T(8,128)(2,1)}, bf16[4608,1152]{1,0:T(8,128)(2,1)}, f32[6,1,768]{2,1,0:T(1,128)}) custom-call(bf16[512,1152]{1,0:T(8,128)(2,1)} %bitcast.368, bf16[14592,1152]{1,0:T(8,128)(2,1)} %bitcast.343, bf16[14592,1152]{1,0:T(8,128)(2,1)} %bitcast.344, f32[512,4608]{1,0:T(8,128)} %get-tuple-element.66.before_ref, ...), custom_call_target="tpu_custom_call" | custom-call | tf_op jit(solution)/shard_map/pallas_call | solution.py:1474
  765.0 13.3 shard_map.204
  790.1 7.0 multiply_reduce_fusion.10
  808.8 146.7 %shard_map.205 = bf16[125,8,1152]{2,1,0:T(8,128)(2,1)} custom-call(bf16[576,8,1152]{2,1,0:T(8,128)(2,1)} %bitcast.353, bf16[576,8,1152]{2,1,0:T(8,128)(2,1)} %bitcast.354), custom_call_target="tpu_custom_call" | custom-call | tf_op jit(solution)/shard_map/pallas_call | solution.py:768
  973.5 53.1 %shard_map.206 = (bf16[8,2,256,432]{3,2,1,0:T(8,128)(2,1)}, f32[2,1,288]{2,1,0:T(1,128)}) custom-call(s32[2,8]{1,0:T(2,128)} %and_select_fusion.start_ref, s32[2,8]{1,0:T(2,128)} %bitcast.400, bf16[8,2,256,432]{3,2,1,0:T(8,128)(2,1)} %bitcast.348, bf16[8,2,256,144]{3,2,1,0:T(8,128)(2,1)} %bitcast.358), custom_call_target="tpu_custom_call" | custom-call | tf_op jit(solution)/shard_map/pallas_call | solution.py:233
  1045.0 6.3 copy.130
  1051.4 12.4 all-to-all-start.3
  1079.7 12.5 copy.132
  1092.2 142.7 %shard_map.207 = bf16[125,8,1152]{2,1,0:T(8,128)(2,1)} custom-call(bf16[48,8,1152]{2,1,0:T(8,128)(2,1)} %bitcast.370, bf16[480,8,1152]{2,1,0:T(8,128)(2,1)} %bitcast.349, bf16[144,8,1152]{2,1,0:T(8,128)(2,1)} %bitcast.373, bf16[144,8,1152]{2,1,0:T(8,128)(2,1)} %bitcast.355, bf16[144,8,1152]{2,1,0:T(8,128)(2,1)} %bitcast.372, ...), custom_call_target="tpu_custom_call" | custom-call | tf_op jit(solution)/shard_map/pallas_call | solution.py:768
  1234.9 6.2 copy.133.grad_ref
  1241.2 17.0 %shard_map.208 = (f32[512,1152]{1,0:T(8,128)}, bf16[3,8,144,1152]{3,2,1,0:T(8,128)(2,1)}) custom-call(bf16[8,512,432]{2,1,0:T(8,128)(2,1)} %copy.133.grad_ref, bf16[3,8,144,1152]{3,2,1,0:T(8,128)(2,1)} %bitcast.346, bf16[512,1152]{1,0:T(8,128)(2,1)} %fusion.52.rows_ref), custom_call_target="tpu_custom_call" | custom-call | tf_op jit(solution)/shard_map/pallas_call | solution.py:1376
  1267.0 6.7 constant_dynamic-update-slice_fusion.5
  1277.1 86.8 %shard_map.209 = (bf16[125,8,1152]{2,1,0:T(8,128)(2,1)}, bf16[32,184,128]{2,1,0:T(8,128)(2,1)}) custom-call(bf16[432,8,1152]{2,1,0:T(8,128)(2,1)} %bitcast.360, bf16[144,8,1152]{2,1,0:T(8,128)(2,1)} %bitcast.356, bf16[184,128]{1,0:T(8,128)(2,1)} %reshape.791.refs_2_), custom_call_target="tpu_custom_call" | custom-call | tf_op jit(solution)/shard_map/pallas_call | solution.py:768
  1384.0 30.9 %shard_map.210 = (f32[32,3,8,128]{3,2,1,0:T(8,128)S(1)}, f32[8,128]{1,0:T(8,128)S(1)}) custom-call(f32[32,4,8,128]{3,2,1,0:T(8,128)S(1)} %concatenate.80.parts_ref), custom_call_target="tpu_custom_call" | custom-call | tf_op jit(solution)/shard_map/pallas_call | solution.py:1254
  1420.6 11.0 multiply_subtract_fusion
  (516 shorter events, 226.9 us)
Async XLA Ops:
  7.2 580.2 %all-gather.3.cloned.1.call-start = ((), (), s32[]{:S(2)}) async-start(), calls=%async_computation.4 | async-start | bytes 4976640 | tf_op jit(solution)/shard_map/all_gather | solution.py:1669
  21.9 264.1 %copy-start.63 = (f32[512]{0:T(512)}, f32[512]{0:T(512)S(1)}, u32[]{:S(2)}) copy-start(f32[512]{0:T(512)S(1)} %broadcast_multiply_fusion.2) | copy-start | bytes 6148
  22.6 263.4 %copy-start.83 = (f32[512]{0:T(512)}, f32[512]{0:T(512)S(1)}, u32[]{:S(2)}) copy-start(f32[512]{0:T(512)S(1)} %fusion.173) | copy-start | bytes 6148
  305.2 229.9 %all-to-all-start = ((bf16[8,512,432]{1,2,0:T(8,128)(2,1)}), bf16[8,512,432]{1,2,0:T(8,128)(2,1)}, u32[]{:S(2)}, u32[]{:S(2)}) async-start(bf16[8,512,432]{1,2,0:T(8,128)(2,1)} %copy.118), calls=%async_computation | async-start | bytes 7077888 | tf_op jit(solution)/shard_map/all_to_all | solution.py:1668
  328.6 196.7 %copy-start.108 = (f32[2,120]{1,0:T(2,128)}, f32[2,120]{1,0:T(2,128)S(1)}, u32[]{:S(2)}) copy-start(f32[2,120]{1,0:T(2,128)S(1)} %compare_convert_fusion.3) | copy-start | bytes 2884
  575.1 36.4 %all-to-all-start.1 = ((bf16[8,512,144]{1,2,0:T(8,128)(2,1)}), bf16[8,512,144]{1,2,0:T(8,128)(2,1)S(1)}, u32[]{:S(2)}, u32[]{:S(2)}) async-start(bf16[8,512,144]{1,2,0:T(8,128)(2,1)} %copy.120), calls=%async_computation.1 | async-start | bytes 2359296 | tf_op jit(solution)/shard_map/all_to_all | solution.py:1685
  582.5 444.2 %all-gather.5.cloned.1.call-start = ((), (), s32[]{:S(2)}) async-start(), calls=%async_computation.5 | async-start | bytes 4976640 | tf_op jit(solution)/shard_map/all_gather | solution.py:1802
  615.7 19.6 %copy-start.2 = (f32[512,1152]{1,0:T(8,128)}, f32[512,1152]{1,0:T(8,128)S(1)}, u32[]{:S(2)}) copy-start(f32[512,1152]{1,0:T(8,128)S(1)} %get-tuple-element.224) | copy-start | bytes 7077892
  644.2 23.9 %copy-start.85 = (f32[512]{0:T(512)}, f32[512]{0:T(512)S(1)}, u32[]{:S(2)}) copy-start(f32[512]{0:T(512)S(1)} %multiply_reduce_fusion.8) | copy-start | bytes 6148
  644.8 23.3 %copy-start.81 = (f32[512]{0:T(512)}, f32[512]{0:T(512)S(1)}, u32[]{:S(2)}) copy-start(f32[512]{0:T(512)S(1)} %get-tuple-element.210) | copy-start | bytes 6148
  646.5 21.6 %copy-start.48 = (f32[2,1152]{1,0:T(2,128)S(1)}, f32[2,1152]{1,0:T(2,128)}, u32[]{:S(2)}) copy-start(f32[2,1152]{1,0:T(2,128)} %get-tuple-element.183) | copy-start | bytes 27652
  677.2 18.3 %copy-start.32 = (f32[32,2,1152]{2,0,1:T(8,128)S(1)}, f32[32,2,1152]{2,0,1:T(8,128)}, u32[]{:S(2)}) copy-start(f32[32,2,1152]{2,0,1:T(8,128)} %copy.123) | copy-start | bytes 884740
  711.3 37.2 %copy-start.1 = (f32[512,1152]{1,0:T(8,128)S(1)}, f32[512,1152]{1,0:T(8,128)}, u32[]{:S(2)}) copy-start(f32[512,1152]{1,0:T(8,128)} %get-tuple-element.156) | copy-start | bytes 7077892
  711.3 37.2 %copy-start.47 = (f32[2,1152]{1,0:T(2,128)S(1)}, f32[2,1152]{1,0:T(2,128)}, u32[]{:S(2)}) copy-start(f32[2,1152]{1,0:T(2,128)} %get-tuple-element.185) | copy-start | bytes 27652
  801.4 169.5 %all-to-all-start.2 = ((bf16[8,512,144]{1,2,0:T(8,128)(2,1)}), bf16[8,512,144]{1,2,0:T(8,128)(2,1)S(1)}, u32[]{:S(2)}, u32[]{:S(2)}) async-start(bf16[8,512,144]{1,2,0:T(8,128)(2,1)} %bitcast.365), calls=%async_computation.2 | async-start | bytes 2359296 | tf_op jit(solution)/shard_map/all_to_all | solution.py:1825
  808.8 146.8 %copy-start.18 = (bf16[8,512,144]{1,2,0:T(8,128)(2,1)S(1)}, bf16[8,512,144]{1,2,0:T(8,128)(2,1)}, u32[]{:S(2)}) copy-start(bf16[8,512,144]{1,2,0:T(8,128)(2,1)} %copy-done.17) | copy-start | bytes 3538948
  808.8 146.8 %copy-start.34 = (bf16[2,256,1152]{2,1,0:T(8,128)(2,1)S(1)}, bf16[2,256,1152]{2,1,0:T(8,128)(2,1)}, u32[]{:S(2)}) copy-start(bf16[2,256,1152]{2,1,0:T(8,128)(2,1)} %copy-done.33) | copy-start | bytes 3538948
  1051.3 16.7 %copy-start.67 = (f32[2,1152]{1,0:T(2,128)S(1)}, f32[2,1152]{1,0:T(2,128)}, u32[]{:S(2)}) copy-start(f32[2,1152]{1,0:T(2,128)} %get-tuple-element.110) | copy-start | bytes 27652
  1051.3 16.7 %copy-start.91 = (f32[6,1,768]{2,1,0:T(1,128)S(1)}, f32[6,1,768]{2,1,0:T(1,128)}, u32[]{:S(2)}) copy-start(f32[6,1,768]{2,1,0:T(1,128)} %get-tuple-element.96) | copy-start | bytes 55300
  1051.3 16.7 %copy-start.74 = (f32[1152]{0:T(1024)S(1)}, f32[1152]{0:T(1024)}, u32[]{:S(2)}) copy-start(f32[1152]{0:T(1024)} %get-tuple-element.167) | copy-start | bytes 13828
  1051.3 17.3 %copy-start.79 = (f32[1152]{0:T(1024)S(1)}, f32[1152]{0:T(1024)}, u32[]{:S(2)}) copy-start(f32[1152]{0:T(1024)} %get-tuple-element.105) | copy-start | bytes 13828
  1051.3 17.9 %copy-start.69 = (f32[2,1152]{1,0:T(2,128)S(1)}, f32[2,1152]{1,0:T(2,128)}, u32[]{:S(2)}) copy-start(f32[2,1152]{1,0:T(2,128)} %get-tuple-element.106) | copy-start | bytes 27652
  1051.3 19.9 %copy-start.52 = (f32[2,1152]{1,0:T(2,128)S(1)}, f32[2,1152]{1,0:T(2,128)}, u32[]{:S(2)}) copy-start(f32[2,1152]{1,0:T(2,128)} %get-tuple-element.189) | copy-start | bytes 27652
  1051.3 19.8 %copy-start.55 = (f32[2,256,16]{1,2,0:T(8,128)S(1)}, f32[2,256,16]{1,2,0:T(8,128)}, u32[]{:S(2)}) copy-start(f32[2,256,16]{1,2,0:T(8,128)} %copy-done.54) | copy-start | bytes 98308
  1051.4 19.8 %copy-start.57 = (f32[2,256,16]{1,2,0:T(8,128)S(1)}, f32[2,256,16]{1,2,0:T(8,128)}, u32[]{:S(2)}) copy-start(f32[2,256,16]{1,2,0:T(8,128)} %copy-done.56) | copy-start | bytes 98308
  1051.4 19.8 %copy-start.62 = (f32[2,1152]{1,0:T(2,128)S(1)}, f32[2,1152]{1,0:T(2,128)}, u32[]{:S(2)}) copy-start(f32[2,1152]{1,0:T(2,128)} %get-tuple-element.190) | copy-start | bytes 27652
  1051.4 183.5 %all-to-all-start.3 = ((bf16[8,512,432]{1,2,0:T(8,128)(2,1)}), bf16[8,512,432]{1,2,0:T(8,128)(2,1)}, u32[]{:S(2)}, u32[]{:S(2)}) async-start(bf16[8,512,432]{1,2,0:T(8,128)(2,1)} %copy.130), calls=%async_computation.3 | async-start | bytes 7077888 | tf_op jit(solution)/shard_map/all_to_all | solution.py:1869
  1241.2 17.0 %copy-start.45 = (f32[2,1152]{1,0:T(2,128)S(1)}, f32[2,1152]{1,0:T(2,128)}, u32[]{:S(2)}) copy-start(f32[2,1152]{1,0:T(2,128)} %copy-done.44) | copy-start | bytes 27652
  1383.1 35.6 %copy-start.134 = (f32[1,128]{1,0:T(1,128)S(1)}, f32[1,128]{1,0:T(1,128)}, u32[]{:S(2)}) copy-start(f32[1,128]{1,0:T(1,128)} %get-tuple-element.99) | copy-start | bytes 1540
  1383.2 36.2 %copy-start.27 = (f32[78,1152]{1,0:T(8,128)S(1)}, f32[78,1152]{1,0:T(8,128)}, u32[]{:S(2)}) copy-start(f32[78,1152]{1,0:T(8,128)} %param.19) | copy-start | bytes 1078276
  1383.2 36.2 %copy-start.41 = (f32[78,1152]{1,0:T(8,128)S(1)}, f32[78,1152]{1,0:T(8,128)}, u32[]{:S(2)}) copy-start(f32[78,1152]{1,0:T(8,128)} %param.22) | copy-start | bytes 1078276
  1383.2 36.2 %copy-start.42 = (f32[78,1152]{1,0:T(8,128)S(1)}, f32[78,1152]{1,0:T(8,128)}, u32[]{:S(2)}) copy-start(f32[78,1152]{1,0:T(8,128)} %param.23) | copy-start | bytes 1078276
  (115 other events, 545.7 us)
Sparse Core Ops, SparseCore 0:
  299.0 156.4 all-gather.2
  786.1 131.0 all-gather.4

commit v2 on v1

--- a/solution.py
+++ b/solution.py
@@ -369,8 +369,9 @@
 ):
     rows_refs, refs = refs[: len(sources)], list(refs[len(sources) :])
     if receivers:
-        block_ref, all_ref = refs.pop(0), refs.pop(1)
-        refs, push_sems = refs[:-3], refs[-3:]
+        block_ref, parts_ref = refs.pop(0), refs.pop(0)
+        all_ref, got_ref = refs.pop(1), refs.pop(1)
+        refs, push, push_parts = refs[:-6], refs[-6:-3], refs[-3:]
     (
     out_ref,
     own_s,
@@ -553,7 +554,8 @@
 
     lax.fori_loop(0, tiles, start_core, 0)
     if receivers:
-        start_push(block_ref, all_ref, devices, receivers, me, *push_sems)
+        start_push(parts_ref, got_ref, devices, devices, me, *push_parts, scatter=True)
+        start_push(block_ref, all_ref, devices, receivers, me, *push)
 
     def one_step(step, carry):
         @pl.when(step < tiles)
@@ -652,7 +654,8 @@
 
     lax.fori_loop(0, tiles, finish, 0)
     if receivers:
-        finish_push(block_ref, all_ref, devices, receivers, me, *push_sems)
+        finish_push(parts_ref, got_ref, devices, devices, me, *push_parts, scatter=True)
+        finish_push(block_ref, all_ref, devices, receivers, me, *push)
     far = TILE_START - TILE * (TILE_START // TILE)
     begin = me * shard_units
     first_at = lax.rem(PIECE - lax.rem(begin + PIECE - far % PIECE, PIECE), PIECE)
@@ -692,11 +695,11 @@
             arrive(covered + step, 1)
 
 
-def push_copy(block_ref, all_ref, devices, me, step, send_sem, recv_sem):
+def push_copy(block_ref, all_ref, devices, me, step, send_sem, recv_sem, scatter):
     seq_count = devices // 4
     other = lax.rem(me + step, devices)
     return other, pltpu.make_async_remote_copy(
-        src_ref=block_ref,
+        src_ref=block_ref.at[other] if scatter else block_ref,
         dst_ref=all_ref.at[me],
         send_sem=send_sem.at[step],
         recv_sem=recv_sem.at[me],
@@ -705,13 +708,17 @@
     )
 
 
-def start_push(block_ref, all_ref, devices, receivers, me, send_sem, recv_sem, keep_sem):
+def start_push(block_ref, all_ref, devices, receivers, me, send_sem, recv_sem, keep_sem, scatter=False):
+    own_ref = block_ref.at[me] if scatter else block_ref
+
     @pl.when(me < receivers)
     def _():
-        pltpu.make_async_copy(block_ref, all_ref.at[me], keep_sem).start()
+        pltpu.make_async_copy(own_ref, all_ref.at[me], keep_sem).start()
 
     def send(step, carry):
-        other, sending = push_copy(block_ref, all_ref, devices, me, step, send_sem, recv_sem)
+        other, sending = push_copy(
+            block_ref, all_ref, devices, me, step, send_sem, recv_sem, scatter
+        )
 
         @pl.when(other < receivers)
         def _():
@@ -722,13 +729,19 @@
     lax.fori_loop(1, devices, send, 0)
 
 
-def finish_push(block_ref, all_ref, devices, receivers, me, send_sem, recv_sem, keep_sem):
+def finish_push(
+    block_ref, all_ref, devices, receivers, me, send_sem, recv_sem, keep_sem, scatter=False
+):
+    own_ref = block_ref.at[me] if scatter else block_ref
+
     @pl.when(me < receivers)
     def _():
-        pltpu.make_async_copy(block_ref, all_ref.at[me], keep_sem).wait()
+        pltpu.make_async_copy(own_ref, all_ref.at[me], keep_sem).wait()
 
     def finish(step, carry):
-        other, sending = push_copy(block_ref, all_ref, devices, me, step, send_sem, recv_sem)
+        other, sending = push_copy(
+            block_ref, all_ref, devices, me, step, send_sem, recv_sem, scatter
+        )
 
         @pl.when(other < receivers)
         def _():
@@ -738,7 +751,7 @@
 
         @pl.when(me < receivers)
         def _():
-            pltpu.make_async_copy(block_ref, all_ref.at[source], recv_sem.at[source]).wait()
+            pltpu.make_async_copy(own_ref, all_ref.at[source], recv_sem.at[source]).wait()
 
         return carry
 
@@ -750,7 +763,7 @@
     return [dma((devices,)), dma((devices,)), dma]
 
 
-def reduce_rows(ranges, shard_units, devices, collective_id, pieces, block=None, receivers=0):
+def reduce_rows(ranges, shard_units, devices, collective_id, pieces, blocks=(), receivers=0):
     tiles = sum(stop - start for start, stop in ranges)
     width = pieces[0][0].shape[1]
     sources = tuple(piece[1:] for piece in pieces)
@@ -762,9 +775,10 @@
         return pltpu.VMEM(shape, jnp.bfloat16)
 
     dma = pltpu.SemaphoreType.DMA
-    blocks = [] if block is None else [block]
     outs = [jax.ShapeDtypeStruct((shard_units, UNIT, width), jnp.bfloat16)]
-    outs += [jax.ShapeDtypeStruct((devices,) + one.shape, one.dtype) for one in blocks]
+    if blocks:
+        outs.append(jax.ShapeDtypeStruct((devices,) + blocks[0].shape, blocks[0].dtype))
+        outs.append(jax.ShapeDtypeStruct(blocks[1].shape, blocks[1].dtype))
     out = pl.pallas_call(
         functools.partial(reduce_kernel, ranges, shard_units, devices, sources, receivers),
         out_shape=outs,
@@ -796,7 +810,7 @@
             dma((tiles, PIECE)),
             dma((shard_units,)),
         ]
-        + (push_sems(devices) if blocks else []),
+        + (push_sems(devices) + push_sems(devices) if blocks else []),
         compiler_params=pltpu.CompilerParams(
             collective_id=collective_id, has_side_effects=True, vmem_limit_bytes=VMEM_BYTES
         ),
@@ -1206,72 +1220,6 @@
     )(block)
 
 
-def sum_kernel(devices, parts_ref, out_ref, extra_ref, got_s, part_s, send_sem, recv_sem, keep_sem, *sems):
-    seq_count = devices // 4
-    me = lax.axis_index("dp") * seq_count + lax.axis_index("seq")
-    keep = pltpu.make_async_copy(parts_ref.at[me], got_s.at[me], keep_sem)
-    keep.start()
-    greet_all(devices, seq_count)
-
-    def scatter(step):
-        other = lax.rem(me + step, devices)
-        return pltpu.make_async_remote_copy(
-            src_ref=parts_ref.at[other],
-            dst_ref=got_s.at[me],
-            send_sem=send_sem.at[step],
-            recv_sem=recv_sem.at[me],
-            device_id=(lax.div(other, seq_count), lax.rem(other, seq_count)),
-            device_id_type=MESH,
-        )
-
-    def start(step, carry):
-        scatter(step).start()
-        return carry
-
-    def finish(step, carry):
-        scatter(step).wait_send()
-        source = lax.rem(me + devices - step, devices)
-        pltpu.make_async_copy(parts_ref.at[0], got_s.at[source], recv_sem.at[source]).wait()
-        return carry
-
-    lax.fori_loop(1, devices, start, 0)
-    keep.wait()
-    lax.fori_loop(1, devices, finish, 0)
-    total = jnp.sum(got_s[...], axis=0)
-    part_s[...] = total[:-1]
-    extra_ref[...] = total[-1]
-    start_push(part_s, out_ref, devices, devices, me, *sems)
-    finish_push(part_s, out_ref, devices, devices, me, *sems)
-
-
-def sum_all(array, extra, devices, collective_id):
-    tile = 8 * 128
-    count = -(-array.size // (tile * devices))
-    flat = jnp.pad(array.reshape(-1), (0, count * tile * devices - array.size))
-    parts = flat.reshape(devices, count, 8, 128)
-    parts = jnp.concatenate([parts, jnp.full((devices, 1, 8, 128), extra)], axis=1)
-    vmem = pl.BlockSpec(memory_space=pltpu.VMEM)
-    out, total = pl.pallas_call(
-        functools.partial(sum_kernel, devices),
-        out_shape=(
-            jax.ShapeDtypeStruct((devices, count, 8, 128), jnp.float32),
-            jax.ShapeDtypeStruct((8, 128), jnp.float32),
-        ),
-        in_specs=[vmem],
-        out_specs=(vmem, vmem),
-        scratch_shapes=[
-            pltpu.VMEM((devices, count + 1, 8, 128), jnp.float32),
-            pltpu.VMEM((count, 8, 128), jnp.float32),
-        ]
-        + push_sems(devices)
-        + push_sems(devices),
-        compiler_params=pltpu.CompilerParams(
-            collective_id=collective_id, has_side_effects=True, vmem_limit_bytes=16 * 1024 * 1024
-        ),
-    )(parts)
-    return out.reshape(-1)[: array.size].reshape(array.shape), total[0, 0]
-
-
 def contrast_kernel(pooled_ref, pick_ref, row_ref, col_ref, scale_ref, pool_ref, text_ref, loss_ref):
     count = pick_ref.shape[1]
     scale = scale_ref[0, 0] / contrastive_sharpness_divisor
@@ -1484,6 +1432,26 @@
         out_specs=(whole, block, block, line),
         compiler_params=pltpu.CompilerParams(vmem_limit_bytes=VMEM_BYTES),
     )(grad, up, down, before, act, rows)
+
+
+def caption_grad_kernel(rows_ref, grad_ref, out_ref):
+    out_ref[...] = low(dot_tn(rows_ref[...], grad_ref[...]))
+
+
+def caption_grad(rows, grad):
+    count, depth = rows.shape
+    block = 512
+    return pl.pallas_call(
+        caption_grad_kernel,
+        out_shape=jax.ShapeDtypeStruct((depth, grad.shape[1]), jnp.bfloat16),
+        grid=(depth // block,),
+        in_specs=[
+            pl.BlockSpec((count, block), lambda j: (0, j)),
+            pl.BlockSpec(grad.shape, lambda j: (0, 0)),
+        ],
+        out_specs=pl.BlockSpec((block, grad.shape[1]), lambda j: (j, 0)),
+        compiler_params=pltpu.CompilerParams(vmem_limit_bytes=VMEM_BYTES),
+    )(rows, grad)
 
 
 def adamw(param, grad, first, second, rate, decay):
@@ -1810,7 +1778,7 @@
     grad_caption_first = caption_act_back(dot_nt(grad_text_low, text_two))[0]
     grad_caption_low = low(grad_caption_first)
     head_rows = TILE_START * UNIT - sum(layout[:3]) + TILE * UNIT // 2 if paired else 0
-    weight_text_one = dot_tn(caption_low[:, head_rows:], grad_caption_low)
+    weight_text_one = caption_grad(caption_low, grad_caption_low)
 
     grad_attended = (grad_one * gate_one).reshape(rows, width)
     grad_gate_one = jnp.sum(grad_one * attended, axis=1, keepdims=True)
@@ -1843,8 +1811,7 @@
         time_rows = layout[0] + layout[1]
         block_rows = layout[2]
         weight_self_out = low(weight_self_out)
-        first_half = low(dot_tn(caption_low[:, :head_rows], grad_caption_low))
-        first_half = jnp.pad(first_half, ((TILE * UNIT // 2 - head_rows, 0), (0, 0)))
+        first_half = jnp.pad(weight_text_one[:head_rows], ((TILE * UNIT // 2 - head_rows, 0), (0, 0)))
         (
             first_half,
             weight_text_one,
@@ -1877,7 +1844,7 @@
             3,
             (
                 (first_half, 0, 1),
-                (weight_text_one, 0, 10),
+                (weight_text_one, head_rows // UNIT, 10),
                 (weight_text_two, 0, 3),
                 (weight_self_out, TILE // 2, 2),
                 (weight_cross_query, 0, 3),
@@ -1904,21 +1871,51 @@
     grad_time_first = time_act_back(dot_nt(grad_embed_low, time_two))[0]
     weight_time_one = dot_tn(time_low, low(grad_time_first))
 
+    grad_vector = jnp.concatenate(
+        [
+            grad_table,
+            grad_final_table,
+            grad_patch_in,
+            grad_patch_out,
+            jnp.sum(grad_zero, axis=0)[None, :],
+            jnp.sum(grad_time_first, axis=0)[None, :],
+            jnp.sum(grad_embed, axis=0)[None, :],
+            grad_table,
+            jnp.sum(grad_caption_first, axis=0)[None, :],
+            jnp.sum(grad_text, axis=0)[None, :],
+            grad_bias_query[None, :],
+            grad_bias_value[None, :],
+            jnp.sum(grad_attended, axis=0)[None, :],
+            jnp.sum(grad_query_cross, axis=0)[None, :],
+            jnp.sum(grad_kv[:, width:], axis=0)[None, :],
+            jnp.sum(grad_two_flat, axis=0)[None, :],
+            grad_b_up.reshape(-1, width),
+            jnp.sum(grad_feed, axis=0)[None, :],
+            jnp.full((2, width), squared_loss),
+        ],
+        axis=0,
+    )
     if paired:
+        tile_size = UNIT * 128
+        tile_count = -(-grad_vector.size // (tile_size * devices))
+        parts = jnp.pad(
+            grad_vector.reshape(-1), (0, tile_count * tile_size * devices - grad_vector.size)
+        ).reshape(devices, tile_count, UNIT, 128)
         holders = -(-(time_rows + block_rows) // shard_rows)
         own_grads = jnp.concatenate(
             [grad_mod_low, grad_embed_low, low(grad_time_first), embed_low, time_act_low, time_low],
             axis=1,
         )
-        summed_joint, grads_all = reduce_rows(
+        summed_joint, grads_all, vector_got = reduce_rows(
             ((7, 12),),
             shard_rows // UNIT,
             devices,
             4,
             ((low(weight_joint), 0, 9), (weight_self_out, 0, 1)),
-            own_grads.reshape(-1, 128),
+            (own_grads.reshape(-1, 128), parts),
             holders,
         )
+        vector_part = jnp.sum(vector_got, axis=0)
         grads_all = jnp.where(device_index() < holders, grads_all, 0)
         grads_all = grads_all.reshape(devices * MICRO, -1)
         ends = [6 * width, 7 * width, 8 * width, 9 * width, 10 * width]
@@ -1973,33 +1970,12 @@
         summed = lax.psum_scatter(
             grad_weights, both_axes, scatter_dimension=0, tiled=True
         ).astype(jnp.float32)
-    grad_vector = jnp.concatenate(
-        [
-            grad_table,
-            grad_final_table,
-            grad_patch_in,
-            grad_patch_out,
-            jnp.sum(grad_zero, axis=0)[None, :],
-            jnp.sum(grad_time_first, axis=0)[None, :],
-            jnp.sum(grad_embed, axis=0)[None, :],
-            grad_table,
-            jnp.sum(grad_caption_first, axis=0)[None, :],
-            jnp.sum(grad_text, axis=0)[None, :],
-            grad_bias_query[None, :],
-            grad_bias_value[None, :],
-            jnp.sum(grad_attended, axis=0)[None, :],
-            jnp.sum(grad_query_cross, axis=0)[None, :],
-            jnp.sum(grad_kv[:, width:], axis=0)[None, :],
-            jnp.sum(grad_two_flat, axis=0)[None, :],
-            grad_b_up.reshape(-1, width),
-            jnp.sum(grad_feed, axis=0)[None, :],
-            jnp.full((2, width), squared_loss),
-        ],
-        axis=0,
-    )
     squares = jnp.sum(summed * summed)
     if paired:
-        grad_vectors, squares_all = sum_all(grad_vector, squares, devices, 6)
+        last = jnp.concatenate([vector_part, jnp.full((1, UNIT, 128), squares)], axis=0)
+        last = share(last, devices, 6)
+        squares_all = jnp.sum(last[:, -1, 0, 0])
+        grad_vectors = last[:, :-1].reshape(-1)[: grad_vector.size].reshape(grad_vector.shape)
     else:
         grad_vectors, squares_all = lax.psum((grad_vector, squares), both_axes)
     loss_sum = grad_vectors[vectors.shape[0], 0] + contrast_value

time: 1440 us -> 1420 us (0.986)
  local copies, waits for them, and re-layouts: 108 us -> 87.6 us
    pallas_call x1, Pallas kernels: 30.9 us -> 9.22 us  [caption_grad(): pl.pallas_call(caption_grad_kernel, out_shape=jax.ShapeDtypeStruct((depth...]
    pallas_call x1 -> x2, Pallas kernels: 11.8 us -> 31.9 us  [share(): pl.pallas_call(functools.partial(share_kernel, devices), out_shape=jax.Sh...]
    dot_general x10 -> x8, matrix products: 29.3 us -> 24.1 us  [dot_tn(): lax.dot_general(left, right, (((0,), (0,)), ((), ())), preferred_element_...]
  transfers between devices with their start and end apart: 6 -> 6, of which waited for: 1 -> 1; matrix products, arithmetic and copies ran while one was open for 7% -> 6% of each run, Pallas kernels for 39% -> 41%
where the time goes in v2:
time: 1420 us
  Pallas kernels  1050 us (74%)
  matrix products  114 us (8%)
  local copies, waits for them, and re-layouts  87.6 us (6%)
  other arithmetic  86.3 us (6%)
  starting transfers between devices  33.2 us (2%)
  between operations  29.2 us (2%)
    pallas_call x3, Pallas kernels, reduce_rows(): pl.pallas_call(functools.partial(reduce_kernel, ranges, shard_units, devi...  385 us
    pallas_call x1, Pallas kernels, gather_rows(): pl.pallas_call(functools.partial(gather_kernel, openings, ahead, devices)...  229 us
    pallas_call x1, Pallas kernels, spread_rows(): pl.pallas_call(functools.partial(spread_kernel, devices), out_shape=(jax....  196 us
    pallas_call x1, Pallas kernels, self_backward(): pl.pallas_call(functools.partial(self_backward_kernel, heads, dim), out_s...  53 us
    dot_general x9, matrix products, dot_nn(): lax.dot_general(left, right, (((1,), (0,)), ((), ())), preferred_element_...  42.3 us
    pallas_call x1, Pallas kernels, feed_backward(): pl.pallas_call(feed_backward_kernel, out_shape=(jax.ShapeDtypeStruct((cou...  37.2 us
    dot_general x7, matrix products, dot_nt(): lax.dot_general(left, right, (((1,), (1,)), ((), ())), preferred_element_...  34.9 us
    pallas_call x2, Pallas kernels, share(): pl.pallas_call(functools.partial(share_kernel, devices), out_shape=jax.Sh...  31.9 us
  transfers between devices with their start and end apart: 6, of which 1 were waited for; matrix products, arithmetic and copies ran while one was open for 6% of the time, Pallas kernels for 41%

profile of v2, /device:TPU:0, one launch (start us, length us, event | category | flops | bytes accessed | tf_op | source)
XLA Modules:
  0.0 1416.8 jit_solution(16586592232406042699)
XLA Ops:
  24.1 229.5 %shard_map.195 = (bf16[2208,8,1152]{2,1,0:T(8,128)(2,1)}, bf16[1824,8,1152]{2,1,0:T(8,128)(2,1)}) custom-call(bf16[125,8,1152]{2,1,0:T(8,128)(2,1)} %convert_bitcast_fusion.shard_ref), custom_call_target="tpu_custom_call" | custom-call | tf_op jit(solution)/shard_map/pallas_call | solution.py:1182
  253.6 7.0 slice.205
  264.8 9.9 fusion.12
  275.4 6.5 fusion.26
  287.6 11.2 shard_map.196
  298.8 6.3 copy.110
  305.1 9.1 all-to-all-start
  329.3 195.9 %shard_map.197 = (bf16[1824,8,1152]{2,1,0:T(8,128)(2,1)}, f32[32,18,128]{2,1,0:T(8,128)}) custom-call(bf16[1824,8,1152]{2,1,0:T(8,128)(2,1)} %get-tuple-element.57.rows_ref, f32[18,128]{1,0:T(8,128)} %broadcast_divide_fusion.block_ref), custom_call_target="tpu_custom_call", output_to_operand_aliasing={{0}: (0, {})} | custom-call | tf_op jit(solution)/shard_map/pallas_call | solution.py:1161
  535.0 6.2 copy.111
  541.2 30.1 %shard_map.198 = bf16[8,2,256,144]{3,2,1,0:T(8,128)(2,1)} custom-call(s32[2,8]{1,0:T(2,128)} %and_select_fusion.start_ref, s32[2,8]{1,0:T(2,128)} %bitcast.391, bf16[8,2,256,432]{3,2,1,0:T(8,128)(2,1)} %bitcast.341), custom_call_target="tpu_custom_call" | custom-call | tf_op jit(solution)/shard_map/pallas_call | solution.py:150
  575.0 7.3 all-to-all-start.1
  594.7 12.8 all-to-all-done.1
  617.6 13.7 shard_map.199
  631.3 6.1 fusion.180
  642.5 21.6 %shard_map.200 = (f32[512,4608]{1,0:T(8,128)}, bf16[512,4608]{1,0:T(8,128)(2,1)}, f32[512,1152]{1,0:T(8,128)}) custom-call(bf16[512,1152]{1,0:T(8,128)(2,1)} %fusion.52.rows_ref, bf16[14592,1152]{1,0:T(8,128)(2,1)} %bitcast.334, bf16[14592,1152]{1,0:T(8,128)(2,1)} %bitcast.335, f32[6,1,768]{2,1,0:T(1,128)} %reshape.813.b_up_ref, ...), custom_call_target="tpu_custom_call" | custom-call | tf_op jit(solution)/shard_map/pallas_call | solution.py:1377
  673.2 6.3 fusion.70
  679.6 11.8 shard_map.201
  707.3 37.2 %shard_map.203 = (f32[512,1152]{1,0:T(8,128)}, bf16[4608,1152]{1,0:T(8,128)(2,1)}, bf16[4608,1152]{1,0:T(8,128)(2,1)}, f32[6,1,768]{2,1,0:T(1,128)}) custom-call(bf16[512,1152]{1,0:T(8,128)(2,1)} %bitcast.361, bf16[14592,1152]{1,0:T(8,128)(2,1)} %bitcast.336, bf16[14592,1152]{1,0:T(8,128)(2,1)} %bitcast.337, f32[512,4608]{1,0:T(8,128)} %get-tuple-element.65.before_ref, ...), custom_call_target="tpu_custom_call" | custom-call | tf_op jit(solution)/shard_map/pallas_call | solution.py:1422
  761.0 13.3 shard_map.204
  786.1 7.1 multiply_reduce_fusion.10
  804.6 147.0 %shard_map.206 = bf16[125,8,1152]{2,1,0:T(8,128)(2,1)} custom-call(bf16[576,8,1152]{2,1,0:T(8,128)(2,1)} %bitcast.348, bf16[576,8,1152]{2,1,0:T(8,128)(2,1)} %bitcast.349), custom_call_target="tpu_custom_call" | custom-call | tf_op jit(solution)/shard_map/pallas_call | solution.py:782
  969.6 53.0 %shard_map.207 = (bf16[8,2,256,432]{3,2,1,0:T(8,128)(2,1)}, f32[2,1,288]{2,1,0:T(1,128)}) custom-call(s32[2,8]{1,0:T(2,128)} %and_select_fusion.start_ref, s32[2,8]{1,0:T(2,128)} %bitcast.392, bf16[8,2,256,432]{3,2,1,0:T(8,128)(2,1)} %bitcast.342, bf16[8,2,256,144]{3,2,1,0:T(8,128)(2,1)} %bitcast.351), custom_call_target="tpu_custom_call" | custom-call | tf_op jit(solution)/shard_map/pallas_call | solution.py:233
  1033.8 9.2 shard_map.205
  1045.1 6.3 copy.122
  1051.5 12.2 all-to-all-start.3
  1069.4 153.5 %shard_map.208 = bf16[125,8,1152]{2,1,0:T(8,128)(2,1)} custom-call(bf16[48,8,1152]{2,1,0:T(8,128)(2,1)} %bitcast.363, bf16[512,8,1152]{2,1,0:T(8,128)(2,1)} %bitcast.340, bf16[144,8,1152]{2,1,0:T(8,128)(2,1)} %bitcast.366, bf16[144,8,1152]{2,1,0:T(8,128)(2,1)} %bitcast.346, bf16[144,8,1152]{2,1,0:T(8,128)(2,1)} %bitcast.365, ...), custom_call_target="tpu_custom_call" | custom-call | tf_op jit(solution)/shard_map/pallas_call | solution.py:782
  1222.9 6.2 copy.123.grad_ref
  1229.2 17.0 %shard_map.209 = (f32[512,1152]{1,0:T(8,128)}, bf16[3,8,144,1152]{3,2,1,0:T(8,128)(2,1)}) custom-call(bf16[8,512,432]{2,1,0:T(8,128)(2,1)} %copy.123.grad_ref, bf16[3,8,144,1152]{3,2,1,0:T(8,128)(2,1)} %bitcast.339, bf16[512,1152]{1,0:T(8,128)(2,1)} %fusion.50.rows_ref), custom_call_target="tpu_custom_call" | custom-call | tf_op jit(solution)/shard_map/pallas_call | solution.py:1324
  1255.0 6.7 constant_dynamic-update-slice_fusion.5
  1268.5 84.8 %shard_map.210 = (bf16[125,8,1152]{2,1,0:T(8,128)(2,1)}, bf16[32,184,128]{2,1,0:T(8,128)(2,1)}, f32[32,3,8,128]{3,2,1,0:T(8,128)}) custom-call(bf16[432,8,1152]{2,1,0:T(8,128)(2,1)} %bitcast.353, bf16[144,8,1152]{2,1,0:T(8,128)(2,1)} %bitcast.347, bf16[184,128]{1,0:T(8,128)(2,1)} %reshape.791.refs_2_, f32[32,3,8,128]{3,2,1,0:T(8,128)} %bitcast.371), custom_call_target="tpu_custom_call" | custom-call | tf_op jit(solution)/shard_map/pallas_call | solution.py:782
  1370.3 20.1 %shard_map.211 = f32[32,4,8,128]{3,2,1,0:T(8,128)S(1)} custom-call(f32[4,8,128]{2,1,0:T(8,128)S(1)} %concatenate.80.block_ref), custom_call_target="tpu_custom_call" | custom-call | tf_op jit(solution)/shard_map/pallas_call | solution.py:1211
  1396.3 11.0 multiply_subtract_fusion
  (485 shorter events, 211.9 us)
Async XLA Ops:
  7.2 580.1 %all-gather.3.cloned.1.call-start = ((), (), s32[]{:S(2)}) async-start(), calls=%async_computation.4 | async-start | bytes 4976640 | tf_op jit(solution)/shard_map/all_gather | solution.py:1637
  21.8 264.2 %copy-start.63 = (f32[512]{0:T(512)}, f32[512]{0:T(512)S(1)}, u32[]{:S(2)}) copy-start(f32[512]{0:T(512)S(1)} %broadcast_multiply_fusion.2) | copy-start | bytes 6148
  22.5 263.4 %copy-start.84 = (f32[512]{0:T(512)}, f32[512]{0:T(512)S(1)}, u32[]{:S(2)}) copy-start(f32[512]{0:T(512)S(1)} %fusion.167) | copy-start | bytes 6148
  260.7 14.0 copy-start.116
  305.1 15.5 %copy-start.58 = (s32[2,4,8]{2,1,0:T(4,128)S(1)}, s32[2,4,8]{2,1,0:T(4,128)}, u32[]{:S(2)}) copy-start(s32[2,4,8]{2,1,0:T(4,128)} %param.15) | copy-start | bytes 772
  305.1 229.9 %all-to-all-start = ((bf16[8,512,432]{1,2,0:T(8,128)(2,1)}), bf16[8,512,432]{1,2,0:T(8,128)(2,1)}, u32[]{:S(2)}, u32[]{:S(2)}) async-start(bf16[8,512,432]{1,2,0:T(8,128)(2,1)} %copy.110), calls=%async_computation | async-start | bytes 7077888 | tf_op jit(solution)/shard_map/all_to_all | solution.py:1636
  328.4 196.7 %copy-start.97 = (f32[2,120]{1,0:T(2,128)}, f32[2,120]{1,0:T(2,128)S(1)}, u32[]{:S(2)}) copy-start(f32[2,120]{1,0:T(2,128)S(1)} %compare_convert_fusion.3) | copy-start | bytes 2884
  575.0 32.6 %all-to-all-start.1 = ((bf16[8,512,144]{1,2,0:T(8,128)(2,1)}), bf16[8,512,144]{1,2,0:T(8,128)(2,1)S(1)}, u32[]{:S(2)}, u32[]{:S(2)}) async-start(bf16[8,512,144]{1,2,0:T(8,128)(2,1)} %copy.112), calls=%async_computation.1 | async-start | bytes 2359296 | tf_op jit(solution)/shard_map/all_to_all | solution.py:1653
  582.3 440.3 %all-gather.5.cloned.1.call-start = ((), (), s32[]{:S(2)}) async-start(), calls=%async_computation.5 | async-start | bytes 4976640 | tf_op jit(solution)/shard_map/all_gather | solution.py:1770
  611.7 19.5 %copy-start.2 = (f32[512,1152]{1,0:T(8,128)}, f32[512,1152]{1,0:T(8,128)S(1)}, u32[]{:S(2)}) copy-start(f32[512,1152]{1,0:T(8,128)S(1)} %get-tuple-element.224) | copy-start | bytes 7077892
  617.6 13.7 copy-start.81
  640.2 23.9 %copy-start.86 = (f32[512]{0:T(512)}, f32[512]{0:T(512)S(1)}, u32[]{:S(2)}) copy-start(f32[512]{0:T(512)S(1)} %multiply_reduce_fusion.8) | copy-start | bytes 6148
  640.8 23.3 %copy-start.82 = (f32[512]{0:T(512)}, f32[512]{0:T(512)S(1)}, u32[]{:S(2)}) copy-start(f32[512]{0:T(512)S(1)} %get-tuple-element.210) | copy-start | bytes 6148
  642.5 21.6 %copy-start.48 = (f32[2,1152]{1,0:T(2,128)S(1)}, f32[2,1152]{1,0:T(2,128)}, u32[]{:S(2)}) copy-start(f32[2,1152]{1,0:T(2,128)} %get-tuple-element.183) | copy-start | bytes 27652
  673.2 18.3 %copy-start.31 = (f32[32,2,1152]{2,0,1:T(8,128)S(1)}, f32[32,2,1152]{2,0,1:T(8,128)}, u32[]{:S(2)}) copy-start(f32[32,2,1152]{2,0,1:T(8,128)} %copy.115) | copy-start | bytes 884740
  707.3 37.2 %copy-start.1 = (f32[512,1152]{1,0:T(8,128)S(1)}, f32[512,1152]{1,0:T(8,128)}, u32[]{:S(2)}) copy-start(f32[512,1152]{1,0:T(8,128)} %get-tuple-element.154) | copy-start | bytes 7077892
  707.3 37.2 %copy-start.47 = (f32[2,1152]{1,0:T(2,128)S(1)}, f32[2,1152]{1,0:T(2,128)}, u32[]{:S(2)}) copy-start(f32[2,1152]{1,0:T(2,128)} %get-tuple-element.185) | copy-start | bytes 27652
  797.5 169.6 %all-to-all-start.2 = ((bf16[8,512,144]{1,2,0:T(8,128)(2,1)}), bf16[8,512,144]{1,2,0:T(8,128)(2,1)S(1)}, u32[]{:S(2)}, u32[]{:S(2)}) async-start(bf16[8,512,144]{1,2,0:T(8,128)(2,1)} %bitcast.358), calls=%async_computation.2 | async-start | bytes 2359296 | tf_op jit(solution)/shard_map/all_to_all | solution.py:1793
  804.6 147.0 %copy-start.18 = (bf16[8,512,144]{1,2,0:T(8,128)(2,1)S(1)}, bf16[8,512,144]{1,2,0:T(8,128)(2,1)}, u32[]{:S(2)}) copy-start(bf16[8,512,144]{1,2,0:T(8,128)(2,1)} %copy-done.17) | copy-start | bytes 3538948
  804.6 147.0 %copy-start.33 = (bf16[2,256,1152]{2,1,0:T(8,128)(2,1)S(1)}, bf16[2,256,1152]{2,1,0:T(8,128)(2,1)}, u32[]{:S(2)}) copy-start(bf16[2,256,1152]{2,1,0:T(8,128)(2,1)} %copy-done.32) | copy-start | bytes 3538948
  1051.4 14.0 copy-start.52
  1051.4 14.0 copy-start.55
  1051.5 14.0 copy-start.57
  1051.5 14.0 copy-start.62
  1051.5 14.0 copy-start.78
  1051.5 14.0 copy-start.118
  1051.5 171.4 %all-to-all-start.3 = ((bf16[8,512,432]{1,2,0:T(8,128)(2,1)}), bf16[8,512,432]{1,2,0:T(8,128)(2,1)}, u32[]{:S(2)}, u32[]{:S(2)}) async-start(bf16[8,512,432]{1,2,0:T(8,128)(2,1)} %copy.122), calls=%async_computation.3 | async-start | bytes 7077888 | tf_op jit(solution)/shard_map/all_to_all | solution.py:1836
  1229.2 17.0 %copy-start.45 = (f32[2,1152]{1,0:T(2,128)S(1)}, f32[2,1152]{1,0:T(2,128)}, u32[]{:S(2)}) copy-start(f32[2,1152]{1,0:T(2,128)} %copy-done.44) | copy-start | bytes 27652
  1369.6 24.9 %copy-start.121 = (f32[1,128]{1,0:T(1,128)S(1)}, f32[1,128]{1,0:T(1,128)}, u32[]{:S(2)}) copy-start(f32[1,128]{1,0:T(1,128)} %get-tuple-element.97) | copy-start | bytes 1540
  1369.6 25.5 %copy-start.26 = (f32[78,1152]{1,0:T(8,128)S(1)}, f32[78,1152]{1,0:T(8,128)}, u32[]{:S(2)}) copy-start(f32[78,1152]{1,0:T(8,128)} %param.19) | copy-start | bytes 1078276
  1369.6 25.5 %copy-start.41 = (f32[78,1152]{1,0:T(8,128)S(1)}, f32[78,1152]{1,0:T(8,128)}, u32[]{:S(2)}) copy-start(f32[78,1152]{1,0:T(8,128)} %param.22) | copy-start | bytes 1078276
  1369.6 25.5 %copy-start.42 = (f32[78,1152]{1,0:T(8,128)S(1)}, f32[78,1152]{1,0:T(8,128)}, u32[]{:S(2)}) copy-start(f32[78,1152]{1,0:T(8,128)} %param.23) | copy-start | bytes 1078276
  (99 other events, 487.3 us)
Sparse Core Ops, SparseCore 0:
  298.9 156.4 all-gather.2
  782.0 131.0 all-gather.4

commit v3 on v2

--- a/solution.py
+++ b/solution.py
@@ -320,6 +320,7 @@
 TILE_START = 1024
 LAG = 2
 RING = LAG + 1
+HOPS = 4
 MESH = pl.DeviceIdType.MESH
 
 
@@ -403,7 +404,7 @@
     seq_count = devices // 4
     y, core, z, x = my_place()
     me = (y * 2 + core) * seq_count + z * 2 + x
-    place = ((core * 2 + y) * 2 + x) * 4 + z
+    stride = 5 if tiles % 5 else 3
     half, quarter, eighth = TILE // 2, TILE // 4, TILE // 8
     across_core = peer(y, 1 - core, z, x)
     across_y = peer(1 - y, core, z, x)
@@ -431,7 +432,7 @@
         )
 
     def start_from(copy, t, side):
-        index = t * 2 + side
+        index = lax.rem(t * stride, tiles) * 2 + side
         at = 0
         for rows_ref, (start, count) in zip(rows_refs, sources):
 
@@ -477,72 +478,135 @@
             across_y,
         )
 
-    def z_copy(t, distance):
-        other = z ^ distance
+    def each_three(t, visit):
+        tile = global_tile(ranges, lax.rem(t * stride, tiles))
+
+        def one(index, carry):
+            row = index * PIECE
+            unit = TILE_START + tile * TILE + ((core * 2 + y) * 2 + x) * eighth + row
+            owner = lax.div(unit, shard_units)
+            at = unit - owner * shard_units
+
+            @pl.when(at + PIECE <= shard_units)
+            def _():
+                visit(row, index, PIECE, owner, at)
+
+            @pl.when(at + PIECE > shard_units)
+            def _():
+                for part in range(PIECE):
+                    over = at + part >= shard_units
+                    visit(
+                        row + part,
+                        4 + part,
+                        1,
+                        jnp.where(over, owner + 1, owner),
+                        jnp.where(over, at + part - shard_units, at + part),
+                    )
+
+            return carry
+
+        lax.fori_loop(0, eighth // PIECE, one, 0)
+
+    def z_copy(t, row, slot, count, way):
+        other = (jnp.maximum(z - 1, 0), jnp.minimum(z + 1, 3))[way]
         return remote(
-            third_s.at[lax.rem(t, RING), pl.ds(other * PIECE, PIECE)],
-            along_s.at[t, distance - 1],
-            z_send.at[lax.rem(t, RING), distance - 1],
-            z_recv.at[t, distance - 1],
+            third_s.at[lax.rem(t, HOPS), pl.ds(row, count)],
+            along_s.at[t, way, pl.ds(row, count)],
+            z_send.at[lax.rem(t, HOPS), slot],
+            z_recv.at[t, way, slot],
             peer(y, core, other, x),
         )
 
-    def add(count, step, target, *sources):
-        def one(index, carry):
-            at = index * step
-            total = sources[0](at, step).astype(jnp.float32)
-            for source in sources[1:]:
-                total = total + source(at, step).astype(jnp.float32)
-            target(at, step, total.astype(jnp.bfloat16))
-            return carry
-
-        lax.fori_loop(0, count // step, one, 0)
-
-    def leaf_send_all(t, stage):
-        unit = TILE_START + global_tile(ranges, t) * TILE + place * PIECE
-        owner = lax.div(unit, shard_units)
-        at = unit - owner * shard_units
-
-        def go(part, count, slot, holder):
-            source = leaf_s.at[t, pl.ds(part, count)]
-            target = out_ref.at[pl.ds(slot, count)]
-            sending = remote(
-                source,
-                target,
-                leaf_send.at[t, part],
-                leaf_recv.at[slot],
-                (lax.div(holder, seq_count), lax.rem(holder, seq_count)),
-            )
-
-            @pl.when(holder != me)
+    def arrived(t, row, slot, count, way):
+        part = along_s.at[t, way, pl.ds(row, count)]
+        pltpu.make_async_copy(part, part, z_recv.at[t, way, slot]).wait()
+
+    def total_of(t, row, count, *ways):
+        total = third_s[lax.rem(t, HOPS), pl.ds(row, count)].astype(jnp.float32)
+        for way in ways:
+            total = total + along_s[t, way, pl.ds(row, count)].astype(jnp.float32)
+        return total.astype(jnp.bfloat16)
+
+    def owner_plane(owner):
+        return lax.rem(lax.div(owner, 2), 4)
+
+    def hop(t, number):
+        def visit(row, slot, count, owner, at):
+            to = owner_plane(owner)
+            for way, here, more in (
+                (0, (z > to) & (3 - z == number), z < 3),
+                (1, (z < to) & (z == number), z > 0),
+            ):
+
+                @pl.when(here)
+                def _(way=way, more=more):
+                    @pl.when(more)
+                    def _():
+                        arrived(t, row, slot, count, way)
+                        total = total_of(t, row, count, way)
+                        third_s[lax.rem(t, HOPS), pl.ds(row, count)] = total
+
+                    z_copy(t, row, slot, count, way).start()
+
+        each_three(t, visit)
+
+    def hand_over(t):
+        def visit(row, slot, count, owner, at):
+            to = owner_plane(owner)
+
+            @pl.when(to == z)
             def _():
-                if stage == 0:
-                    sending.start()
-                else:
-                    sending.wait_send()
-
+                for here, ways in (
+                    (z == 0, (0,)),
+                    ((z > 0) & (z < 3), (0, 1)),
+                    (z == 3, (1,)),
+                ):
+
+                    @pl.when(here)
+                    def _(ways=ways):
+                        for way in ways:
+                            arrived(t, row, slot, count, way)
+                        leaf_s[t, pl.ds(row, count)] = total_of(t, row, count, *ways)
+
+                leaf_copy(t, row, slot, count, owner, at, 0)
+
+            @pl.when(to != z)
+            def _():
+                z_copy(t, row, slot, count, 0).wait_send()
+
+        each_three(t, visit)
+
+    def leaf_copy(t, row, slot, count, owner, at, stage):
+        source = leaf_s.at[t, pl.ds(row, count)]
+        target = out_ref.at[pl.ds(at, count)]
+        sending = remote(
+            source,
+            target,
+            leaf_send.at[t, slot],
+            leaf_recv.at[at],
+            (lax.div(owner, seq_count), lax.rem(owner, seq_count)),
+        )
+
+        @pl.when(owner != me)
+        def _():
             if stage == 0:
-
-                @pl.when(holder == me)
-                def _():
-                    pltpu.make_async_copy(source, target, leaf_recv.at[slot]).start()
-
-        together = at + PIECE <= shard_units
-
-        @pl.when(together)
-        def _():
-            go(0, PIECE, at, owner)
-
-        @pl.when(jnp.logical_not(together))
-        def _():
-            for part in range(PIECE):
-                over = at + part >= shard_units
-                go(
-                    part,
-                    1,
-                    jnp.where(over, at + part - shard_units, at + part),
-                    jnp.where(over, owner + 1, owner),
-                )
+                sending.start()
+            else:
+                sending.wait_send()
+
+        if stage == 0:
+
+            @pl.when(owner == me)
+            def _():
+                pltpu.make_async_copy(source, target, leaf_recv.at[at]).start()
+
+    def leaf_done(t):
+        def visit(row, slot, count, owner, at):
+            @pl.when(owner_plane(owner) == z)
+            def _():
+                leaf_copy(t, row, slot, count, owner, at, 1)
+
+        each_three(t, visit)
 
     for t in range(min(2, tiles)):
         start_from(load, t, core)
@@ -621,35 +685,31 @@
                 at = pl.ds(index * 4, 4)
                 mine = first_two_s[slot, pl.ds(x * eighth + index * 4, 4)].astype(jnp.float32)
                 total = mine + first_x_s[t, at].astype(jnp.float32)
-                third_s[slot, at, :, :SPLIT] = total.astype(jnp.bfloat16)
+                third_s[lax.rem(t, HOPS), at, :, :SPLIT] = total.astype(jnp.bfloat16)
                 mine = second_two_s[slot, pl.ds(y * eighth + index * 4, 4)].astype(jnp.float32)
                 total = mine + second_y_s[t, at].astype(jnp.float32)
-                third_s[slot, at, :, SPLIT:] = total.astype(jnp.bfloat16)
+                third_s[lax.rem(t, HOPS), at, :, SPLIT:] = total.astype(jnp.bfloat16)
                 return inner
 
             lax.fori_loop(0, eighth // 4, one, 0)
-            for distance in (1, 2, 3):
-                z_copy(t, distance).start()
-
-        @pl.when(step >= 3 * LAG)
-        def _():
-            t = step - 3 * LAG
-            slot = lax.rem(t, RING)
-            for distance in (1, 2, 3):
-                z_copy(t, distance).wait()
-            total = third_s[slot, pl.ds(z * PIECE, PIECE)].astype(jnp.float32)
-            for distance in (1, 2, 3):
-                total = total + along_s[t, distance - 1].astype(jnp.float32)
-            leaf_s[t] = total.astype(jnp.bfloat16)
-            leaf_send_all(t, 0)
+
+        for number in range(4):
+            old = step - 2 * LAG - number
+
+            @pl.when((old >= 0) & (old < tiles))
+            def _(old=old, number=number):
+                if number < 3:
+                    hop(old, number)
+                else:
+                    hand_over(old)
 
         return carry
 
-    lax.fori_loop(0, tiles + 3 * LAG, one_step, 0)
+    lax.fori_loop(0, tiles + 2 * LAG + 3, one_step, 0)
 
     def finish(t, carry):
         core_copy(t).wait_send()
-        leaf_send_all(t, 1)
+        leaf_done(t)
         return carry
 
     lax.fori_loop(0, tiles, finish, 0)
@@ -795,9 +855,9 @@
             vmem(RING, quarter, UNIT, rest),
             vmem(tiles, eighth, UNIT, SPLIT),
             vmem(tiles, eighth, UNIT, rest),
-            vmem(RING, eighth, UNIT, width),
-            vmem(tiles, 3, PIECE, UNIT, width),
-            vmem(tiles, PIECE, UNIT, width),
+            vmem(HOPS, eighth, UNIT, width),
+            vmem(tiles, 2, eighth, UNIT, width),
+            vmem(tiles, eighth, UNIT, width),
             dma((2,)),
             dma((tiles,)),
             dma((tiles,)),
@@ -805,9 +865,9 @@
             dma((tiles, 3)),
             dma((RING, 2)),
             dma((tiles, 2)),
-            dma((RING, 3)),
-            dma((tiles, 3)),
-            dma((tiles, PIECE)),
+            dma((HOPS, 7)),
+            dma((tiles, 2, 7)),
+            dma((tiles, 7)),
             dma((shard_units,)),
         ]
         + (push_sems(devices) + push_sems(devices) if blocks else []),

time: 1420 us -> 1410 us (level)
  transfers between devices with their start and end apart: 6 -> 6, of which waited for: 1 -> 1; matrix products, arithmetic and copies ran while one was open for 6% -> 6% of each run, Pallas kernels for 41% -> 40%
where the time goes in v3:
time: 1410 us; the launch traced here: 1400 us
  Pallas kernels  1040 us (74%)
  matrix products  115 us (8%)
  local copies, waits for them, and re-layouts  87.4 us (6%)
  other arithmetic  86.3 us (6%)
  between operations  29.2 us (2%)
  starting transfers between devices  25.3 us (2%)
  waiting for transfers between devices  14.9 us (1%)
    pallas_call x3, Pallas kernels, reduce_rows(): pl.pallas_call(functools.partial(reduce_kernel, ranges, shard_units, devi...  392 us
    pallas_call x1, Pallas kernels, gather_rows(): pl.pallas_call(functools.partial(gather_kernel, openings, ahead, devices)...  229 us
    pallas_call x1, Pallas kernels, spread_rows(): pl.pallas_call(functools.partial(spread_kernel, devices), out_shape=(jax....  196 us
    dot_general x9, matrix products, dot_nn(): lax.dot_general(left, right, (((1,), (0,)), ((), ())), preferred_element_...  42.6 us
    pallas_call x1, Pallas kernels, self_backward(): pl.pallas_call(functools.partial(self_backward_kernel, heads, dim), out_s...  40.6 us
    pallas_call x1, Pallas kernels, feed_backward(): pl.pallas_call(feed_backward_kernel, out_shape=(jax.ShapeDtypeStruct((cou...  37.2 us
    dot_general x7, matrix products, dot_nt(): lax.dot_general(left, right, (((1,), (1,)), ((), ())), preferred_element_...  34.9 us
    pallas_call x2, Pallas kernels, share(): pl.pallas_call(functools.partial(share_kernel, devices), out_shape=jax.Sh...  31.4 us
  transfers between devices with their start and end apart: 6, of which 1 were waited for; matrix products, arithmetic and copies ran while one was open for 6% of the time, Pallas kernels for 40%

profile of v3, /device:TPU:0, one launch (start us, length us, event | category | flops | bytes accessed | tf_op | source)
XLA Modules:
  0.0 1401.0 jit_solution(8781269771383172825)
XLA Ops:
  24.1 229.5 %shard_map.195 = (bf16[2208,8,1152]{2,1,0:T(8,128)(2,1)}, bf16[1824,8,1152]{2,1,0:T(8,128)(2,1)}) custom-call(bf16[125,8,1152]{2,1,0:T(8,128)(2,1)} %convert_bitcast_fusion.shard_ref), custom_call_target="tpu_custom_call" | custom-call | tf_op jit(solution)/shard_map/pallas_call | solution.py:1242
  253.6 7.0 slice.205
  264.8 9.9 fusion.12
  275.4 6.5 fusion.26
  287.6 11.2 shard_map.196
  298.8 6.3 copy.110
  305.1 9.1 all-to-all-start
  329.3 195.9 %shard_map.197 = (bf16[1824,8,1152]{2,1,0:T(8,128)(2,1)}, f32[32,18,128]{2,1,0:T(8,128)}) custom-call(bf16[1824,8,1152]{2,1,0:T(8,128)(2,1)} %get-tuple-element.57.rows_ref, f32[18,128]{1,0:T(8,128)} %broadcast_divide_fusion.block_ref), custom_call_target="tpu_custom_call", output_to_operand_aliasing={{0}: (0, {})} | custom-call | tf_op jit(solution)/shard_map/pallas_call | solution.py:1221
  535.0 6.2 copy.111
  541.2 26.1 %shard_map.198 = bf16[8,2,256,144]{3,2,1,0:T(8,128)(2,1)} custom-call(s32[2,8]{1,0:T(2,128)} %and_select_fusion.start_ref, s32[2,8]{1,0:T(2,128)} %bitcast.391, bf16[8,2,256,432]{3,2,1,0:T(8,128)(2,1)} %bitcast.341), custom_call_target="tpu_custom_call" | custom-call | tf_op jit(solution)/shard_map/pallas_call | solution.py:150
  570.9 7.3 all-to-all-start.1
  590.7 14.9 %all-to-all-done.1 = bf16[8,512,144]{1,2,0:T(8,128)(2,1)S(1)} async-done(((bf16[8,512,144]{1,2,0:T(8,128)(2,1)}), bf16[8,512,144]{1,2,0:T(8,128)(2,1)S(1)}, u32[]{:S(2)}, u32[]{:S(2)}) %all-to-all-start.1) | async-done | bytes 1179680 | tf_op jit(solution)/shard_map/all_to_all | solution.py:1713
  609.7 5.9 fusion.25
  615.6 13.7 shard_map.199
  629.2 6.1 fusion.180
  640.5 21.6 %shard_map.200 = (f32[512,4608]{1,0:T(8,128)}, bf16[512,4608]{1,0:T(8,128)(2,1)}, f32[512,1152]{1,0:T(8,128)}) custom-call(bf16[512,1152]{1,0:T(8,128)(2,1)} %fusion.52.rows_ref, bf16[14592,1152]{1,0:T(8,128)(2,1)} %bitcast.334, bf16[14592,1152]{1,0:T(8,128)(2,1)} %bitcast.335, f32[6,1,768]{2,1,0:T(1,128)} %reshape.813.b_up_ref, ...), custom_call_target="tpu_custom_call" | custom-call | tf_op jit(solution)/shard_map/pallas_call | solution.py:1437
  671.2 6.3 fusion.70
  677.5 14.6 %shard_map.201 = f32[32,18,128]{2,1,0:T(8,128)S(1)} custom-call(f32[18,128]{1,0:T(8,128)S(1)} %reshape.766.block_ref), custom_call_target="tpu_custom_call" | custom-call | tf_op jit(solution)/shard_map/pallas_call | solution.py:1271
  708.1 37.2 %shard_map.203 = (f32[512,1152]{1,0:T(8,128)}, bf16[4608,1152]{1,0:T(8,128)(2,1)}, bf16[4608,1152]{1,0:T(8,128)(2,1)}, f32[6,1,768]{2,1,0:T(1,128)}) custom-call(bf16[512,1152]{1,0:T(8,128)(2,1)} %bitcast.361, bf16[14592,1152]{1,0:T(8,128)(2,1)} %bitcast.336, bf16[14592,1152]{1,0:T(8,128)(2,1)} %bitcast.337, f32[512,4608]{1,0:T(8,128)} %get-tuple-element.65.before_ref, ...), custom_call_target="tpu_custom_call" | custom-call | tf_op jit(solution)/shard_map/pallas_call | solution.py:1482
  761.8 13.3 shard_map.204
  786.9 7.1 multiply_reduce_fusion.10
  804.8 149.7 %shard_map.206 = bf16[125,8,1152]{2,1,0:T(8,128)(2,1)} custom-call(bf16[576,8,1152]{2,1,0:T(8,128)(2,1)} %bitcast.348, bf16[576,8,1152]{2,1,0:T(8,128)(2,1)} %bitcast.349), custom_call_target="tpu_custom_call" | custom-call | tf_op jit(solution)/shard_map/pallas_call | solution.py:842
  972.5 40.6 %shard_map.207 = (bf16[8,2,256,432]{3,2,1,0:T(8,128)(2,1)}, f32[2,1,288]{2,1,0:T(1,128)}) custom-call(s32[2,8]{1,0:T(2,128)} %and_select_fusion.start_ref, s32[2,8]{1,0:T(2,128)} %bitcast.392, bf16[8,2,256,432]{3,2,1,0:T(8,128)(2,1)} %bitcast.342, bf16[8,2,256,144]{3,2,1,0:T(8,128)(2,1)} %bitcast.351), custom_call_target="tpu_custom_call" | custom-call | tf_op jit(solution)/shard_map/pallas_call | solution.py:233
  1024.3 9.2 shard_map.205
  1035.6 6.3 copy.122
  1052.6 151.2 %shard_map.208 = bf16[125,8,1152]{2,1,0:T(8,128)(2,1)} custom-call(bf16[48,8,1152]{2,1,0:T(8,128)(2,1)} %bitcast.363, bf16[512,8,1152]{2,1,0:T(8,128)(2,1)} %bitcast.340, bf16[144,8,1152]{2,1,0:T(8,128)(2,1)} %bitcast.366, bf16[144,8,1152]{2,1,0:T(8,128)(2,1)} %bitcast.346, bf16[144,8,1152]{2,1,0:T(8,128)(2,1)} %bitcast.365, ...), custom_call_target="tpu_custom_call" | custom-call | tf_op jit(solution)/shard_map/pallas_call | solution.py:842
  1203.8 6.2 copy.123.grad_ref
  1210.0 17.0 %shard_map.209 = (f32[512,1152]{1,0:T(8,128)}, bf16[3,8,144,1152]{3,2,1,0:T(8,128)(2,1)}) custom-call(bf16[8,512,432]{2,1,0:T(8,128)(2,1)} %copy.123.grad_ref, bf16[3,8,144,1152]{3,2,1,0:T(8,128)(2,1)} %bitcast.339, bf16[512,1152]{1,0:T(8,128)(2,1)} %fusion.50.rows_ref), custom_call_target="tpu_custom_call" | custom-call | tf_op jit(solution)/shard_map/pallas_call | solution.py:1384
  1235.9 7.0 constant_dynamic-update-slice_fusion.5
  1249.6 91.4 %shard_map.210 = (bf16[125,8,1152]{2,1,0:T(8,128)(2,1)}, bf16[32,184,128]{2,1,0:T(8,128)(2,1)}, f32[32,3,8,128]{3,2,1,0:T(8,128)}) custom-call(bf16[432,8,1152]{2,1,0:T(8,128)(2,1)} %bitcast.353, bf16[144,8,1152]{2,1,0:T(8,128)(2,1)} %bitcast.347, bf16[184,128]{1,0:T(8,128)(2,1)} %reshape.791.refs_2_, f32[32,3,8,128]{3,2,1,0:T(8,128)} %bitcast.371), custom_call_target="tpu_custom_call" | custom-call | tf_op jit(solution)/shard_map/pallas_call | solution.py:842
  1357.9 16.8 %shard_map.211 = f32[32,4,8,128]{3,2,1,0:T(8,128)S(1)} custom-call(f32[4,8,128]{2,1,0:T(8,128)S(1)} %concatenate.80.block_ref), custom_call_target="tpu_custom_call" | custom-call | tf_op jit(solution)/shard_map/pallas_call | solution.py:1271
  1380.5 11.0 multiply_subtract_fusion
  (485 shorter events, 210.1 us)
Async XLA Ops:
  7.2 576.0 %all-gather.3.cloned.1.call-start = ((), (), s32[]{:S(2)}) async-start(), calls=%async_computation.4 | async-start | bytes 4976640 | tf_op jit(solution)/shard_map/all_gather | solution.py:1697
  21.8 264.2 %copy-start.63 = (f32[512]{0:T(512)}, f32[512]{0:T(512)S(1)}, u32[]{:S(2)}) copy-start(f32[512]{0:T(512)S(1)} %broadcast_multiply_fusion.2) | copy-start | bytes 6148
  22.5 263.4 %copy-start.84 = (f32[512]{0:T(512)}, f32[512]{0:T(512)S(1)}, u32[]{:S(2)}) copy-start(f32[512]{0:T(512)S(1)} %fusion.167) | copy-start | bytes 6148
  260.7 14.0 copy-start.116
  264.8 9.9 copy-start.59
  264.8 10.6 copy-start.25
  275.4 10.6 copy-start.44
  305.1 15.5 %copy-start.58 = (s32[2,4,8]{2,1,0:T(4,128)S(1)}, s32[2,4,8]{2,1,0:T(4,128)}, u32[]{:S(2)}) copy-start(s32[2,4,8]{2,1,0:T(4,128)} %param.15) | copy-start | bytes 772
  305.1 229.9 %all-to-all-start = ((bf16[8,512,432]{1,2,0:T(8,128)(2,1)}), bf16[8,512,432]{1,2,0:T(8,128)(2,1)}, u32[]{:S(2)}, u32[]{:S(2)}) async-start(bf16[8,512,432]{1,2,0:T(8,128)(2,1)} %copy.110), calls=%async_computation | async-start | bytes 7077888 | tf_op jit(solution)/shard_map/all_to_all | solution.py:1696
  328.4 196.7 %copy-start.97 = (f32[2,120]{1,0:T(2,128)}, f32[2,120]{1,0:T(2,128)S(1)}, u32[]{:S(2)}) copy-start(f32[2,120]{1,0:T(2,128)S(1)} %compare_convert_fusion.3) | copy-start | bytes 2884
  567.3 11.0 copy-start.112
  570.9 34.6 %all-to-all-start.1 = ((bf16[8,512,144]{1,2,0:T(8,128)(2,1)}), bf16[8,512,144]{1,2,0:T(8,128)(2,1)S(1)}, u32[]{:S(2)}, u32[]{:S(2)}) async-start(bf16[8,512,144]{1,2,0:T(8,128)(2,1)} %copy.112), calls=%async_computation.1 | async-start | bytes 2359296 | tf_op jit(solution)/shard_map/all_to_all | solution.py:1713
  578.3 434.8 %all-gather.5.cloned.1.call-start = ((), (), s32[]{:S(2)}) async-start(), calls=%async_computation.5 | async-start | bytes 4976640 | tf_op jit(solution)/shard_map/all_gather | solution.py:1830
  609.7 19.5 %copy-start.2 = (f32[512,1152]{1,0:T(8,128)}, f32[512,1152]{1,0:T(8,128)S(1)}, u32[]{:S(2)}) copy-start(f32[512,1152]{1,0:T(8,128)S(1)} %get-tuple-element.224) | copy-start | bytes 7077892
  615.6 13.7 copy-start.81
  638.2 23.9 %copy-start.86 = (f32[512]{0:T(512)}, f32[512]{0:T(512)S(1)}, u32[]{:S(2)}) copy-start(f32[512]{0:T(512)S(1)} %multiply_reduce_fusion.8) | copy-start | bytes 6148
  638.8 23.3 %copy-start.82 = (f32[512]{0:T(512)}, f32[512]{0:T(512)S(1)}, u32[]{:S(2)}) copy-start(f32[512]{0:T(512)S(1)} %get-tuple-element.210) | copy-start | bytes 6148
  640.5 21.6 %copy-start.48 = (f32[2,1152]{1,0:T(2,128)S(1)}, f32[2,1152]{1,0:T(2,128)}, u32[]{:S(2)}) copy-start(f32[2,1152]{1,0:T(2,128)} %get-tuple-element.183) | copy-start | bytes 27652
  671.2 21.2 %copy-start.31 = (f32[32,2,1152]{2,0,1:T(8,128)S(1)}, f32[32,2,1152]{2,0,1:T(8,128)}, u32[]{:S(2)}) copy-start(f32[32,2,1152]{2,0,1:T(8,128)} %copy.115) | copy-start | bytes 884740
  692.1 8.6 copy-start.77
  692.3 8.4 copy-start.7
  708.1 37.2 %copy-start.1 = (f32[512,1152]{1,0:T(8,128)S(1)}, f32[512,1152]{1,0:T(8,128)}, u32[]{:S(2)}) copy-start(f32[512,1152]{1,0:T(8,128)} %get-tuple-element.154) | copy-start | bytes 7077892
  708.1 37.2 %copy-start.47 = (f32[2,1152]{1,0:T(2,128)S(1)}, f32[2,1152]{1,0:T(2,128)}, u32[]{:S(2)}) copy-start(f32[2,1152]{1,0:T(2,128)} %get-tuple-element.185) | copy-start | bytes 27652
  798.2 171.7 %all-to-all-start.2 = ((bf16[8,512,144]{1,2,0:T(8,128)(2,1)}), bf16[8,512,144]{1,2,0:T(8,128)(2,1)S(1)}, u32[]{:S(2)}, u32[]{:S(2)}) async-start(bf16[8,512,144]{1,2,0:T(8,128)(2,1)} %bitcast.358), calls=%async_computation.2 | async-start | bytes 2359296 | tf_op jit(solution)/shard_map/all_to_all | solution.py:1853
  804.7 149.7 %copy-start.18 = (bf16[8,512,144]{1,2,0:T(8,128)(2,1)S(1)}, bf16[8,512,144]{1,2,0:T(8,128)(2,1)}, u32[]{:S(2)}) copy-start(bf16[8,512,144]{1,2,0:T(8,128)(2,1)} %copy-done.17) | copy-start | bytes 3538948
  804.8 149.7 %copy-start.33 = (bf16[2,256,1152]{2,1,0:T(8,128)(2,1)S(1)}, bf16[2,256,1152]{2,1,0:T(8,128)(2,1)}, u32[]{:S(2)}) copy-start(bf16[2,256,1152]{2,1,0:T(8,128)(2,1)} %copy-done.32) | copy-start | bytes 3538948
  1042.0 161.8 %all-to-all-start.3 = ((bf16[8,512,432]{1,2,0:T(8,128)(2,1)}), bf16[8,512,432]{1,2,0:T(8,128)(2,1)}, u32[]{:S(2)}, u32[]{:S(2)}) async-start(bf16[8,512,432]{1,2,0:T(8,128)(2,1)} %copy.122), calls=%async_computation.3 | async-start | bytes 7077888 | tf_op jit(solution)/shard_map/all_to_all | solution.py:1896
  1210.0 17.0 %copy-start.45 = (f32[2,1152]{1,0:T(2,128)S(1)}, f32[2,1152]{1,0:T(2,128)}, u32[]{:S(2)}) copy-start(f32[2,1152]{1,0:T(2,128)} %copy-done.44) | copy-start | bytes 27652
  1357.1 21.5 %copy-start.121 = (f32[1,128]{1,0:T(1,128)S(1)}, f32[1,128]{1,0:T(1,128)}, u32[]{:S(2)}) copy-start(f32[1,128]{1,0:T(1,128)} %get-tuple-element.97) | copy-start | bytes 1540
  1357.1 22.2 %copy-start.26 = (f32[78,1152]{1,0:T(8,128)S(1)}, f32[78,1152]{1,0:T(8,128)}, u32[]{:S(2)}) copy-start(f32[78,1152]{1,0:T(8,128)} %param.19) | copy-start | bytes 1078276
  1357.1 22.2 %copy-start.41 = (f32[78,1152]{1,0:T(8,128)S(1)}, f32[78,1152]{1,0:T(8,128)}, u32[]{:S(2)}) copy-start(f32[78,1152]{1,0:T(8,128)} %param.22) | copy-start | bytes 1078276
  1357.1 22.2 %copy-start.42 = (f32[78,1152]{1,0:T(8,128)S(1)}, f32[78,1152]{1,0:T(8,128)}, u32[]{:S(2)}) copy-start(f32[78,1152]{1,0:T(8,128)} %param.23) | copy-start | bytes 1078276
  (99 other events, 380.4 us)
Sparse Core Ops, SparseCore 0:
  298.9 156.4 all-gather.2
  782.8 110.1 all-gather.4

commit v4 on v3

--- a/solution.py
+++ b/solution.py
@@ -320,7 +320,8 @@
 TILE_START = 1024
 LAG = 2
 RING = LAG + 1
-HOPS = 4
+HOP_LAG = 2
+HOPS = 3 * HOP_LAG + 1
 MESH = pl.DeviceIdType.MESH
 
 
@@ -694,7 +695,7 @@
             lax.fori_loop(0, eighth // 4, one, 0)
 
         for number in range(4):
-            old = step - 2 * LAG - number
+            old = step - 2 * LAG - number * HOP_LAG
 
             @pl.when((old >= 0) & (old < tiles))
             def _(old=old, number=number):
@@ -705,7 +706,7 @@
 
         return carry
 
-    lax.fori_loop(0, tiles + 2 * LAG + 3, one_step, 0)
+    lax.fori_loop(0, tiles + 2 * LAG + 3 * HOP_LAG, one_step, 0)
 
     def finish(t, carry):
         core_copy(t).wait_send()

time: 1410 us -> 1420 us (level)
  transfers between devices with their start and end apart: 6 -> 6, of which waited for: 1 -> 1; matrix products, arithmetic and copies ran while one was open for 6% -> 6% of each run, Pallas kernels for 40% -> 41%
where the time goes in v4:
time: 1420 us; the launch traced here: 1410 us
  Pallas kernels  1050 us (74%)
  matrix products  115 us (8%)
  local copies, waits for them, and re-layouts  87.4 us (6%)
  other arithmetic  86.3 us (6%)
  between operations  29.2 us (2%)
  starting transfers between devices  26.2 us (2%)
  waiting for transfers between devices  16.8 us (1%)
    pallas_call x3, Pallas kernels, reduce_rows(): pl.pallas_call(functools.partial(reduce_kernel, ranges, shard_units, devi...  389 us
    pallas_call x1, Pallas kernels, gather_rows(): pl.pallas_call(functools.partial(gather_kernel, openings, ahead, devices)...  229 us
    pallas_call x1, Pallas kernels, spread_rows(): pl.pallas_call(functools.partial(spread_kernel, devices), out_shape=(jax....  196 us
    pallas_call x1, Pallas kernels, self_backward(): pl.pallas_call(functools.partial(self_backward_kernel, heads, dim), out_s...  53 us
    dot_general x9, matrix products, dot_nn(): lax.dot_general(left, right, (((1,), (0,)), ((), ())), preferred_element_...  42.6 us
    pallas_call x1, Pallas kernels, feed_backward(): pl.pallas_call(feed_backward_kernel, out_shape=(jax.ShapeDtypeStruct((cou...  37.2 us
    dot_general x7, matrix products, dot_nt(): lax.dot_general(left, right, (((1,), (1,)), ((), ())), preferred_element_...  34.9 us
    pallas_call x1, Pallas kernels, self_forward(): pl.pallas_call(functools.partial(self_forward_kernel, heads, dim), out_sh...  30.1 us
  transfers between devices with their start and end apart: 6, of which 1 were waited for; matrix products, arithmetic and copies ran while one was open for 6% of the time, Pallas kernels for 41%

profile of v4, /device:TPU:0, one launch (start us, length us, event | category | flops | bytes accessed | tf_op | source)
XLA Modules:
  0.0 1413.6 jit_solution(8299794284800419409)
XLA Ops:
  24.1 229.5 %shard_map.195 = (bf16[2208,8,1152]{2,1,0:T(8,128)(2,1)}, bf16[1824,8,1152]{2,1,0:T(8,128)(2,1)}) custom-call(bf16[125,8,1152]{2,1,0:T(8,128)(2,1)} %convert_bitcast_fusion.shard_ref), custom_call_target="tpu_custom_call" | custom-call | tf_op jit(solution)/shard_map/pallas_call | solution.py:1243
  253.6 7.0 slice.205
  264.8 9.9 fusion.12
  275.4 6.5 fusion.26
  287.6 11.2 shard_map.196
  298.8 6.3 copy.110
  305.1 9.1 all-to-all-start
  329.3 195.9 %shard_map.197 = (bf16[1824,8,1152]{2,1,0:T(8,128)(2,1)}, f32[32,18,128]{2,1,0:T(8,128)}) custom-call(bf16[1824,8,1152]{2,1,0:T(8,128)(2,1)} %get-tuple-element.57.rows_ref, f32[18,128]{1,0:T(8,128)} %broadcast_divide_fusion.block_ref), custom_call_target="tpu_custom_call", output_to_operand_aliasing={{0}: (0, {})} | custom-call | tf_op jit(solution)/shard_map/pallas_call | solution.py:1222
  535.0 6.2 copy.111
  541.2 30.1 %shard_map.198 = bf16[8,2,256,144]{3,2,1,0:T(8,128)(2,1)} custom-call(s32[2,8]{1,0:T(2,128)} %and_select_fusion.start_ref, s32[2,8]{1,0:T(2,128)} %bitcast.391, bf16[8,2,256,432]{3,2,1,0:T(8,128)(2,1)} %bitcast.341), custom_call_target="tpu_custom_call" | custom-call | tf_op jit(solution)/shard_map/pallas_call | solution.py:150
  575.0 7.4 all-to-all-start.1
  594.7 16.7 %all-to-all-done.1 = bf16[8,512,144]{1,2,0:T(8,128)(2,1)S(1)} async-done(((bf16[8,512,144]{1,2,0:T(8,128)(2,1)}), bf16[8,512,144]{1,2,0:T(8,128)(2,1)S(1)}, u32[]{:S(2)}, u32[]{:S(2)}) %all-to-all-start.1) | async-done | bytes 1179680 | tf_op jit(solution)/shard_map/all_to_all | solution.py:1714
  615.6 5.9 fusion.25
  621.5 13.7 shard_map.199
  635.1 6.1 fusion.180
  646.3 21.6 %shard_map.200 = (f32[512,4608]{1,0:T(8,128)}, bf16[512,4608]{1,0:T(8,128)(2,1)}, f32[512,1152]{1,0:T(8,128)}) custom-call(bf16[512,1152]{1,0:T(8,128)(2,1)} %fusion.52.rows_ref, bf16[14592,1152]{1,0:T(8,128)(2,1)} %bitcast.334, bf16[14592,1152]{1,0:T(8,128)(2,1)} %bitcast.335, f32[6,1,768]{2,1,0:T(1,128)} %reshape.813.b_up_ref, ...), custom_call_target="tpu_custom_call" | custom-call | tf_op jit(solution)/shard_map/pallas_call | solution.py:1438
  677.1 6.3 fusion.70
  683.4 11.8 shard_map.201
  711.1 37.2 %shard_map.203 = (f32[512,1152]{1,0:T(8,128)}, bf16[4608,1152]{1,0:T(8,128)(2,1)}, bf16[4608,1152]{1,0:T(8,128)(2,1)}, f32[6,1,768]{2,1,0:T(1,128)}) custom-call(bf16[512,1152]{1,0:T(8,128)(2,1)} %bitcast.361, bf16[14592,1152]{1,0:T(8,128)(2,1)} %bitcast.336, bf16[14592,1152]{1,0:T(8,128)(2,1)} %bitcast.337, f32[512,4608]{1,0:T(8,128)} %get-tuple-element.65.before_ref, ...), custom_call_target="tpu_custom_call" | custom-call | tf_op jit(solution)/shard_map/pallas_call | solution.py:1483
  764.9 13.3 shard_map.204
  789.9 7.0 multiply_reduce_fusion.10
  808.6 146.8 %shard_map.206 = bf16[125,8,1152]{2,1,0:T(8,128)(2,1)} custom-call(bf16[576,8,1152]{2,1,0:T(8,128)(2,1)} %bitcast.348, bf16[576,8,1152]{2,1,0:T(8,128)(2,1)} %bitcast.349), custom_call_target="tpu_custom_call" | custom-call | tf_op jit(solution)/shard_map/pallas_call | solution.py:843
  973.5 53.0 %shard_map.207 = (bf16[8,2,256,432]{3,2,1,0:T(8,128)(2,1)}, f32[2,1,288]{2,1,0:T(1,128)}) custom-call(s32[2,8]{1,0:T(2,128)} %and_select_fusion.start_ref, s32[2,8]{1,0:T(2,128)} %bitcast.392, bf16[8,2,256,432]{3,2,1,0:T(8,128)(2,1)} %bitcast.342, bf16[8,2,256,144]{3,2,1,0:T(8,128)(2,1)} %bitcast.351), custom_call_target="tpu_custom_call" | custom-call | tf_op jit(solution)/shard_map/pallas_call | solution.py:233
  1037.7 9.2 shard_map.205
  1049.0 6.3 copy.122
  1066.0 148.5 %shard_map.208 = bf16[125,8,1152]{2,1,0:T(8,128)(2,1)} custom-call(bf16[48,8,1152]{2,1,0:T(8,128)(2,1)} %bitcast.363, bf16[512,8,1152]{2,1,0:T(8,128)(2,1)} %bitcast.340, bf16[144,8,1152]{2,1,0:T(8,128)(2,1)} %bitcast.366, bf16[144,8,1152]{2,1,0:T(8,128)(2,1)} %bitcast.346, bf16[144,8,1152]{2,1,0:T(8,128)(2,1)} %bitcast.365, ...), custom_call_target="tpu_custom_call" | custom-call | tf_op jit(solution)/shard_map/pallas_call | solution.py:843
  1214.5 6.2 copy.123.grad_ref
  1220.8 17.0 %shard_map.209 = (f32[512,1152]{1,0:T(8,128)}, bf16[3,8,144,1152]{3,2,1,0:T(8,128)(2,1)}) custom-call(bf16[8,512,432]{2,1,0:T(8,128)(2,1)} %copy.123.grad_ref, bf16[3,8,144,1152]{3,2,1,0:T(8,128)(2,1)} %bitcast.339, bf16[512,1152]{1,0:T(8,128)(2,1)} %fusion.50.rows_ref), custom_call_target="tpu_custom_call" | custom-call | tf_op jit(solution)/shard_map/pallas_call | solution.py:1385
  1246.6 7.0 constant_dynamic-update-slice_fusion.5
  1260.3 93.8 %shard_map.210 = (bf16[125,8,1152]{2,1,0:T(8,128)(2,1)}, bf16[32,184,128]{2,1,0:T(8,128)(2,1)}, f32[32,3,8,128]{3,2,1,0:T(8,128)}) custom-call(bf16[432,8,1152]{2,1,0:T(8,128)(2,1)} %bitcast.353, bf16[144,8,1152]{2,1,0:T(8,128)(2,1)} %bitcast.347, bf16[184,128]{1,0:T(8,128)(2,1)} %reshape.791.refs_2_, f32[32,3,8,128]{3,2,1,0:T(8,128)} %bitcast.371), custom_call_target="tpu_custom_call" | custom-call | tf_op jit(solution)/shard_map/pallas_call | solution.py:843
  1371.1 16.2 %shard_map.211 = f32[32,4,8,128]{3,2,1,0:T(8,128)S(1)} custom-call(f32[4,8,128]{2,1,0:T(8,128)S(1)} %concatenate.80.block_ref), custom_call_target="tpu_custom_call" | custom-call | tf_op jit(solution)/shard_map/pallas_call | solution.py:1272
  1393.1 11.0 multiply_subtract_fusion
  (485 shorter events, 211.0 us)
Async XLA Ops:
  7.2 580.1 %all-gather.3.cloned.1.call-start = ((), (), s32[]{:S(2)}) async-start(), calls=%async_computation.4 | async-start | bytes 4976640 | tf_op jit(solution)/shard_map/all_gather | solution.py:1698
  21.8 264.2 %copy-start.63 = (f32[512]{0:T(512)}, f32[512]{0:T(512)S(1)}, u32[]{:S(2)}) copy-start(f32[512]{0:T(512)S(1)} %broadcast_multiply_fusion.2) | copy-start | bytes 6148
  22.5 263.4 %copy-start.84 = (f32[512]{0:T(512)}, f32[512]{0:T(512)S(1)}, u32[]{:S(2)}) copy-start(f32[512]{0:T(512)S(1)} %fusion.167) | copy-start | bytes 6148
  260.7 14.0 copy-start.116
  264.8 9.9 copy-start.59
  264.8 10.6 copy-start.25
  275.4 10.6 copy-start.44
  305.1 15.5 %copy-start.58 = (s32[2,4,8]{2,1,0:T(4,128)S(1)}, s32[2,4,8]{2,1,0:T(4,128)}, u32[]{:S(2)}) copy-start(s32[2,4,8]{2,1,0:T(4,128)} %param.15) | copy-start | bytes 772
  305.1 229.9 %all-to-all-start = ((bf16[8,512,432]{1,2,0:T(8,128)(2,1)}), bf16[8,512,432]{1,2,0:T(8,128)(2,1)}, u32[]{:S(2)}, u32[]{:S(2)}) async-start(bf16[8,512,432]{1,2,0:T(8,128)(2,1)} %copy.110), calls=%async_computation | async-start | bytes 7077888 | tf_op jit(solution)/shard_map/all_to_all | solution.py:1697
  328.4 196.7 %copy-start.97 = (f32[2,120]{1,0:T(2,128)}, f32[2,120]{1,0:T(2,128)S(1)}, u32[]{:S(2)}) copy-start(f32[2,120]{1,0:T(2,128)S(1)} %compare_convert_fusion.3) | copy-start | bytes 2884
  571.3 11.1 copy-start.112
  575.0 36.4 %all-to-all-start.1 = ((bf16[8,512,144]{1,2,0:T(8,128)(2,1)}), bf16[8,512,144]{1,2,0:T(8,128)(2,1)S(1)}, u32[]{:S(2)}, u32[]{:S(2)}) async-start(bf16[8,512,144]{1,2,0:T(8,128)(2,1)} %copy.112), calls=%async_computation.1 | async-start | bytes 2359296 | tf_op jit(solution)/shard_map/all_to_all | solution.py:1714
  582.3 444.1 %all-gather.5.cloned.1.call-start = ((), (), s32[]{:S(2)}) async-start(), calls=%async_computation.5 | async-start | bytes 4976640 | tf_op jit(solution)/shard_map/all_gather | solution.py:1831
  615.6 19.5 %copy-start.2 = (f32[512,1152]{1,0:T(8,128)}, f32[512,1152]{1,0:T(8,128)S(1)}, u32[]{:S(2)}) copy-start(f32[512,1152]{1,0:T(8,128)S(1)} %get-tuple-element.224) | copy-start | bytes 7077892
  621.4 13.7 copy-start.81
  644.1 23.9 %copy-start.86 = (f32[512]{0:T(512)}, f32[512]{0:T(512)S(1)}, u32[]{:S(2)}) copy-start(f32[512]{0:T(512)S(1)} %multiply_reduce_fusion.8) | copy-start | bytes 6148
  644.7 23.3 %copy-start.82 = (f32[512]{0:T(512)}, f32[512]{0:T(512)S(1)}, u32[]{:S(2)}) copy-start(f32[512]{0:T(512)S(1)} %get-tuple-element.210) | copy-start | bytes 6148
  646.3 21.6 %copy-start.48 = (f32[2,1152]{1,0:T(2,128)S(1)}, f32[2,1152]{1,0:T(2,128)}, u32[]{:S(2)}) copy-start(f32[2,1152]{1,0:T(2,128)} %get-tuple-element.183) | copy-start | bytes 27652
  677.1 18.3 %copy-start.31 = (f32[32,2,1152]{2,0,1:T(8,128)S(1)}, f32[32,2,1152]{2,0,1:T(8,128)}, u32[]{:S(2)}) copy-start(f32[32,2,1152]{2,0,1:T(8,128)} %copy.115) | copy-start | bytes 884740
  695.2 8.5 copy-start.77
  695.4 8.4 copy-start.7
  711.1 37.2 %copy-start.1 = (f32[512,1152]{1,0:T(8,128)S(1)}, f32[512,1152]{1,0:T(8,128)}, u32[]{:S(2)}) copy-start(f32[512,1152]{1,0:T(8,128)} %get-tuple-element.154) | copy-start | bytes 7077892
  711.1 37.2 %copy-start.47 = (f32[2,1152]{1,0:T(2,128)S(1)}, f32[2,1152]{1,0:T(2,128)}, u32[]{:S(2)}) copy-start(f32[2,1152]{1,0:T(2,128)} %get-tuple-element.185) | copy-start | bytes 27652
  801.3 169.7 %all-to-all-start.2 = ((bf16[8,512,144]{1,2,0:T(8,128)(2,1)}), bf16[8,512,144]{1,2,0:T(8,128)(2,1)S(1)}, u32[]{:S(2)}, u32[]{:S(2)}) async-start(bf16[8,512,144]{1,2,0:T(8,128)(2,1)} %bitcast.358), calls=%async_computation.2 | async-start | bytes 2359296 | tf_op jit(solution)/shard_map/all_to_all | solution.py:1854
  808.6 146.8 %copy-start.18 = (bf16[8,512,144]{1,2,0:T(8,128)(2,1)S(1)}, bf16[8,512,144]{1,2,0:T(8,128)(2,1)}, u32[]{:S(2)}) copy-start(bf16[8,512,144]{1,2,0:T(8,128)(2,1)} %copy-done.17) | copy-start | bytes 3538948
  808.6 146.8 %copy-start.33 = (bf16[2,256,1152]{2,1,0:T(8,128)(2,1)S(1)}, bf16[2,256,1152]{2,1,0:T(8,128)(2,1)}, u32[]{:S(2)}) copy-start(bf16[2,256,1152]{2,1,0:T(8,128)(2,1)} %copy-done.32) | copy-start | bytes 3538948
  1055.4 159.1 %all-to-all-start.3 = ((bf16[8,512,432]{1,2,0:T(8,128)(2,1)}), bf16[8,512,432]{1,2,0:T(8,128)(2,1)}, u32[]{:S(2)}, u32[]{:S(2)}) async-start(bf16[8,512,432]{1,2,0:T(8,128)(2,1)} %copy.122), calls=%async_computation.3 | async-start | bytes 7077888 | tf_op jit(solution)/shard_map/all_to_all | solution.py:1897
  1220.8 17.0 %copy-start.45 = (f32[2,1152]{1,0:T(2,128)S(1)}, f32[2,1152]{1,0:T(2,128)}, u32[]{:S(2)}) copy-start(f32[2,1152]{1,0:T(2,128)} %copy-done.44) | copy-start | bytes 27652
  1370.3 20.9 %copy-start.121 = (f32[1,128]{1,0:T(1,128)S(1)}, f32[1,128]{1,0:T(1,128)}, u32[]{:S(2)}) copy-start(f32[1,128]{1,0:T(1,128)} %get-tuple-element.97) | copy-start | bytes 1540
  1370.3 21.5 %copy-start.26 = (f32[78,1152]{1,0:T(8,128)S(1)}, f32[78,1152]{1,0:T(8,128)}, u32[]{:S(2)}) copy-start(f32[78,1152]{1,0:T(8,128)} %param.19) | copy-start | bytes 1078276
  1370.3 21.5 %copy-start.41 = (f32[78,1152]{1,0:T(8,128)S(1)}, f32[78,1152]{1,0:T(8,128)}, u32[]{:S(2)}) copy-start(f32[78,1152]{1,0:T(8,128)} %param.22) | copy-start | bytes 1078276
  1370.3 21.6 %copy-start.42 = (f32[78,1152]{1,0:T(8,128)S(1)}, f32[78,1152]{1,0:T(8,128)}, u32[]{:S(2)}) copy-start(f32[78,1152]{1,0:T(8,128)} %param.23) | copy-start | bytes 1078276
  (99 other events, 381.1 us)
Sparse Core Ops, SparseCore 0:
  298.9 156.4 all-gather.2
  785.9 115.4 all-gather.4

commit v5 on v4

--- a/solution.py
+++ b/solution.py
@@ -318,7 +318,7 @@
 PIECE = 3
 TILE = 96
 TILE_START = 1024
-LAG = 2
+LAG = 3
 RING = LAG + 1
 HOP_LAG = 2
 HOPS = 3 * HOP_LAG + 1

time: 1420 us -> 1420 us (level)
  transfers between devices with their start and end apart: 6 -> 6, of which waited for: 1 -> 1; matrix products, arithmetic and copies ran while one was open for 6% -> 6% of each run, Pallas kernels for 41% -> 40%
where the time goes in v5:
time: 1420 us; the launch traced here: 1410 us
  Pallas kernels  1050 us (74%)
  matrix products  115 us (8%)
  local copies, waits for them, and re-layouts  87.4 us (6%)
  other arithmetic  86.3 us (6%)
  between operations  29.2 us (2%)
  starting transfers between devices  23.6 us (2%)
  waiting for transfers between devices  15.6 us (1%)
    pallas_call x3, Pallas kernels, reduce_rows(): pl.pallas_call(functools.partial(reduce_kernel, ranges, shard_units, devi...  396 us
    pallas_call x1, Pallas kernels, gather_rows(): pl.pallas_call(functools.partial(gather_kernel, openings, ahead, devices)...  234 us
    pallas_call x1, Pallas kernels, spread_rows(): pl.pallas_call(functools.partial(spread_kernel, devices), out_shape=(jax....  196 us
    dot_general x9, matrix products, dot_nn(): lax.dot_general(left, right, (((1,), (0,)), ((), ())), preferred_element_...  42.6 us
    pallas_call x1, Pallas kernels, self_backward(): pl.pallas_call(functools.partial(self_backward_kernel, heads, dim), out_s...  40.6 us
    pallas_call x1, Pallas kernels, feed_backward(): pl.pallas_call(feed_backward_kernel, out_shape=(jax.ShapeDtypeStruct((cou...  37.2 us
    dot_general x7, matrix products, dot_nt(): lax.dot_general(left, right, (((1,), (1,)), ((), ())), preferred_element_...  34.9 us
    pallas_call x2, Pallas kernels, share(): pl.pallas_call(functools.partial(share_kernel, devices), out_shape=jax.Sh...  30.6 us
  transfers between devices with their start and end apart: 6, of which 1 were waited for; matrix products, arithmetic and copies ran while one was open for 6% of the time, Pallas kernels for 40%

profile of v5, /device:TPU:0, one launch (start us, length us, event | category | flops | bytes accessed | tf_op | source)
XLA Modules:
  0.0 1408.2 jit_solution(10269486574552814444)
XLA Ops:
  24.1 234.3 %shard_map.195 = (bf16[2208,8,1152]{2,1,0:T(8,128)(2,1)}, bf16[1824,8,1152]{2,1,0:T(8,128)(2,1)}) custom-call(bf16[125,8,1152]{2,1,0:T(8,128)(2,1)} %convert_bitcast_fusion.shard_ref), custom_call_target="tpu_custom_call" | custom-call | tf_op jit(solution)/shard_map/pallas_call | solution.py:1243
  258.4 7.0 slice.205
  269.7 9.9 fusion.12
  280.2 6.5 fusion.26
  292.4 11.2 shard_map.196
  303.6 6.3 copy.110
  309.9 9.4 all-to-all-start
  334.4 196.0 %shard_map.197 = (bf16[1824,8,1152]{2,1,0:T(8,128)(2,1)}, f32[32,18,128]{2,1,0:T(8,128)}) custom-call(bf16[1824,8,1152]{2,1,0:T(8,128)(2,1)} %get-tuple-element.57.rows_ref, f32[18,128]{1,0:T(8,128)} %broadcast_divide_fusion.block_ref), custom_call_target="tpu_custom_call", output_to_operand_aliasing={{0}: (0, {})} | custom-call | tf_op jit(solution)/shard_map/pallas_call | solution.py:1222
  540.3 6.2 copy.111
  546.5 26.0 %shard_map.198 = bf16[8,2,256,144]{3,2,1,0:T(8,128)(2,1)} custom-call(s32[2,8]{1,0:T(2,128)} %and_select_fusion.start_ref, s32[2,8]{1,0:T(2,128)} %bitcast.391, bf16[8,2,256,432]{3,2,1,0:T(8,128)(2,1)} %bitcast.341), custom_call_target="tpu_custom_call" | custom-call | tf_op jit(solution)/shard_map/pallas_call | solution.py:150
  593.3 15.5 %all-to-all-done.1 = bf16[8,512,144]{1,2,0:T(8,128)(2,1)S(1)} async-done(((bf16[8,512,144]{1,2,0:T(8,128)(2,1)}), bf16[8,512,144]{1,2,0:T(8,128)(2,1)S(1)}, u32[]{:S(2)}, u32[]{:S(2)}) %all-to-all-start.1) | async-done | bytes 1179680 | tf_op jit(solution)/shard_map/all_to_all | solution.py:1714
  613.0 5.9 fusion.25
  618.9 13.7 shard_map.199
  632.5 6.1 fusion.180
  643.8 21.6 %shard_map.200 = (f32[512,4608]{1,0:T(8,128)}, bf16[512,4608]{1,0:T(8,128)(2,1)}, f32[512,1152]{1,0:T(8,128)}) custom-call(bf16[512,1152]{1,0:T(8,128)(2,1)} %fusion.52.rows_ref, bf16[14592,1152]{1,0:T(8,128)(2,1)} %bitcast.334, bf16[14592,1152]{1,0:T(8,128)(2,1)} %bitcast.335, f32[6,1,768]{2,1,0:T(1,128)} %reshape.813.b_up_ref, ...), custom_call_target="tpu_custom_call" | custom-call | tf_op jit(solution)/shard_map/pallas_call | solution.py:1438
  674.5 6.3 fusion.70
  680.8 13.9 shard_map.201
  710.7 37.2 %shard_map.203 = (f32[512,1152]{1,0:T(8,128)}, bf16[4608,1152]{1,0:T(8,128)(2,1)}, bf16[4608,1152]{1,0:T(8,128)(2,1)}, f32[6,1,768]{2,1,0:T(1,128)}) custom-call(bf16[512,1152]{1,0:T(8,128)(2,1)} %bitcast.361, bf16[14592,1152]{1,0:T(8,128)(2,1)} %bitcast.336, bf16[14592,1152]{1,0:T(8,128)(2,1)} %bitcast.337, f32[512,4608]{1,0:T(8,128)} %get-tuple-element.65.before_ref, ...), custom_call_target="tpu_custom_call" | custom-call | tf_op jit(solution)/shard_map/pallas_call | solution.py:1483
  759.4 5.1 convolution_convert_fusion.5
  764.4 13.3 shard_map.204
  789.5 7.0 multiply_reduce_fusion.10
  808.0 146.9 %shard_map.206 = bf16[125,8,1152]{2,1,0:T(8,128)(2,1)} custom-call(bf16[576,8,1152]{2,1,0:T(8,128)(2,1)} %bitcast.348, bf16[576,8,1152]{2,1,0:T(8,128)(2,1)} %bitcast.349), custom_call_target="tpu_custom_call" | custom-call | tf_op jit(solution)/shard_map/pallas_call | solution.py:843
  972.9 40.6 %shard_map.207 = (bf16[8,2,256,432]{3,2,1,0:T(8,128)(2,1)}, f32[2,1,288]{2,1,0:T(1,128)}) custom-call(s32[2,8]{1,0:T(2,128)} %and_select_fusion.start_ref, s32[2,8]{1,0:T(2,128)} %bitcast.392, bf16[8,2,256,432]{3,2,1,0:T(8,128)(2,1)} %bitcast.342, bf16[8,2,256,144]{3,2,1,0:T(8,128)(2,1)} %bitcast.351), custom_call_target="tpu_custom_call" | custom-call | tf_op jit(solution)/shard_map/pallas_call | solution.py:233
  1024.7 9.2 shard_map.205
  1036.0 6.3 copy.122
  1053.0 160.2 %shard_map.208 = bf16[125,8,1152]{2,1,0:T(8,128)(2,1)} custom-call(bf16[48,8,1152]{2,1,0:T(8,128)(2,1)} %bitcast.363, bf16[512,8,1152]{2,1,0:T(8,128)(2,1)} %bitcast.340, bf16[144,8,1152]{2,1,0:T(8,128)(2,1)} %bitcast.366, bf16[144,8,1152]{2,1,0:T(8,128)(2,1)} %bitcast.346, bf16[144,8,1152]{2,1,0:T(8,128)(2,1)} %bitcast.365, ...), custom_call_target="tpu_custom_call" | custom-call | tf_op jit(solution)/shard_map/pallas_call | solution.py:843
  1213.2 6.2 copy.123.grad_ref
  1219.4 17.0 %shard_map.209 = (f32[512,1152]{1,0:T(8,128)}, bf16[3,8,144,1152]{3,2,1,0:T(8,128)(2,1)}) custom-call(bf16[8,512,432]{2,1,0:T(8,128)(2,1)} %copy.123.grad_ref, bf16[3,8,144,1152]{3,2,1,0:T(8,128)(2,1)} %bitcast.339, bf16[512,1152]{1,0:T(8,128)(2,1)} %fusion.50.rows_ref), custom_call_target="tpu_custom_call" | custom-call | tf_op jit(solution)/shard_map/pallas_call | solution.py:1385
  1245.3 7.0 constant_dynamic-update-slice_fusion.5
  1259.0 89.3 %shard_map.210 = (bf16[125,8,1152]{2,1,0:T(8,128)(2,1)}, bf16[32,184,128]{2,1,0:T(8,128)(2,1)}, f32[32,3,8,128]{3,2,1,0:T(8,128)}) custom-call(bf16[432,8,1152]{2,1,0:T(8,128)(2,1)} %bitcast.353, bf16[144,8,1152]{2,1,0:T(8,128)(2,1)} %bitcast.347, bf16[184,128]{1,0:T(8,128)(2,1)} %reshape.791.refs_2_, f32[32,3,8,128]{3,2,1,0:T(8,128)} %bitcast.371), custom_call_target="tpu_custom_call" | custom-call | tf_op jit(solution)/shard_map/pallas_call | solution.py:843
  1365.2 16.6 %shard_map.211 = f32[32,4,8,128]{3,2,1,0:T(8,128)S(1)} custom-call(f32[4,8,128]{2,1,0:T(8,128)S(1)} %concatenate.80.block_ref), custom_call_target="tpu_custom_call" | custom-call | tf_op jit(solution)/shard_map/pallas_call | solution.py:1272
  1387.7 11.0 multiply_subtract_fusion
  (485 shorter events, 210.3 us)
Async XLA Ops:
  7.2 578.7 %all-gather.3.cloned.1.call-start = ((), (), s32[]{:S(2)}) async-start(), calls=%async_computation.4 | async-start | bytes 4976640 | tf_op jit(solution)/shard_map/all_gather | solution.py:1698
  21.8 269.0 %copy-start.63 = (f32[512]{0:T(512)}, f32[512]{0:T(512)S(1)}, u32[]{:S(2)}) copy-start(f32[512]{0:T(512)S(1)} %broadcast_multiply_fusion.2) | copy-start | bytes 6148
  22.5 268.3 %copy-start.84 = (f32[512]{0:T(512)}, f32[512]{0:T(512)S(1)}, u32[]{:S(2)}) copy-start(f32[512]{0:T(512)S(1)} %fusion.167) | copy-start | bytes 6148
  265.6 14.0 copy-start.116
  269.7 9.9 copy-start.59
  269.7 10.6 copy-start.25
  280.2 10.6 copy-start.44
  309.9 15.8 %copy-start.58 = (s32[2,4,8]{2,1,0:T(4,128)S(1)}, s32[2,4,8]{2,1,0:T(4,128)}, u32[]{:S(2)}) copy-start(s32[2,4,8]{2,1,0:T(4,128)} %param.15) | copy-start | bytes 772
  309.9 230.3 %all-to-all-start = ((bf16[8,512,432]{1,2,0:T(8,128)(2,1)}), bf16[8,512,432]{1,2,0:T(8,128)(2,1)}, u32[]{:S(2)}, u32[]{:S(2)}) async-start(bf16[8,512,432]{1,2,0:T(8,128)(2,1)} %copy.110), calls=%async_computation | async-start | bytes 7077888 | tf_op jit(solution)/shard_map/all_to_all | solution.py:1697
  333.6 196.9 %copy-start.97 = (f32[2,120]{1,0:T(2,128)}, f32[2,120]{1,0:T(2,128)S(1)}, u32[]{:S(2)}) copy-start(f32[2,120]{1,0:T(2,128)S(1)} %compare_convert_fusion.3) | copy-start | bytes 2884
  572.6 8.4 copy-start.112
  576.2 32.6 %all-to-all-start.1 = ((bf16[8,512,144]{1,2,0:T(8,128)(2,1)}), bf16[8,512,144]{1,2,0:T(8,128)(2,1)S(1)}, u32[]{:S(2)}, u32[]{:S(2)}) async-start(bf16[8,512,144]{1,2,0:T(8,128)(2,1)} %copy.112), calls=%async_computation.1 | async-start | bytes 2359296 | tf_op jit(solution)/shard_map/all_to_all | solution.py:1714
  580.9 432.6 %all-gather.5.cloned.1.call-start = ((), (), s32[]{:S(2)}) async-start(), calls=%async_computation.5 | async-start | bytes 4976640 | tf_op jit(solution)/shard_map/all_gather | solution.py:1831
  613.0 19.5 %copy-start.2 = (f32[512,1152]{1,0:T(8,128)}, f32[512,1152]{1,0:T(8,128)S(1)}, u32[]{:S(2)}) copy-start(f32[512,1152]{1,0:T(8,128)S(1)} %get-tuple-element.224) | copy-start | bytes 7077892
  618.9 13.7 copy-start.81
  641.5 23.9 %copy-start.86 = (f32[512]{0:T(512)}, f32[512]{0:T(512)S(1)}, u32[]{:S(2)}) copy-start(f32[512]{0:T(512)S(1)} %multiply_reduce_fusion.8) | copy-start | bytes 6148
  642.1 23.3 %copy-start.82 = (f32[512]{0:T(512)}, f32[512]{0:T(512)S(1)}, u32[]{:S(2)}) copy-start(f32[512]{0:T(512)S(1)} %get-tuple-element.210) | copy-start | bytes 6148
  643.8 21.6 %copy-start.48 = (f32[2,1152]{1,0:T(2,128)S(1)}, f32[2,1152]{1,0:T(2,128)}, u32[]{:S(2)}) copy-start(f32[2,1152]{1,0:T(2,128)} %get-tuple-element.183) | copy-start | bytes 27652
  674.5 20.5 %copy-start.31 = (f32[32,2,1152]{2,0,1:T(8,128)S(1)}, f32[32,2,1152]{2,0,1:T(8,128)}, u32[]{:S(2)}) copy-start(f32[32,2,1152]{2,0,1:T(8,128)} %copy.115) | copy-start | bytes 884740
  694.8 8.6 copy-start.77
  695.0 8.4 copy-start.7
  710.7 37.2 %copy-start.1 = (f32[512,1152]{1,0:T(8,128)S(1)}, f32[512,1152]{1,0:T(8,128)}, u32[]{:S(2)}) copy-start(f32[512,1152]{1,0:T(8,128)} %get-tuple-element.154) | copy-start | bytes 7077892
  710.7 37.2 %copy-start.47 = (f32[2,1152]{1,0:T(2,128)S(1)}, f32[2,1152]{1,0:T(2,128)}, u32[]{:S(2)}) copy-start(f32[2,1152]{1,0:T(2,128)} %get-tuple-element.185) | copy-start | bytes 27652
  800.9 169.5 %all-to-all-start.2 = ((bf16[8,512,144]{1,2,0:T(8,128)(2,1)}), bf16[8,512,144]{1,2,0:T(8,128)(2,1)S(1)}, u32[]{:S(2)}, u32[]{:S(2)}) async-start(bf16[8,512,144]{1,2,0:T(8,128)(2,1)} %bitcast.358), calls=%async_computation.2 | async-start | bytes 2359296 | tf_op jit(solution)/shard_map/all_to_all | solution.py:1854
  808.0 146.9 %copy-start.18 = (bf16[8,512,144]{1,2,0:T(8,128)(2,1)S(1)}, bf16[8,512,144]{1,2,0:T(8,128)(2,1)}, u32[]{:S(2)}) copy-start(bf16[8,512,144]{1,2,0:T(8,128)(2,1)} %copy-done.17) | copy-start | bytes 3538948
  808.0 146.9 %copy-start.33 = (bf16[2,256,1152]{2,1,0:T(8,128)(2,1)S(1)}, bf16[2,256,1152]{2,1,0:T(8,128)(2,1)}, u32[]{:S(2)}) copy-start(bf16[2,256,1152]{2,1,0:T(8,128)(2,1)} %copy-done.32) | copy-start | bytes 3538948
  1042.4 170.8 %all-to-all-start.3 = ((bf16[8,512,432]{1,2,0:T(8,128)(2,1)}), bf16[8,512,432]{1,2,0:T(8,128)(2,1)}, u32[]{:S(2)}, u32[]{:S(2)}) async-start(bf16[8,512,432]{1,2,0:T(8,128)(2,1)} %copy.122), calls=%async_computation.3 | async-start | bytes 7077888 | tf_op jit(solution)/shard_map/all_to_all | solution.py:1897
  1219.4 17.0 %copy-start.45 = (f32[2,1152]{1,0:T(2,128)S(1)}, f32[2,1152]{1,0:T(2,128)}, u32[]{:S(2)}) copy-start(f32[2,1152]{1,0:T(2,128)} %copy-done.44) | copy-start | bytes 27652
  1364.4 21.4 %copy-start.121 = (f32[1,128]{1,0:T(1,128)S(1)}, f32[1,128]{1,0:T(1,128)}, u32[]{:S(2)}) copy-start(f32[1,128]{1,0:T(1,128)} %get-tuple-element.97) | copy-start | bytes 1540
  1364.5 22.0 %copy-start.26 = (f32[78,1152]{1,0:T(8,128)S(1)}, f32[78,1152]{1,0:T(8,128)}, u32[]{:S(2)}) copy-start(f32[78,1152]{1,0:T(8,128)} %param.19) | copy-start | bytes 1078276
  1364.5 22.0 %copy-start.41 = (f32[78,1152]{1,0:T(8,128)S(1)}, f32[78,1152]{1,0:T(8,128)}, u32[]{:S(2)}) copy-start(f32[78,1152]{1,0:T(8,128)} %param.22) | copy-start | bytes 1078276
  1364.5 22.0 %copy-start.42 = (f32[78,1152]{1,0:T(8,128)S(1)}, f32[78,1152]{1,0:T(8,128)}, u32[]{:S(2)}) copy-start(f32[78,1152]{1,0:T(8,128)} %param.23) | copy-start | bytes 1078276
  (99 other events, 381.0 us)
Sparse Core Ops, SparseCore 0:
  303.8 157.0 all-gather.2
  785.5 113.2 all-gather.4
